TPU v7x, 32 devices: a whole 2x2x4 slice. The times are simulated.
32 devices in a mesh: groups: 2 (over x), sub: 16 (over z, y, core).
Axes of the slice: x: 2, y: 2, z: 4, core: 2. Of those that a mesh axis runs over, the one named last changes fastest.
Arguments:
- loads: float32 [8192, 1024], P(('groups', 'sub')), parts along dimension 0, may hold values from -250 to 250
- row_ids: int32 [8192], P(('groups', 'sub')), parts along dimension 0, may hold values from 0 to 4095, as said below
- densities: float32 [8192, 12], P(('groups', 'sub')), parts along dimension 0, may hold values from 0 to 1
- block_cols: int32 [8192, 12], P(('groups', 'sub')), parts along dimension 0, may hold values from 0 to 4095, as said below
- block_types: int32 [8192, 12], P(('groups', 'sub')), parts along dimension 0, may hold values from 0 to 2
- ref_blocks: float32 [3, 64, 64], replicated, may hold values from -1 to 1.5, as said below
Outputs:
- solution: float32 [8192, 1024], P(('groups', 'sub')), parts along dimension 0
- residual: float32 [8192, 1024], P(('groups', 'sub')), parts along dimension 0
There are 2 independent parts, one for each index of `groups`. A program takes and returns all parts, laid end to end along the dimension named above; an argument that names none is the same for every part. Nothing has to cross between parts.
Inputs may be any that keep to these rules, and one draw needn't show every extreme that they name: `row_ids`: A permutation of the mesh's block rows. Device d's rows are 256 * d to 256 * d + 255; its partner is device (d + 8) mod 16. The slots of device d hold rows of devices d - 1, d, d + 1 and of its partner; at most 64 rows of one device belong to each other device; across some boundary exactly 64 go each way, and some pair of partners swaps exactly 64. `block_cols`: every column lies within 32 rows of its block row, and some lies exactly 32 away. Couplings are symmetric: if a slot of row g points to row h with a density and a type, a slot of row h points to g with the same. A slot of density zero may point to its own row. `ref_blocks`: each block is symmetric and positive definite.
All inputs are finite; a program needn't handle non-finite values.
Results may differ from a plain program's by a relative error of at most 0.0003.
Values sent between devices are 32-bit elements; how exact they have to be, the bound alone decides.
No kernel may reach another device: no remote copies, remote signals or barrier semaphores. Data moves between devices by JAX's collectives and lax.ppermute only.
A program may use at most 128 MiB of HBM per device.

v0:
```python
import jax
import jax.numpy as jnp
from jax import lax
from jax.sharding import PartitionSpec as P

HALO = 32
TYPES = 3
ITERS = 3


mass_shift = 0.5


def with_halo(cells, sides, width):
    for axis, dim in sides:
        count = lax.axis_size(axis)
        ends = count - 1
        head = lax.slice_in_dim(cells, 0, width, axis=dim)
        tail = lax.slice_in_dim(cells, cells.shape[dim] - width, cells.shape[dim], axis=dim)
        cells = jnp.concatenate(
            [
                lax.ppermute(tail, axis, [(i, (i + 1) % count) for i in range(ends)]),
                cells,
                lax.ppermute(head, axis, [((i + 1) % count, i) for i in range(ends)]),
            ],
            axis=dim,
        )
    return cells


def gram_solve(matrix, target):
    factor = jnp.linalg.cholesky(matrix)
    return jax.scipy.linalg.cho_solve((factor, True), target)


def cross_gram(left, right, cases):
    left_flat = left.reshape(-1, cases)
    right_flat = right.reshape(-1, cases)
    return jnp.dot(
        left_flat.T, right_flat, precision=lax.Precision.HIGHEST, preferred_element_type=jnp.float32
    )


def times_small(vector_in, matrix, cases):
    flat = vector_in.reshape(-1, cases)
    return jnp.dot(
        flat, matrix, precision=lax.Precision.HIGHEST, preferred_element_type=jnp.float32
    ).reshape(vector_in.shape)


def pack_rows(members, target_slot, length):
    return tuple(
        (
            jnp.zeros((length,) + member.shape[1:], member.dtype)
            .at[target_slot]
            .set(member, mode="drop")
            for member in members
        )
    )


def on_device(loads, row_ids, densities, block_cols, block_types, ref_blocks):
    block_rows = loads.shape[0]
    width = loads.shape[1]
    dof_count = ref_blocks.shape[1]
    cases = width // dof_count
    devices = lax.axis_size("sub")
    position = lax.axis_index("sub")
    first_row = position * block_rows
    capacity = block_rows // 4
    owner = row_ids // block_rows
    leaving = owner != position
    row_tags = row_ids + 1
    slot_index = jnp.arange(block_rows, dtype=jnp.int32)
    same_owner = owner[:, None] == owner[None, :]
    earlier = slot_index[None, :] < slot_index[:, None]
    order_rank = jnp.sum((same_owner & earlier).astype(jnp.int32), axis=1)
    members = (loads, row_tags, densities, block_cols, block_types)
    kept_rows = (loads, jnp.where(leaving, 0, row_tags), densities, block_cols, block_types)
    target_slot = jnp.where(leaving, owner * capacity + order_rank, devices * capacity)
    outgoing = pack_rows(members, target_slot, devices * capacity)
    arrived = lax.all_to_all(outgoing, "sub", split_axis=0, concat_axis=0, tiled=True)
    pooled = [jnp.concatenate([kept_rows[number], arrived[number]], axis=0) for number in range(5)]
    local_slot = jnp.where(pooled[1] > 0, pooled[1] - 1 - first_row, block_rows)

    def arrange(member):
        return (
            jnp.zeros((block_rows,) + member.shape[1:], member.dtype)
            .at[local_slot]
            .set(member, mode="drop")
        )

    loads_geo = arrange(pooled[0])
    density_geo = arrange(pooled[2])
    column_geo = arrange(pooled[3])
    type_geo = arrange(pooled[4])
    kinds = jnp.arange(TYPES, dtype=jnp.int32)
    weights = density_geo[:, :, None] * (type_geo[:, :, None] == kinds[None, None, :]).astype(
        jnp.float32
    )
    local_cols = column_geo - first_row + HALO
    slot_count = column_geo.shape[1]
    solution = jnp.zeros_like(loads_geo)
    residual = loads_geo
    direction = loads_geo
    residual_gram = lax.psum(cross_gram(residual, residual, cases), "sub")
    for step in range(ITERS):
        vector_in = direction
        padded = with_halo(vector_in, (("sub", 0),), HALO)

        def add_slot(column, bucket):
            chosen_cols = lax.dynamic_index_in_dim(local_cols, column, 1, keepdims=False)
            chosen_weights = lax.dynamic_index_in_dim(weights, column, 1, keepdims=False)
            difference = vector_in - jnp.take(padded, chosen_cols, axis=0)
            return bucket + chosen_weights.T[:, :, None] * difference[None]

        bucket = lax.fori_loop(
            0, slot_count, add_slot, jnp.zeros((TYPES, block_rows, width), jnp.float32)
        )
        blocks = bucket.reshape(TYPES, block_rows, dof_count, cases)
        applied = jnp.einsum("tij,tgjc->gic", ref_blocks, blocks, precision=lax.Precision.HIGHEST)
        applied = mass_shift * vector_in + applied.reshape(block_rows, width)
        curvature_gram = lax.psum(cross_gram(direction, applied, cases), "sub")
        step_size = gram_solve(curvature_gram, residual_gram)
        solution = solution + times_small(direction, step_size, cases)
        residual = residual - times_small(applied, step_size, cases)
        if step + 1 < ITERS:
            next_gram = lax.psum(cross_gram(residual, residual, cases), "sub")
            update_mix = gram_solve(residual_gram, next_gram)
            direction = residual + times_small(direction, update_mix, cases)
            residual_gram = next_gram
    return (solution, residual)


def solution(mesh):
    placed = (
        P(("groups", "sub"), None),
        P(("groups", "sub")),
        P(("groups", "sub"), None),
        P(("groups", "sub"), None),
        P(("groups", "sub"), None),
        P(),
    )
    return jax.shard_map(
        on_device,
        mesh=mesh,
        in_specs=placed,
        out_specs=(P(("groups", "sub"), None), P(("groups", "sub"), None)),
        check_vma=False,
    )
```

profile of v0, /device:TPU:0, one launch (start us, length us, event | category | flops | bytes accessed | tf_op | source)
XLA Modules:
  0.0 995.6 jit_solution(7187218562811317491)
XLA Ops:
  3.6 7.4 all-to-all-start
  41.4 4.3 scatter_custom_fusion.1
  48.1 4.7 all-to-all-start.1
  55.9 6.2 scatter_custom_fusion.6
  63.9 6.4 scatter_custom_fusion.4
  71.7 6.2 scatter_custom_fusion.8
  78.6 51.7 %all-to-all-done.1 = f32[16,64,1024]{2,1,0:T(8,128)} async-done(((f32[16,64,1024]{2,1,0:T(8,128)}), f32[16,64,1024]{2,1,0:T(8,128)}, u32[]{:S(2)}, u32[]{:S(2)}) %all-to-all-start.1) | async-done | bytes 4194336 | tf_op jit(solution)/shard_map/all_to_all | solution.py:82
  130.4 9.5 scatter_custom_fusion.2
  139.9 4.9 reshape.185
  149.4 19.3 %fusion.77 = f32[16,16]{0,1:T(8,128)S(1)} fusion(f32[16384,16]{1,0:T(8,128)} %reshape.185), kind=kOutput, calls=%fused_computation.151 | convolution fusion | flops 50331648 | bytes 1049600 | tf_op jit(solution)/shard_map/dot_general | solution.py:39
  168.9 95.2 %while.42 = (s32[]{:T(128)}, f32[3,256,1024]{2,1,0:T(8,128)}, f32[256,12,3]{0,2,1:T(4,128)}, s32[256,12]{0,1:T(8,128)S(1)}, f32[320,1024]{1,0:T(8,128)S(1)}, /*index=5*/f32[256,1024]{1,0:T(8,128)S(1)}, s32[]{:T(128)}, s32[]{:T(128)}) while((s32[]{:T(128)}, f32[3,256,1024]{2,1,0:T(8,128)}, f32[256,12,3]{0,2,1:T(4,128)}, ...), condition=%wide.region_11.13_spmd.clone, body=%wide.region_10.12_spmd.clone.sunk | while | flops 2886915 | bytes 12604015 | solution.py:117
  187.3 4.0 select_add_fusion.6
  195.4 4.0 select_add_fusion.6
  203.5 4.0 select_add_fusion.6
  219.7 4.0 select_add_fusion.6
  227.7 4.0 select_add_fusion.6
  235.8 4.0 select_add_fusion.6
  243.9 4.0 select_add_fusion.6
  267.7 5.7 fusion.12
  274.6 16.4 %reshape.188 = f32[16384,16]{1,0:T(8,128)} reshape(f32[256,1024]{1,0:T(8,128)S(1)} %multiply_add_fusion.2) | data formatting | bytes 2097152 | tf_op jit(solution)/shard_map/reshape | solution.py:38
  290.9 17.3 %fusion.76 = f32[16,16]{0,1:T(8,128)S(1)} fusion(f32[16384,16]{1,0:T(8,128)} %reshape.185, f32[16384,16]{1,0:T(8,128)} %reshape.188), kind=kOutput, calls=%fused_computation.150 | convolution fusion | flops 50331648 | bytes 2098176 | tf_op jit(solution)/shard_map/dot_general | solution.py:39
  308.2 74.5 %all-reduce = (f32[16,16]{0,1:T(8,128)S(1)}, f32[16,16]{0,1:T(8,128)S(1)}) all-reduce(f32[16,16]{0,1:T(8,128)S(1)} %fusion.77, f32[16,16]{0,1:T(8,128)S(1)} %fusion.76), channel_id=1, replica_groups=mesh['groups'=2,'sub'=16] {'sub'}, use_global_device_ids=true, to_apply=%region_15.18 | all-reduce | flops 512 | bytes 4096 | tf_op jit(solution)/shard_map/psum | solution.py:106
  387.2 10.6 %fusion.78 = f32[16384,16]{0,1:T(8,128)} fusion(f32[16384,16]{1,0:T(8,128)} %reshape.185, f32[16,16]{1,0:T(8,128)S(1)} %fusion.64), kind=kOutput, calls=%fused_computation.152 | convolution fusion | flops 50331648 | bytes 2098176 | tf_op jit(solution)/shard_map/dot_general | solution.py:46
  397.8 8.8 fusion.79
  406.6 7.9 reshape.189
  414.6 4.9 reshape.190
  419.5 19.8 %fusion.80 = f32[16,16]{0,1:T(8,128)S(1)} fusion(f32[16384,16]{1,0:T(8,128)} %reshape.190), kind=kOutput, calls=%fused_computation.154 | convolution fusion | flops 50331648 | bytes 1049600 | tf_op jit(solution)/shard_map/dot_general | solution.py:39
  439.3 30.0 %psum.44 = f32[16,16]{0,1:T(8,128)S(1)} all-reduce(f32[16,16]{0,1:T(8,128)S(1)} %fusion.80), channel_id=1, replica_groups=mesh['groups'=2,'sub'=16] {'sub'}, use_global_device_ids=true, to_apply=%region_16.20 | all-reduce | flops 256 | bytes 2048 | tf_op jit(solution)/shard_map/psum | solution.py:128
  473.7 17.2 %fusion.81 = f32[16384,16]{1,0:T(8,128)} fusion(f32[16384,16]{1,0:T(8,128)} %reshape.185, f32[16,16]{1,0:T(8,128)S(1)} %fusion.59), kind=kOutput, calls=%fused_computation.155 | convolution fusion | flops 50331648 | bytes 2098176 | tf_op jit(solution)/shard_map/dot_general | solution.py:46
  490.9 7.9 reshape.191
  499.9 6.2 reshape.192
  516.7 83.7 %while.43 = (s32[]{:T(128)}, f32[3,256,1024]{2,1,0:T(8,128)}, f32[256,12,3]{0,2,1:T(4,128)}, s32[256,12]{0,1:T(8,128)S(1)}, f32[320,1024]{1,0:T(8,128)S(1)}, /*index=5*/f32[256,1024]{1,0:T(8,128)}, s32[]{:T(128)}, s32[]{:T(128)}) while((s32[]{:T(128)}, f32[3,256,1024]{2,1,0:T(8,128)}, f32[256,12,3]{0,2,1:T(4,128)}, ...), condition=%wide.region_18.22_spmd.clone, body=%wide.region_17.21_spmd.clone.sunk | while | flops 2886915 | bytes 12604015 | solution.py:117
  609.1 4.9 reshape.195
  614.0 17.5 %fusion.82 = f32[16,16]{0,1:T(8,128)S(1)} fusion(f32[16384,16]{1,0:T(8,128)} %reshape.192, f32[16384,16]{1,0:T(8,128)} %reshape.195), kind=kOutput, calls=%fused_computation.156 | convolution fusion | flops 50331648 | bytes 2098176 | tf_op jit(solution)/shard_map/dot_general | solution.py:39
  631.5 31.1 %psum.45 = f32[16,16]{0,1:T(8,128)S(1)} all-reduce(f32[16,16]{0,1:T(8,128)S(1)} %fusion.82), channel_id=1, replica_groups=mesh['groups'=2,'sub'=16] {'sub'}, use_global_device_ids=true, to_apply=%region_19.23 | all-reduce | flops 256 | bytes 2048 | tf_op jit(solution)/shard_map/psum | solution.py:123
  667.1 17.1 %fusion.83 = f32[16384,16]{1,0:T(8,128)} fusion(f32[16384,16]{1,0:T(8,128)} %reshape.195, f32[16,16]{1,0:T(8,128)S(1)} %fusion.54), kind=kOutput, calls=%fused_computation.157 | convolution fusion | flops 50331648 | bytes 2098176 | tf_op jit(solution)/shard_map/dot_general | solution.py:46
  684.2 8.0 reshape.196
  692.3 4.9 reshape.197
  697.2 19.5 %fusion.84 = f32[16,16]{1,0:T(8,128)S(1)} fusion(f32[16384,16]{1,0:T(8,128)} %reshape.197), kind=kOutput, calls=%fused_computation.158 | convolution fusion | flops 50331648 | bytes 1049600 | tf_op jit(solution)/shard_map/dot_general | solution.py:39
  716.8 30.0 %psum.46 = f32[16,16]{1,0:T(8,128)S(1)} all-reduce(f32[16,16]{1,0:T(8,128)S(1)} %fusion.84), channel_id=1, replica_groups=mesh['groups'=2,'sub'=16] {'sub'}, use_global_device_ids=true, to_apply=%region_20.24 | all-reduce | flops 256 | bytes 2048 | tf_op jit(solution)/shard_map/psum | solution.py:128
  747.1 17.3 %fusion.85 = f32[16384,16]{1,0:T(8,128)} fusion(f32[16384,16]{1,0:T(8,128)} %reshape.192, f32[16,16]{1,0:T(8,128)S(1)} %fusion.49), kind=kOutput, calls=%fused_computation.159 | convolution fusion | flops 50331648 | bytes 2098176 | tf_op jit(solution)/shard_map/dot_general | solution.py:46
  764.4 8.0 reshape.198
  778.8 10.7 %convolution_add_fusion.1 = f32[16384,16]{0,1:T(8,128)} fusion(f32[16384,16]{0,1:T(8,128)S(1)} %copy-done.7, f32[16384,16]{1,0:T(8,128)} %reshape.192, f32[16,16]{1,0:T(8,128)S(1)} %fusion.54), kind=kOutput, calls=%fused_computation.34 | convolution fusion | flops 50593792 | bytes 3146752 | tf_op jit(solution)/shard_map/dot_general | solution.py:46
  789.5 6.2 reshape.199
  797.0 84.6 %while.44 = (s32[]{:T(128)}, f32[3,256,1024]{2,1,0:T(8,128)}, f32[256,12,3]{0,2,1:T(4,128)}, s32[256,12]{0,1:T(8,128)S(1)}, f32[320,1024]{1,0:T(8,128)S(1)}, /*index=5*/f32[256,1024]{1,0:T(8,128)}, s32[]{:T(128)}, s32[]{:T(128)}) while((s32[]{:T(128)}, f32[3,256,1024]{2,1,0:T(8,128)}, f32[256,12,3]{0,2,1:T(4,128)}, ...), condition=%wide.region_22.26_spmd.clone, body=%wide.region_21.25_spmd.clone.sunk | while | flops 2886915 | bytes 12604015 | solution.py:117
  805.6 4.0 select_add_fusion.8
  812.8 4.0 select_add_fusion.8
  820.0 4.0 select_add_fusion.8
  827.2 4.0 select_add_fusion.8
  834.4 4.0 select_add_fusion.8
  841.6 4.0 select_add_fusion.8
  848.8 4.0 select_add_fusion.8
  856.0 4.0 select_add_fusion.8
  863.2 4.0 select_add_fusion.8
  870.4 4.0 select_add_fusion.8
  877.6 4.0 select_add_fusion.8
  890.3 4.9 reshape.202
  895.2 17.5 %fusion.86 = f32[16,16]{0,1:T(8,128)S(1)} fusion(f32[16384,16]{1,0:T(8,128)} %reshape.199, f32[16384,16]{1,0:T(8,128)} %reshape.202), kind=kOutput, calls=%fused_computation.160 | convolution fusion | flops 50331648 | bytes 2098176 | tf_op jit(solution)/shard_map/dot_general | solution.py:39
  912.6 31.2 %psum.47 = f32[16,16]{0,1:T(8,128)S(1)} all-reduce(f32[16,16]{0,1:T(8,128)S(1)} %fusion.86), channel_id=1, replica_groups=mesh['groups'=2,'sub'=16] {'sub'}, use_global_device_ids=true, to_apply=%region_23.27 | all-reduce | flops 256 | bytes 2048 | tf_op jit(solution)/shard_map/psum | solution.py:123
  948.3 17.0 %fusion.87 = f32[16384,16]{1,0:T(8,128)} fusion(f32[16384,16]{1,0:T(8,128)} %reshape.202, f32[16,16]{1,0:T(8,128)S(1)} %fusion.44), kind=kOutput, calls=%fused_computation.161 | convolution fusion | flops 50331648 | bytes 2098176 | tf_op jit(solution)/shard_map/dot_general | solution.py:46
  965.2 7.4 convolution_add_fusion
  972.6 4.6 copy.194
  977.2 8.9 add.198
  986.1 8.0 reshape.203
  (436 shorter events, 299.2 us)
Async XLA Ops:
  0.6 267.0 %copy-start = (f32[3,64,64]{2,1,0:T(8,128)S(1)}, f32[3,64,64]{2,1,0:T(8,128)}, u32[]{:S(2)}) copy-start(f32[3,64,64]{2,1,0:T(8,128)} %param.22) | copy-start | bytes 147460
  3.6 13.7 %all-to-all-start = ((s32[16,64,1]{1,2,0:T(1,128)}), s32[16,64,1]{1,2,0:T(1,128)S(1)}, u32[]{:S(2)}, u32[]{:S(2)}) async-start(s32[16,64,1]{1,2,0:T(1,128)} %bitcast.1), calls=%async_computation | async-start | bytes 16384 | tf_op jit(solution)/shard_map/all_to_all | solution.py:82
  17.4 10.2 %all-to-all-start.3 = ((f32[16,1,768]{2,1,0:T(1,128)}), f32[16,1,768]{2,1,0:T(1,128)S(1)}, u32[]{:S(2)}, u32[]{:S(2)}) async-start(f32[16,1,768]{2,1,0:T(1,128)} %reshape.346), calls=%async_computation.3 | async-start | bytes 98304 | tf_op jit(solution)/shard_map/all_to_all | solution.py:82
  27.6 10.2 %all-to-all-start.2 = ((s32[16,1,768]{2,1,0:T(1,128)}), s32[16,1,768]{2,1,0:T(1,128)S(1)}, u32[]{:S(2)}, u32[]{:S(2)}) async-start(s32[16,1,768]{2,1,0:T(1,128)} %reshape.348), calls=%async_computation.2 | async-start | bytes 98304 | tf_op jit(solution)/shard_map/all_to_all | solution.py:82
  37.8 10.2 %all-to-all-start.4 = ((s32[16,1,768]{2,1,0:T(1,128)}), s32[16,1,768]{2,1,0:T(1,128)S(1)}, u32[]{:S(2)}, u32[]{:S(2)}) async-start(s32[16,1,768]{2,1,0:T(1,128)} %reshape.350), calls=%async_computation.4 | async-start | bytes 98304 | tf_op jit(solution)/shard_map/all_to_all | solution.py:82
  45.7 9.9 copy-start.9
  48.1 15.5 %copy-start.10 = (s32[256,12]{0,1:T(8,128)S(1)}, s32[256,12]{0,1:T(8,128)}, u32[]{:S(2)}) copy-start(s32[256,12]{0,1:T(8,128)} %param.21) | copy-start | bytes 36868
  48.1 23.3 %copy-start.11 = (s32[256,12]{0,1:T(8,128)S(1)}, s32[256,12]{0,1:T(8,128)}, u32[]{:S(2)}) copy-start(s32[256,12]{0,1:T(8,128)} %param.20) | copy-start | bytes 36868
  48.1 82.3 %copy-start.8 = (f32[256,1024]{1,0:T(8,128)S(1)}, f32[256,1024]{1,0:T(8,128)}, u32[]{:S(2)}) copy-start(f32[256,1024]{1,0:T(8,128)} %param.17) | copy-start | bytes 3145732
  48.1 82.3 %all-to-all-start.1 = ((f32[16,64,1024]{2,1,0:T(8,128)}), f32[16,64,1024]{2,1,0:T(8,128)}, u32[]{:S(2)}, u32[]{:S(2)}) async-start(f32[16,64,1024]{2,1,0:T(8,128)} %bitcast.170), calls=%async_computation.1 | async-start | bytes 8388608 | tf_op jit(solution)/shard_map/all_to_all | solution.py:82
  144.8 23.9 %collective-permute-start.1 = (f32[32,1024]{1,0:T(8,128)S(1)}, f32[32,1024]{1,0:T(8,128)S(1)}, u32[]{:S(2)}, u32[]{:S(2)}) collective-permute-start(f32[32,1024]{1,0:T(8,128)S(1)} %get-tuple-element.515), channel_id=1, source_target_pairs={{1,0},{2,1},{3,2},{4,3},{5,4},{6,5},{7,6},{8,7},{9,8},{10,9},{11,1... | collective-permute-start | bytes 393224 | tf_op jit(solution)/shard_map/ppermute | solution.py:24
  146.1 22.6 %collective-permute-start = (f32[32,1024]{1,0:T(8,128)S(1)}, f32[32,1024]{1,0:T(8,128)S(1)}, u32[]{:S(2)}, u32[]{:S(2)}) collective-permute-start(f32[32,1024]{1,0:T(8,128)S(1)} %get-tuple-element.514), channel_id=1, source_target_pairs={{0,1},{1,2},{2,3},{3,4},{4,5},{5,6},{6,7},{7,8},{8,9},{9,10},{10,1... | collective-permute-start | bytes 393224 | tf_op jit(solution)/shard_map/ppermute | solution.py:22
  386.8 11.0 %copy-start.1 = (f32[16384,16]{1,0:T(8,128)S(1)}, f32[16384,16]{1,0:T(8,128)}, u32[]{:S(2)}) copy-start(f32[16384,16]{1,0:T(8,128)} %reshape.188) | copy-start | bytes 3145732
  414.6 84.1 %copy-start.2 = (f32[256,1024]{1,0:T(8,128)}, f32[256,1024]{1,0:T(8,128)S(1)}, u32[]{:S(2)}) copy-start(f32[256,1024]{1,0:T(8,128)S(1)} %sub.65) | copy-start | bytes 3145732
  507.1 8.3 collective-permute-start.3
  508.4 7.0 collective-permute-start.2
  684.2 8.0 copy-start.3
  692.3 80.1 %copy-start.4 = (f32[256,1024]{1,0:T(8,128)}, f32[256,1024]{1,0:T(8,128)S(1)}, u32[]{:S(2)}) copy-start(f32[256,1024]{1,0:T(8,128)S(1)} %sub.66) | copy-start | bytes 3145732
  764.4 14.4 %copy-start.7 = (f32[16384,16]{0,1:T(8,128)S(1)}, f32[16384,16]{0,1:T(8,128)}, u32[]{:S(2)}) copy-start(f32[16384,16]{0,1:T(8,128)} %fusion.78) | copy-start | bytes 3145732
  774.5 21.2 %collective-permute-start.5 = (f32[32,1024]{1,0:T(8,128)S(1)}, f32[32,1024]{1,0:T(8,128)S(1)}, u32[]{:S(2)}, u32[]{:S(2)}) collective-permute-start(f32[32,1024]{1,0:T(8,128)S(1)} %get-tuple-element.511), channel_id=1, source_target_pairs={{1,0},{2,1},{3,2},{4,3},{5,4},{6,5},{7,6},{8,7},{9,8},{10,9},{11,1... | collective-permute-start | bytes 393224 | tf_op jit(solution)/shard_map/ppermute | solution.py:24
  775.8 19.9 %collective-permute-start.4 = (f32[32,1024]{1,0:T(8,128)S(1)}, f32[32,1024]{1,0:T(8,128)S(1)}, u32[]{:S(2)}, u32[]{:S(2)}) collective-permute-start(f32[32,1024]{1,0:T(8,128)S(1)} %get-tuple-element.510), channel_id=1, source_target_pairs={{0,1},{1,2},{2,3},{3,4},{4,5},{5,6},{6,7},{7,8},{8,9},{9,10},{10,1... | collective-permute-start | bytes 393224 | tf_op jit(solution)/shard_map/ppermute | solution.py:22
  948.1 17.1 %slice-start = ((s8[8388608]{0:T(1024)(128)(4,1)}), s8[4194304]{0:T(1024)(128)(4,1)S(1)}, s32[]{:S(2)}) async-start(s8[8388608]{0:T(1024)(128)(4,1)} %bitcast.168), calls=%async_computation.5 | async-start | bytes 8388608
  948.2 17.0 %slice-start.1 = ((s8[8388608]{0:T(1024)(128)(4,1)}), s8[4194304]{0:T(1024)(128)(4,1)S(1)}, s32[]{:S(2)}) async-start(s8[8388608]{0:T(1024)(128)(4,1)} %bitcast.168), calls=%async_computation.6 | async-start | bytes 8388608
  948.2 17.0 %copy-start.6 = (f32[16384,16]{0,1:T(8,128)S(1)}, f32[16384,16]{0,1:T(8,128)}, u32[]{:S(2)}) copy-start(f32[16384,16]{0,1:T(8,128)} %convolution_add_fusion.1) | copy-start | bytes 3145732
  986.1 8.0 copy-start.5
where the time goes:
time: 1010 us; the launch traced here: 996 us
  local copies, waits for them, and re-layouts  232 us (23%)
  matrix products  232 us (23%)
  other arithmetic  231 us (23%)
  blocking collectives  197 us (20%)
  waiting for transfers between devices  64.7 us (6%)
  starting transfers between devices  35.8 us (4%)
    add x36, other arithmetic, add_slot(): return bucket + chosen_weights.T[:, :, None] * difference[None]  137 us
    dot_general x6, matrix products, cross_gram(): jnp.dot(left_flat.T, right_flat, precision=lax.Precision.HIGHEST, preferr...  111 us
    dot_general x8, matrix products, times_small(): jnp.dot(flat, matrix, precision=lax.Precision.HIGHEST, preferred_element_...  106 us
    psum x1, blocking collectives, on_device(): residual_gram = lax.psum(cross_gram(residual, residual, cases), 'sub')  74.5 us
    all_to_all x5, waiting for transfers between devices, on_device(): lax.all_to_all(outgoing, 'sub', split_axis=0, concat_axis=0, tiled=True)  64.7 us
    psum x2, blocking collectives, on_device(): curvature_gram = lax.psum(cross_gram(direction, applied, cases), 'sub')  62.3 us
    psum x2, blocking collectives, on_device(): next_gram = lax.psum(cross_gram(residual, residual, cases), 'sub')  60 us
    sub x36, other arithmetic, add_slot(): difference = vector_in - jnp.take(padded, chosen_cols, axis=0)  50.1 us
  transfers between devices with their start and end apart: 11, of which 5 were waited for; matrix products, arithmetic and copies ran while one was open for 8% of the time, Pallas kernels for 0%

commit v1 on v0

v1 whole, which is shorter than its diff:
```python
import functools

import jax
import jax.numpy as jnp
from jax import lax
from jax.experimental import pallas as pl
from jax.experimental.pallas import tpu as pltpu
from jax.sharding import PartitionSpec as P

HALO = 32
TYPES = 3
ITERS = 3
MASS_SHIFT = 0.5
META = 128
TILE = 256

F32 = jnp.float32
BF16 = jnp.bfloat16
VMEM = pl.BlockSpec(memory_space=pltpu.VMEM)
SMEM = pl.BlockSpec(memory_space=pltpu.SMEM)
PARAMS = pltpu.CompilerParams(vmem_limit_bytes=40 * 1024 * 1024)


def dot(left, right):
    return jnp.dot(left, right, preferred_element_type=F32)


def dot_nt(left, right):
    return lax.dot_general(left, right, (((1,), (1,)), ((), ())), preferred_element_type=F32)


def dot_tn(left, right):
    return lax.dot_general(left, right, (((0,), (0,)), ((), ())), preferred_element_type=F32)


def halves(value):
    high = value.astype(BF16)
    return high, (value - high.astype(F32)).astype(BF16)


def iota(shape, axis):
    return lax.broadcasted_iota(jnp.int32, shape, axis)


def one_hot(condition):
    return jnp.where(condition, 1.0, 0.0).astype(BF16)


def basis_shift(blocks, slots):
    dof = blocks.shape[1]
    same = iota((dof, dof), 0) == iota((dof, dof), 1)
    total = sum(jnp.where(same, blocks[t], 0.0) for t in range(TYPES))
    mean = jnp.sum(jnp.sum(total, axis=1, keepdims=True), axis=0, keepdims=True) / (TYPES * dof)
    return MASS_SHIFT + 0.2 * slots * mean


def pack_kernel(devices, pos_ref, loads_ref, rows_ref, dens_ref, cols_ref, types_ref,
                left_ref, right_ref, partner_ref, meta_ref):
    rows, width = loads_ref.shape
    slots = dens_ref.shape[0]
    cap = rows // 4
    pos = pos_ref[0, 0]
    ids = rows_ref[...]
    owner = lax.div(ids, jnp.int32(rows))
    local = (ids - owner * rows + 1).astype(F32)
    kept = owner == pos
    opposite = lax.rem(pos + devices // 2, jnp.int32(devices))
    goes = [owner == pos - 1, owner == pos + 1]
    goes.append((owner == opposite) & ~goes[0] & ~goes[1])
    flags = jnp.concatenate(
        [jnp.where(g, 1.0, 0.0) for g in goes] + [jnp.zeros((5, rows), F32)], axis=0
    )
    before = one_hot(iota((rows, rows), 0) < iota((rows, rows), 1))
    rank = dot(flags.astype(BF16), before).astype(jnp.int32)
    target = jnp.full((1, rows), -1, jnp.int32)
    for side in range(3):
        target = jnp.where(goes[side], rank[side:side + 1] + side * cap, target)
    pick = one_hot(iota((3 * cap, rows), 0) == target)

    density = dens_ref[...]
    kinds = types_ref[...]
    for kind in range(TYPES):
        meta_ref[kind * slots:(kind + 1) * slots, :] = jnp.where(kinds == kind, density, 0.0)
    meta_ref[3 * slots:4 * slots, :] = (cols_ref[...] - ids).astype(F32)
    meta_ref[4 * slots:, :] = jnp.zeros((META - 4 * slots, rows), F32)
    meta_ref[4 * slots:4 * slots + 1, :] = local
    meta_ref[4 * slots + 1:4 * slots + 2, :] = jnp.where(kept, local, 0.0)

    twice = jnp.concatenate([pick, pick], axis=1)
    body = dot(twice, jnp.concatenate(halves(loads_ref[...]), axis=0))
    meta = dot_nt(twice, jnp.concatenate(halves(meta_ref[...]), axis=1))
    for side, out_ref in enumerate((left_ref, right_ref, partner_ref)):
        out_ref[:, :width] = body[side * cap:(side + 1) * cap]
        out_ref[:, width:] = meta[side * cap:(side + 1) * cap]


def lane_order(width, dof, transpose):
    cases = width // dof
    source = iota((width, width), 1 if transpose else 0)
    target = iota((width, width), 0 if transpose else 1)
    return one_hot(target == (source % cases) * dof + source // cases)


def arrange_kernel(dof, slots, loads_ref, meta_ref, left_ref, right_ref, partner_ref,
                   geo_ref, field_ref, geo_meta_ref, head_ref, tail_ref):
    rows, width = loads_ref.shape
    edge = head_ref.shape[0]
    arrived = jnp.concatenate([left_ref[...], right_ref[...], partner_ref[...]], axis=0)
    count = arrived.shape[0]
    arrived_meta = arrived[:, width:]
    unit = one_hot(iota((8, META), 1) == 4 * slots)
    tags = dot_nt(unit, arrived_meta.astype(BF16))[0:1]
    place = iota((rows, rows), 0) + 1
    own = one_hot(place == meta_ref[4 * slots + 1:4 * slots + 2, :].astype(jnp.int32))
    other = one_hot(iota((rows, count), 0) + 1 == tags.astype(jnp.int32))

    parts = []
    for part_own, part_other in zip(halves(loads_ref[...]), halves(arrived[:, :width])):
        parts.append((dot(own, part_own) + dot(other, part_other)).astype(BF16))
    both = jnp.concatenate(parts, axis=0)
    geo_ref[...] = both
    meta = dot_nt(
        jnp.concatenate([own, own], axis=1), jnp.concatenate(halves(meta_ref[...]), axis=1)
    )
    for part in halves(arrived_meta):
        meta += dot(other, part)
    geo_meta_ref[...] = meta

    moved = dot(both, lane_order(width, dof, False))
    field = moved[:rows] + moved[rows:]
    field_ref[...] = field
    head_ref[:, :width] = field[:edge]
    head_ref[:, width:] = meta[:edge]
    tail_ref[:, :width] = field[rows - edge:]
    tail_ref[:, width:] = meta[rows - edge:]


def krylov_kernel(slots, before_ref, field_ref, meta_ref, after_ref, blocks_ref, geo_ref,
                  basis_ref, moments_ref, v_refs, ext_meta, stencil, mixer):
    rows, width = field_ref.shape
    dof = blocks_ref.shape[1]
    cases = width // dof
    tiles = width // TILE
    edge = before_ref.shape[0]
    span = rows + 2 * edge
    half = (span - 2 * HALO) // 2
    window = half + 2 * HALO
    chunks = half // HALO

    shift = basis_shift(blocks_ref[...], slots)

    fold = one_hot(iota((TILE, dof), 0) % dof == iota((TILE, dof), 1))
    unfold = one_hot(iota((dof, TILE), 1) % dof == iota((dof, TILE), 0))
    same_case = iota((TILE, TILE), 0) // dof == iota((TILE, TILE), 1) // dof
    for kind in range(TYPES):
        for copies, part in zip(((0, 2), (1,)), halves(blocks_ref[kind])):
            spread = dot(dot_nt(fold, part).astype(BF16), unfold)
            spread = jnp.where(same_case, spread, 0.0).astype(BF16)
            for copy in copies:
                start = (copy * TYPES + kind) * TILE
                mixer[start:start + TILE, :] = spread

    ext_meta[:edge, :] = before_ref[:, width:]
    ext_meta[edge:edge + rows, :] = meta_ref[...]
    ext_meta[edge + rows:, :] = after_ref[:, width:]

    def build(chunk, carry):
        part = lax.div(chunk, jnp.int32(chunks))
        first = pl.multiple_of(lax.rem(chunk, jnp.int32(chunks)) * HALO, HALO)
        meta = ext_meta[pl.ds(pl.multiple_of(HALO + chunk * HALO, HALO), HALO), :]
        lane = iota((HALO, META), 1)
        spot = iota((HALO, window), 1)
        centre = iota((HALO, 1), 0) + (first + HALO)
        sums = [jnp.zeros((HALO, window), F32) for _ in range(TYPES)]
        for slot in range(slots):
            column = centre + meta[:, 3 * slots + slot:3 * slots + slot + 1].astype(jnp.int32)
            hit = spot == column
            for kind in range(TYPES):
                weight = meta[:, kind * slots + slot:kind * slots + slot + 1]
                sums[kind] += jnp.where(hit, weight, 0.0)
        for kind in range(TYPES):
            inside = (lane >= kind * slots) & (lane < (kind + 1) * slots)
            total = jnp.sum(jnp.where(inside, meta, 0.0), axis=1, keepdims=True)
            high, low = halves(jnp.where(spot == centre, total, 0.0) - sums[kind])
            stencil[part, kind, pl.ds(first, HALO), 0:window] = high
            stencil[part, kind, pl.ds(first, HALO), window:2 * window] = high
            stencil[part, kind, pl.ds(first, HALO), 2 * window:3 * window] = low
        return carry

    lax.fori_loop(0, 2 * chunks, build, 0)

    for tile in range(tiles):
        lanes = slice(tile * TILE, (tile + 1) * TILE)
        for start, source in ((0, before_ref), (edge, field_ref), (edge + rows, after_ref)):
            high, low = halves(source[:, lanes])
            v_refs[0, 0, tile, start:start + high.shape[0], :] = high
            v_refs[0, 1, tile, start:start + high.shape[0], :] = low
        for step in range(1, ITERS):
            for part in range(2):
                blank = jnp.zeros((HALO * step, TILE), BF16)
                v_refs[step, part, tile, :HALO * step, :] = blank
                v_refs[step, part, tile, span - HALO * step:, :] = blank

    def advance(tile, carry):
        for step in range(ITERS):
            for part in range(2):
                low_row = HALO * step if part == 0 else 0
                high_row = half if part == 0 else half - HALO * step
                count = high_row - low_row
                start = part * half
                first = start + HALO + low_row
                near = v_refs[step, 0, tile, start:start + window, :]
                fine = v_refs[step, 1, tile, start:start + window, :]
                gather = jnp.concatenate(
                    [stencil[part, kind, low_row:high_row, :] for kind in range(TYPES)], axis=0
                )
                bucket = dot(gather, jnp.concatenate([near, fine, near], axis=0))
                high, low = halves(bucket)
                highs = [high[kind * count:(kind + 1) * count] for kind in range(TYPES)]
                lows = [low[kind * count:(kind + 1) * count] for kind in range(TYPES)]
                applied = dot(jnp.concatenate(highs + highs + lows, axis=1), mixer[...])
                here = (
                    v_refs[step, 0, tile, first:first + count, :].astype(F32)
                    + v_refs[step, 1, tile, first:first + count, :].astype(F32)
                )
                high, low = halves(applied + (MASS_SHIFT - shift) * here)
                v_refs[step + 1, 0, tile, first:first + count, :] = high
                v_refs[step + 1, 1, tile, first:first + count, :] = low
        return carry

    lax.fori_loop(0, tiles, advance, 0)

    back = lane_order(width, dof, True)
    for step in range(1, ITERS + 1):
        both = jnp.concatenate(
            [
                jnp.concatenate(
                    [v_refs[step, part, tile, edge:edge + rows, :] for tile in range(tiles)],
                    axis=1,
                )
                for part in range(2)
            ],
            axis=0,
        )
        basis_ref[step - 1] = dot(both, back).astype(BF16)

    def stacked(step, order):
        pieces = []
        for tile in range(tiles):
            lanes = slice(tile * TILE, (tile + 1) * TILE)
            for part in order:
                block = slice(part * rows, (part + 1) * rows)
                if step == 0:
                    pieces.append(geo_ref[block, lanes])
                else:
                    pieces.append(basis_ref[step - 1, block, lanes])
        return jnp.concatenate(pieces, axis=0)

    same_dof = iota((TILE, TILE), 0) // cases == iota((TILE, TILE), 1) // cases
    group = iota((cases, META), 1) // cases
    moments = jnp.zeros((cases, META), F32)
    for number in range(2 * ITERS):
        left, right = number // 2, (number + 1) // 2
        gram = dot_tn(stacked(left, (0, 0, 1)), stacked(right, (0, 1, 0)))
        gram = jnp.where(same_dof, gram, 0.0)
        rows_sum = gram[0:cases]
        for part in range(1, TILE // cases):
            rows_sum = rows_sum + gram[part * cases:(part + 1) * cases]
        lanes_sum = rows_sum[:, :META] + rows_sum[:, META:]
        step = META // 2
        while step >= cases:
            lanes_sum = lanes_sum + pltpu.roll(lanes_sum, step, 1)
            step //= 2
        moments = jnp.where(group == number, lanes_sum, moments)
    for device in range(moments_ref.shape[0]):
        moments_ref[device] = moments


def finish_kernel(slots, moments_ref, blocks_ref, geo_ref, basis_ref, solution_ref, residual_ref):
    rows, width = solution_ref.shape
    dof = blocks_ref.shape[1]
    cases = width // dof
    tiles = width // TILE
    shift = basis_shift(blocks_ref[...], slots)
    moments = moments_ref[0]
    for device in range(1, moments_ref.shape[0]):
        moments = moments + moments_ref[device]
    group = iota((cases, META), 1) // cases
    system = []
    for row in range(ITERS):
        plain = moments if row == 0 else pltpu.roll(moments, META - cases * row, 1)
        ahead = pltpu.roll(moments, META - cases * (row + 1), 1)
        target = pltpu.roll(moments, cases * (ITERS - row), 1)
        system.append(jnp.where(group < ITERS, ahead + shift * plain, target))
    system = jnp.concatenate(system, axis=0)
    size = ITERS * cases
    index = iota((size, 1), 0)
    for pivot in range(size):
        column = system[:, pivot:pivot + 1]
        line = system[pivot:pivot + 1, :]
        line = line / line[:, pivot:pivot + 1]
        system = jnp.where(index == pivot, line, system - column * line)

    same_dof = iota((TILE, TILE), 0) // cases == iota((TILE, TILE), 1) // cases
    unit = jnp.where(iota((cases, META), 1) % cases == iota((cases, META), 0), 1.0, 0.0)

    answers = []
    for row in range(ITERS):
        part = jnp.where(group == ITERS, system[row * cases:(row + 1) * cases], 0.0)
        step = cases
        while step < META:
            part = part + pltpu.roll(part, step, 1)
            step *= 2
        answers.append(part)
    left_over = [unit - shift * answers[0]]
    for row in range(1, ITERS):
        left_over.append(-(answers[row - 1] + shift * answers[row]))
    left_over.append(-answers[ITERS - 1])

    def spread(parts):
        highs, lows = [], []
        for part in parts:
            tall = jnp.concatenate([part] * (TILE // cases), axis=0)
            wide = jnp.concatenate([tall] * (TILE // META), axis=1)
            high, low = halves(jnp.where(same_dof, wide, 0.0))
            highs.append(high)
            lows.append(low)
        return jnp.concatenate(highs + highs + lows, axis=0)

    for out_ref, matrix in ((solution_ref, spread(answers)), (residual_ref, spread(left_over))):
        terms = matrix.shape[0] // (3 * TILE)
        for tile in range(tiles):
            lanes = slice(tile * TILE, (tile + 1) * TILE)
            highs, lows = [], []
            for term in range(terms):
                for part, pile in ((0, highs), (1, lows)):
                    block = slice(part * rows, (part + 1) * rows)
                    if term == 0:
                        pile.append(geo_ref[block, lanes])
                    else:
                        pile.append(basis_ref[term - 1, block, lanes])
            out_ref[:, lanes] = dot(jnp.concatenate(highs + lows + highs, axis=1), matrix)


def on_device(loads, row_ids, densities, block_cols, block_types, ref_blocks):
    rows, width = loads.shape
    dof = ref_blocks.shape[1]
    slots = densities.shape[1]
    cases = width // dof
    cap = rows // 4
    edge = ITERS * HALO
    span = rows + 2 * edge
    half = (span - 2 * HALO) // 2
    window = half + 2 * HALO
    tiles = width // TILE
    devices = lax.axis_size("sub")
    position = lax.axis_index("sub").astype(jnp.int32).reshape(1, 1)
    shape = jax.ShapeDtypeStruct
    up = [(i, i + 1) for i in range(devices - 1)]
    down = [(i + 1, i) for i in range(devices - 1)]
    across = [(i, (i + devices // 2) % devices) for i in range(devices)]

    block = shape((cap, width + META), F32)
    to_left, to_right, to_partner, meta = pl.pallas_call(
        functools.partial(pack_kernel, devices),
        out_shape=(block, block, block, shape((META, rows), F32)),
        in_specs=[SMEM] + [VMEM] * 5,
        out_specs=(VMEM,) * 4,
        compiler_params=PARAMS,
        name="pack",
    )(position, loads, row_ids.reshape(1, rows), densities.T, block_cols.T, block_types.T)

    from_right = lax.ppermute(to_left, "sub", down)
    from_left = lax.ppermute(to_right, "sub", up)
    from_partner = lax.ppermute(to_partner, "sub", across)

    border = shape((edge, width + META), F32)
    geo, field, geo_meta, head, tail = pl.pallas_call(
        functools.partial(arrange_kernel, dof, slots),
        out_shape=(
            shape((2 * rows, width), BF16),
            shape((rows, width), F32),
            shape((rows, META), F32),
            border,
            border,
        ),
        in_specs=[VMEM] * 5,
        out_specs=(VMEM,) * 5,
        compiler_params=PARAMS,
        name="arrange",
    )(loads, meta, from_left, from_right, from_partner)

    after = lax.ppermute(head, "sub", down)
    before = lax.ppermute(tail, "sub", up)

    basis, moments = pl.pallas_call(
        functools.partial(krylov_kernel, slots),
        out_shape=(
            shape((ITERS, 2 * rows, width), BF16),
            shape((devices, cases, META), F32),
        ),
        in_specs=[VMEM] * 6,
        out_specs=(VMEM,) * 2,
        scratch_shapes=[
            pltpu.VMEM((ITERS + 1, 2, tiles, span, TILE), BF16),
            pltpu.VMEM((span, META), F32),
            pltpu.VMEM((2, TYPES, half, 3 * window), BF16),
            pltpu.VMEM((3 * TYPES * TILE, TILE), BF16),
        ],
        compiler_params=PARAMS,
        name="krylov",
    )(before, field, geo_meta, after, ref_blocks, geo)

    moments = lax.all_to_all(moments, "sub", split_axis=0, concat_axis=0, tiled=True)

    return pl.pallas_call(
        functools.partial(finish_kernel, slots),
        out_shape=(shape((rows, width), F32), shape((rows, width), F32)),
        in_specs=[VMEM] * 4,
        out_specs=(VMEM,) * 2,
        compiler_params=PARAMS,
        name="finish",
    )(moments, ref_blocks, geo, basis)


def solution(mesh):
    placed = (
        P(("groups", "sub"), None),
        P(("groups", "sub")),
        P(("groups", "sub"), None),
        P(("groups", "sub"), None),
        P(("groups", "sub"), None),
        P(),
    )
    return jax.shard_map(
        on_device,
        mesh=mesh,
        in_specs=placed,
        out_specs=(P(("groups", "sub"), None), P(("groups", "sub"), None)),
        check_vma=False,
    )
```

time: 1010 us -> 95 us (0.09); the launches traced: 996 us -> 94.5 us
  matrix products: 232 us -> 0 us
  other arithmetic: 231 us -> 0 us
  local copies, waits for them, and re-layouts: 232 us -> 5.28 us
  blocking collectives: 197 us -> 19.1 us
  waiting for transfers between devices: 64.7 us -> 18.1 us
  Pallas kernels: 0 us -> 38.2 us
  starting transfers between devices: 35.8 us -> 13.2 us
    dot_general x17 -> x0, matrix products: 230 us -> none  [the longest x6 111 us: cross_gram(): jnp.dot(left_flat.T, right_flat, precision=lax.Precision.HIGHEST, preferr...]
    psum x5 -> x0, blocking collectives: 197 us -> none  [the longest x1 74.5 us: on_device(): residual_gram = lax.psum(cross_gram(residual, residual, cases), 'sub')]
    add x42 -> x0, other arithmetic: 142 us -> none  [the longest x36 137 us: add_slot(): return bucket + chosen_weights.T[:, :, None] * difference[None]]
    reshape x16 -> x0, local copies, waits for them, and re-layouts: 93.8 us -> none  [the longest x5 39.6 us: times_small(): return jnp.dot(flat, matrix, precision=lax.Precision.HIGHEST, preferred_e...]
    all_to_all x5 -> x0, waiting for transfers between devices: 64.7 us -> none  [on_device(): lax.all_to_all(outgoing, 'sub', split_axis=0, concat_axis=0, tiled=True)]
    sub x39 -> x0, other arithmetic: 51.5 us -> none  [the longest x36 50.1 us: add_slot(): difference = vector_in - jnp.take(padded, chosen_cols, axis=0)]
    gather x36 -> x0, local copies, waits for them, and re-layouts: 49.9 us -> none  [add_slot(): difference = vector_in - jnp.take(padded, chosen_cols, axis=0)]
    pallas_call x0 -> x4, Pallas kernels: none -> 38.2 us  [the longest x1 26.9 us: on_device(): pl.pallas_call(functools.partial(krylov_kernel, slots), out_shape=(shape(...]
  transfers between devices with their start and end apart: 11 -> 5, of which waited for: 5 -> 3; matrix products, arithmetic and copies ran while one was open for 8% -> 0% of each run, Pallas kernels for 0% -> 0%
where the time goes in v1:
time: 95 us; the launch traced here: 94.5 us
  Pallas kernels  38.2 us (40%)
  blocking collectives  19.1 us (20%)
  waiting for transfers between devices  18.1 us (19%)
  starting transfers between devices  13.2 us (14%)
  local copies, waits for them, and re-layouts  5.28 us (6%)
    pallas_call x1, Pallas kernels, on_device(): pl.pallas_call(functools.partial(krylov_kernel, slots), out_shape=(shape(...  26.9 us
    all_to_all x1, blocking collectives, on_device(): lax.all_to_all(moments, 'sub', split_axis=0, concat_axis=0, tiled=True)  19.1 us
    ppermute x1, waiting for transfers between devices, on_device(): from_partner = lax.ppermute(to_partner, 'sub', across)  15.7 us
    pallas_call x1, Pallas kernels, on_device(): pl.pallas_call(functools.partial(finish_kernel, slots), out_shape=(shape(...  8.51 us
    ppermute x1, starting transfers between devices, on_device(): from_partner = lax.ppermute(to_partner, 'sub', across)  6.89 us
    unnamed x14, local copies, waits for them, and re-layouts  5.28 us
    ppermute x1, starting transfers between devices, on_device(): from_left = lax.ppermute(to_right, 'sub', up)  2.38 us
    ppermute x1, waiting for transfers between devices, on_device(): after = lax.ppermute(head, 'sub', down)  2.31 us
  transfers between devices with their start and end apart: 5, of which 3 were waited for; matrix products, arithmetic and copies ran while one was open for 0% of the time, Pallas kernels for 0%

profile of v1, /device:TPU:0, one launch (start us, length us, event | category | flops | bytes accessed | tf_op | source)
XLA Modules:
  0.0 94.5 jit_solution(4629691402708844918)
XLA Ops:
  0.6 0.0 copy-start
  0.6 1.2 %copy-done = f32[256,1024]{1,0:T(8,128)S(1)} copy-done((f32[256,1024]{1,0:T(8,128)S(1)}, f32[256,1024]{1,0:T(8,128)}, u32[]{:S(2)}) %copy-start) | copy-done | bytes 1048600
  1.9 0.0 copy-start.3
  1.9 0.7 copy-done.3
  2.6 0.0 copy-start.4
  2.6 0.7 copy-done.4
  3.3 0.0 copy-start.5
  3.3 0.7 copy-done.5
  4.0 0.0 copy-start.6
  4.0 0.7 copy-done.6
  4.7 0.0 copy-start.2
  4.7 0.6 pack.1
  5.3 2.4 %collective-permute-start = (f32[64,1152]{1,0:T(8,128)S(1)}, f32[64,1152]{1,0:T(8,128)S(1)}, u32[]{:S(2)}, u32[]{:S(2)}) collective-permute-start(f32[64,1152]{1,0:T(8,128)S(1)} %get-tuple-element.14), channel_id=1, source_target_pairs={{0,1},{1,2},{2,3},{3,4},{4,5},{5,6},{6,7},{7,8},{8,9},{9,10},{10,1... | collective-permute-start | bytes 884744 | tf_op jit(solution)/shard_map/ppermute | solution.py:374
  7.7 1.3 %collective-permute-start.1 = (f32[64,1152]{1,0:T(8,128)S(1)}, f32[64,1152]{1,0:T(8,128)S(1)}, u32[]{:S(2)}, u32[]{:S(2)}) collective-permute-start(f32[64,1152]{1,0:T(8,128)S(1)} %get-tuple-element.15), channel_id=1, source_target_pairs={{1,0},{2,1},{3,2},{4,3},{5,4},{6,5},{7,6},{8,7},{9,8},{10,9},{11,1... | collective-permute-start | bytes 884744 | tf_op jit(solution)/shard_map/ppermute | solution.py:373
  9.0 6.9 %collective-permute-start.2 = (f32[64,1152]{1,0:T(8,128)S(1)}, f32[64,1152]{1,0:T(8,128)S(1)}, u32[]{:S(2)}, u32[]{:S(2)}) collective-permute-start(f32[64,1152]{1,0:T(8,128)S(1)} %get-tuple-element.16), channel_id=1, source_target_pairs={{0,8},{1,9},{2,10},{3,11},{4,12},{5,13},{6,14},{7,15},{8,0},{9,1},... | collective-permute-start | bytes 884744 | tf_op jit(solution)/shard_map/ppermute | solution.py:375
  15.9 0.0 collective-permute-done.left_ref
  15.9 0.0 collective-permute-done.1.right_ref
  15.9 15.7 %collective-permute-done.2.partner_ref = f32[64,1152]{1,0:T(8,128)S(1)} collective-permute-done((f32[64,1152]{1,0:T(8,128)S(1)}, f32[64,1152]{1,0:T(8,128)S(1)}, u32[]{:S(2)}, u32[]{:S(2)}) %collective-permute-start.2) | collective-permute-done | bytes 294944 | tf_op jit(solution)/shard_map/ppermute | solution.py:375
  31.6 0.0 copy-start.1
  31.6 1.2 %copy-done.1 = f32[256,1024]{1,0:T(8,128)S(1)} copy-done((f32[256,1024]{1,0:T(8,128)S(1)}, f32[256,1024]{1,0:T(8,128)}, u32[]{:S(2)}) %copy-start.1) | copy-done | bytes 1048600
  32.8 2.1 %arrange.1 = (bf16[512,1024]{1,0:T(8,128)(2,1)S(1)}, f32[256,1024]{1,0:T(8,128)S(1)}, f32[256,128]{1,0:T(8,128)S(1)}, f32[96,1152]{1,0:T(8,128)S(1)}, f32[96,1152]{1,0:T(8,128)S(1)}) custom-call(f32[256,1024]{1,0:T(8,128)S(1)} %copy-done.1, f32[128,256]{1,0:T(8,128)S(1)} %get-tuple-element.13.meta_ref, f32[64,1152]{1,0:T(8,128)S(1)} %collective-permute-done.left_ref, ...), custom_call_target="tpu_custom_call" | custom-call | tf_op jit(solution)/shard_map/arrange/pallas_call | solution.py:378
  34.9 1.3 %collective-permute-start.3 = (f32[96,1152]{1,0:T(8,128)S(1)}, f32[96,1152]{1,0:T(8,128)S(1)}, u32[]{:S(2)}, u32[]{:S(2)}) collective-permute-start(f32[96,1152]{1,0:T(8,128)S(1)} %get-tuple-element.17), channel_id=1, source_target_pairs={{0,1},{1,2},{2,3},{3,4},{4,5},{5,6},{6,7},{7,8},{8,9},{9,10},{10,1... | collective-permute-start | bytes 1327112 | tf_op jit(solution)/shard_map/ppermute | solution.py:394
  36.2 1.3 %collective-permute-start.4 = (f32[96,1152]{1,0:T(8,128)S(1)}, f32[96,1152]{1,0:T(8,128)S(1)}, u32[]{:S(2)}, u32[]{:S(2)}) collective-permute-start(f32[96,1152]{1,0:T(8,128)S(1)} %get-tuple-element.20), channel_id=1, source_target_pairs={{1,0},{2,1},{3,2},{4,3},{5,4},{6,5},{7,6},{8,7},{9,8},{10,9},{11,1... | collective-permute-start | bytes 1327112 | tf_op jit(solution)/shard_map/ppermute | solution.py:393
  37.5 0.1 collective-permute-done.3.before_ref
  37.6 2.3 %collective-permute-done.4.after_ref = f32[96,1152]{1,0:T(8,128)S(1)} collective-permute-done((f32[96,1152]{1,0:T(8,128)S(1)}, f32[96,1152]{1,0:T(8,128)S(1)}, u32[]{:S(2)}, u32[]{:S(2)}) %collective-permute-start.4) | collective-permute-done | bytes 442400 | tf_op jit(solution)/shard_map/ppermute | solution.py:393
  39.9 0.0 copy-done.2
  39.9 26.9 %krylov.1 = (bf16[3,512,1024]{2,1,0:T(8,128)(2,1)S(1)}, f32[16,16,128]{2,1,0:T(8,128)S(1)}) custom-call(f32[96,1152]{1,0:T(8,128)S(1)} %collective-permute-done.3.before_ref, f32[256,1024]{1,0:T(8,128)S(1)} %get-tuple-element.18.field_ref, f32[256,128]{1,0:T(8,128)S(1)} %get-tuple-element.19.meta_ref, f32[96,1152]{1,0:T(8,128)S(1)} %collective-permute-done.4.after_ref, ...), custom_call_target="tpu_custom_call" | custom-call | tf_op jit(solution)/shard_map/krylov/pallas_call | solution.py:396
  66.9 19.1 %all_to_all.5.moments_ref = f32[16,16,128]{2,1,0:T(8,128)S(1)} all-to-all(f32[16,16,128]{2,1,0:T(8,128)S(1)} %get-tuple-element.22), channel_id=1, replica_groups=mesh['groups'=2,'sub'=16] {'sub'}, dimensions={0} | all-to-all | bytes 262144 | tf_op jit(solution)/shard_map/all_to_all | solution.py:414
  86.0 8.5 %finish.1 = (f32[256,1024]{1,0:T(8,128)}, f32[256,1024]{1,0:T(8,128)}) custom-call(f32[16,16,128]{2,1,0:T(8,128)S(1)} %all_to_all.5.moments_ref, f32[3,64,64]{2,1,0:T(8,128)S(1)} %copy-done.2, bf16[512,1024]{1,0:T(8,128)(2,1)S(1)} %get-tuple-element.21.geo_ref, bf16[3,512,1024]{2,1,0:T(8,128)(2,1)S(1)} %get-tuple-element.23.basis_ref), custom_call_target="tpu_custom_call" | custom-call | tf_op jit(solution)/shard_map/finish/pallas_call | solution.py:416
Async XLA Ops:
  0.6 1.2 %copy-start = (f32[256,1024]{1,0:T(8,128)S(1)}, f32[256,1024]{1,0:T(8,128)}, u32[]{:S(2)}) copy-start(f32[256,1024]{1,0:T(8,128)} %loads_ref.3) | copy-start | bytes 3145732
  1.9 0.7 copy-start.3
  2.6 0.7 copy-start.4
  3.3 0.7 copy-start.5
  4.0 0.7 copy-start.6
  4.7 35.2 %copy-start.2 = (f32[3,64,64]{2,1,0:T(8,128)S(1)}, f32[3,64,64]{2,1,0:T(8,128)}, u32[]{:S(2)}) copy-start(f32[3,64,64]{2,1,0:T(8,128)} %blocks_ref.3) | copy-start | bytes 147460
  5.3 10.6 %collective-permute-start = (f32[64,1152]{1,0:T(8,128)S(1)}, f32[64,1152]{1,0:T(8,128)S(1)}, u32[]{:S(2)}, u32[]{:S(2)}) collective-permute-start(f32[64,1152]{1,0:T(8,128)S(1)} %get-tuple-element.14), channel_id=1, source_target_pairs={{0,1},{1,2},{2,3},{3,4},{4,5},{5,6},{6,7},{7,8},{8,9},{9,10},{10,1... | collective-permute-start | bytes 884744 | tf_op jit(solution)/shard_map/ppermute | solution.py:374
  7.7 8.2 %collective-permute-start.1 = (f32[64,1152]{1,0:T(8,128)S(1)}, f32[64,1152]{1,0:T(8,128)S(1)}, u32[]{:S(2)}, u32[]{:S(2)}) collective-permute-start(f32[64,1152]{1,0:T(8,128)S(1)} %get-tuple-element.15), channel_id=1, source_target_pairs={{1,0},{2,1},{3,2},{4,3},{5,4},{6,5},{7,6},{8,7},{9,8},{10,9},{11,1... | collective-permute-start | bytes 884744 | tf_op jit(solution)/shard_map/ppermute | solution.py:373
  9.0 22.6 %collective-permute-start.2 = (f32[64,1152]{1,0:T(8,128)S(1)}, f32[64,1152]{1,0:T(8,128)S(1)}, u32[]{:S(2)}, u32[]{:S(2)}) collective-permute-start(f32[64,1152]{1,0:T(8,128)S(1)} %get-tuple-element.16), channel_id=1, source_target_pairs={{0,8},{1,9},{2,10},{3,11},{4,12},{5,13},{6,14},{7,15},{8,0},{9,1},... | collective-permute-start | bytes 884744 | tf_op jit(solution)/shard_map/ppermute | solution.py:375
  31.6 1.2 %copy-start.1 = (f32[256,1024]{1,0:T(8,128)S(1)}, f32[256,1024]{1,0:T(8,128)}, u32[]{:S(2)}) copy-start(f32[256,1024]{1,0:T(8,128)} %loads_ref.3) | copy-start | bytes 3145732
  34.9 2.7 %collective-permute-start.3 = (f32[96,1152]{1,0:T(8,128)S(1)}, f32[96,1152]{1,0:T(8,128)S(1)}, u32[]{:S(2)}, u32[]{:S(2)}) collective-permute-start(f32[96,1152]{1,0:T(8,128)S(1)} %get-tuple-element.17), channel_id=1, source_target_pairs={{0,1},{1,2},{2,3},{3,4},{4,5},{5,6},{6,7},{7,8},{8,9},{9,10},{10,1... | collective-permute-start | bytes 1327112 | tf_op jit(solution)/shard_map/ppermute | solution.py:394
  36.2 3.7 %collective-permute-start.4 = (f32[96,1152]{1,0:T(8,128)S(1)}, f32[96,1152]{1,0:T(8,128)S(1)}, u32[]{:S(2)}, u32[]{:S(2)}) collective-permute-start(f32[96,1152]{1,0:T(8,128)S(1)} %get-tuple-element.20), channel_id=1, source_target_pairs={{1,0},{2,1},{3,2},{4,3},{5,4},{6,5},{7,6},{8,7},{9,8},{10,9},{11,1... | collective-permute-start | bytes 1327112 | tf_op jit(solution)/shard_map/ppermute | solution.py:393

commit v2 on v1

v2 whole, which is shorter than its diff:
```python
import functools

import jax
import jax.numpy as jnp
from jax import lax
from jax.experimental import pallas as pl
from jax.experimental.pallas import tpu as pltpu
from jax.sharding import PartitionSpec as P

HALO = 32
TYPES = 3
ITERS = 3
MASS_SHIFT = 0.5
META = 128
TILE = 256

F32 = jnp.float32
BF16 = jnp.bfloat16
VMEM = pl.BlockSpec(memory_space=pltpu.VMEM)
SMEM = pl.BlockSpec(memory_space=pltpu.SMEM)
HBM = pl.BlockSpec(memory_space=pltpu.HBM)
PARAMS = pltpu.CompilerParams(vmem_limit_bytes=40 * 1024 * 1024)


def dot(left, right):
    return jnp.dot(left, right, preferred_element_type=F32)


def dot_nt(left, right):
    return lax.dot_general(left, right, (((1,), (1,)), ((), ())), preferred_element_type=F32)


def dot_tn(left, right):
    return lax.dot_general(left, right, (((0,), (0,)), ((), ())), preferred_element_type=F32)


def halves(value):
    high = value.astype(BF16)
    return high, (value - high.astype(F32)).astype(BF16)


def iota(shape, axis):
    return lax.broadcasted_iota(jnp.int32, shape, axis)


def one_hot(condition):
    return jnp.where(condition, 1.0, 0.0).astype(BF16)


PACK_PARAMS = pltpu.CompilerParams(vmem_limit_bytes=62 * 1024 * 1024)


def basis_shift(blocks, slots):
    dof = blocks.shape[1]
    same = iota((dof, dof), 0) == iota((dof, dof), 1)
    total = sum(jnp.where(same, blocks[t], 0.0) for t in range(TYPES))
    mean = jnp.sum(jnp.sum(total, axis=1, keepdims=True), axis=0, keepdims=True) / (TYPES * dof)
    return MASS_SHIFT + 0.2 * slots * mean


def swap_blocks(piece):
    lane = iota(piece(0, 0).shape, 1)
    low = lane < META // 2
    out = []
    for tile in range(4):
        for part in range(2):
            first, second = piece(2 * part, tile // 2), piece(2 * part + 1, tile // 2)
            if tile % 2 == 0:
                second = pltpu.roll(second, META // 2, 1)
            else:
                first = pltpu.roll(first, META // 2, 1)
            out.append(jnp.where(low, first, second))
    return out


def given_to_gram():
    source, target = iota((TILE, TILE), 0), iota((TILE, TILE), 1)
    return one_hot((target // 16 == source % 16) & (target % 16 == source // 16))


def pack_kernel(devices, pos_ref, loads_hbm, rows_hbm, dens_hbm, cols_hbm, types_hbm,
                left_ref, right_ref, partner_ref, meta_ref,
                loads_ref, rows_ref, dens_ref, cols_ref, types_ref, sems):
    pairs = (
        (rows_hbm, rows_ref), (dens_hbm, dens_ref), (cols_hbm, cols_ref),
        (types_hbm, types_ref), (loads_hbm, loads_ref),
    )
    copies = [
        pltpu.make_async_copy(source, target, sems.at[number])
        for number, (source, target) in enumerate(pairs)
    ]
    for copy in copies:
        copy.start()
    for copy in copies[:4]:
        copy.wait()
    rows, width = loads_ref.shape
    slots = dens_ref.shape[0]
    cap = rows // 4
    pos = pos_ref[0, 0]
    ids = rows_ref[...]
    owner = lax.div(ids, jnp.int32(rows))
    local = (ids - owner * rows + 1).astype(F32)
    kept = owner == pos
    opposite = lax.rem(pos + devices // 2, jnp.int32(devices))
    goes = [owner == pos - 1, owner == pos + 1]
    goes.append((owner == opposite) & ~goes[0] & ~goes[1])
    flags = jnp.concatenate(
        [jnp.where(g, 1.0, 0.0) for g in goes] + [jnp.zeros((5, rows), F32)], axis=0
    )
    before = one_hot(iota((rows, rows), 0) < iota((rows, rows), 1))
    rank = dot(flags.astype(BF16), before).astype(jnp.int32)
    target = jnp.full((1, rows), -1, jnp.int32)
    for side in range(3):
        target = jnp.where(goes[side], rank[side:side + 1] + side * cap, target)
    pick = one_hot(iota((3 * cap, rows), 0) == target)

    density = dens_ref[...]
    kinds = types_ref[...]
    for kind in range(TYPES):
        meta_ref[kind * slots:(kind + 1) * slots, :] = jnp.where(kinds == kind, density, 0.0)
    meta_ref[3 * slots:4 * slots, :] = (cols_ref[...] - ids).astype(F32)
    meta_ref[4 * slots:, :] = jnp.zeros((META - 4 * slots, rows), F32)
    meta_ref[4 * slots:4 * slots + 1, :] = local
    meta_ref[4 * slots + 1:4 * slots + 2, :] = jnp.where(kept, local, 0.0)

    twice = jnp.concatenate([pick, pick], axis=1)
    meta = dot_nt(twice, jnp.concatenate(halves(meta_ref[...]), axis=1))
    copies[4].wait()
    body = dot(twice, jnp.concatenate(halves(loads_ref[...]), axis=0))
    for side, out_ref in enumerate((left_ref, right_ref, partner_ref)):
        out_ref[:, :width] = body[side * cap:(side + 1) * cap]
        out_ref[:, width:] = meta[side * cap:(side + 1) * cap]


def reorder(parts, tiles):
    count = parts[0].shape[0]
    tall = [p[:, t * TILE:(t + 1) * TILE] for t in range(tiles) for p in parts]
    moved = dot(jnp.concatenate(tall, axis=0), given_to_gram()).astype(BF16)
    return [
        jnp.concatenate(
            [moved[(2 * t + p) * count:(2 * t + p + 1) * count] for t in range(tiles)], axis=1
        )
        for p in range(2)
    ]


def prepare_kernel(slots, loads_ref, meta_ref, blocks_ref, kept_ref, kept_meta_ref, mixer_ref):
    rows, width = loads_ref.shape
    dof = blocks_ref.shape[1]
    tiles = width // TILE
    place = iota((rows, rows), 0) + 1
    own = one_hot(place == meta_ref[4 * slots + 1:4 * slots + 2, :].astype(jnp.int32))
    twice = jnp.concatenate([own, own], axis=1)
    kept_ref[...] = dot(twice, jnp.concatenate(reorder(halves(loads_ref[...]), tiles), axis=0))
    kept_meta_ref[...] = dot_nt(twice, jnp.concatenate(halves(meta_ref[...]), axis=1))

    def dof_of(lane):
        return lane // 64 * 16 + lane % 16

    fold = one_hot(dof_of(iota((TILE, dof), 0)) == iota((TILE, dof), 1))
    unfold = one_hot(dof_of(iota((dof, TILE), 1)) == iota((dof, TILE), 0))
    same_case = iota((TILE, TILE), 0) // 16 % 4 == iota((TILE, TILE), 1) // 16 % 4
    for kind in range(TYPES):
        for copies, part in zip(((0, 2), (1,)), halves(blocks_ref[kind])):
            wide = dot(dot_nt(fold, part).astype(BF16), unfold)
            wide = jnp.where(same_case, wide, 0.0).astype(BF16)
            for copy in copies:
                start = (copy * TYPES + kind) * TILE
                mixer_ref[start:start + TILE, :] = wide


def arrange_kernel(slots, kept_ref, kept_meta_ref, left_ref, right_ref, partner_ref,
                   geo_ref, field_ref, meta_ref, head_ref, tail_ref):
    rows, width = kept_ref.shape
    tiles = width // TILE
    edge = head_ref.shape[0]
    arrived = jnp.concatenate([left_ref[...], right_ref[...], partner_ref[...]], axis=0)
    count = arrived.shape[0]
    arrived_meta = arrived[:, width:]
    unit = one_hot(iota((8, META), 1) == 4 * slots)
    tags = dot_nt(unit, arrived_meta.astype(BF16))[0:1]
    other = one_hot(iota((rows, count), 0) + 1 == tags.astype(jnp.int32))
    twice = jnp.concatenate([other, other], axis=1)
    moved = reorder(halves(arrived[:, :width]), tiles)
    geo = kept_ref[...] + dot(twice, jnp.concatenate(moved, axis=0))
    meta = kept_meta_ref[...] + dot(twice, jnp.concatenate(halves(arrived_meta), axis=0))
    meta_ref[...] = meta
    head_ref[:, width:] = meta[:edge]
    tail_ref[:, width:] = meta[rows - edge:]

    def piece(tile, part):
        start = tile * TILE + part * META
        return geo[:, start:start + META]

    for number, value in enumerate(swap_blocks(piece)):
        lanes = slice(number * META, (number + 1) * META)
        head_ref[:, lanes] = value[:edge]
        tail_ref[:, lanes] = value[rows - edge:]
        inner = slice(number % 2 * META, (number % 2 + 1) * META)
        for part, half in enumerate(halves(value)):
            field_ref[part, number // 2, :, inner] = half
    for part, half in enumerate(halves(geo)):
        for tile in range(tiles):
            geo_ref[part, tile] = half[:, tile * TILE:(tile + 1) * TILE]


def stencil_rows(meta, slots, first):
    lane = iota((HALO, META), 1)
    spot = iota((HALO, TILE), 1)
    centre = iota((HALO, 1), 0) + first
    sums = [jnp.zeros((HALO, TILE), F32) for _ in range(TYPES)]
    for slot in range(slots):
        column = centre + meta[:, 3 * slots + slot:3 * slots + slot + 1].astype(jnp.int32)
        hit = spot == column
        for kind in range(TYPES):
            weight = meta[:, kind * slots + slot:kind * slots + slot + 1]
            sums[kind] += jnp.where(hit, weight, 0.0)
    out = []
    for kind in range(TYPES):
        inside = (lane >= kind * slots) & (lane < (kind + 1) * slots)
        total = jnp.sum(jnp.where(inside, meta, 0.0), axis=1, keepdims=True)
        high, low = halves(jnp.where(spot == centre, total, 0.0) - sums[kind])
        out.append(jnp.concatenate([high, high, low], axis=1))
    return out


def gathered(weights, near, fine):
    return halves(dot(weights, jnp.concatenate([near, fine, near], axis=0)))


def mixed(buckets, mixer_ref, count):
    highs = [buckets[0, kind, :count, :] for kind in range(TYPES)]
    lows = [buckets[1, kind, :count, :] for kind in range(TYPES)]
    return dot(jnp.concatenate(highs + highs + lows, axis=1), mixer_ref[...])


def interior_kernel(slots, field_ref, meta_ref, mixer_ref, blocks_ref,
                    inner_ref, weights_ref, stencil, buckets):
    tiles, rows = field_ref.shape[1:3]
    edge = ITERS * HALO
    shift = basis_shift(blocks_ref[...], slots)
    inside = rows - 2 * HALO

    def build(chunk, carry):
        first = pl.multiple_of(chunk * HALO, HALO)
        start = pl.multiple_of(chunk * HALO + HALO, HALO)
        for kind, value in enumerate(
            stencil_rows(meta_ref[pl.ds(start, HALO), :], slots, first + HALO)
        ):
            stencil[kind, pl.ds(first, HALO), :] = value
        return carry

    lax.fori_loop(0, inside // HALO, build, 0)

    def build_outer(chunk, carry):
        side = lax.div(chunk, jnp.int32(ITERS))
        first = pl.multiple_of(lax.rem(chunk, jnp.int32(ITERS)) * HALO, HALO)
        start = pl.multiple_of(first + side * (rows - edge), HALO)
        spot = jnp.where(side == 0, first + edge, first + rows - 2 * edge)
        for kind, value in enumerate(stencil_rows(meta_ref[pl.ds(start, HALO), :], slots, spot)):
            weights_ref[side, kind, pl.ds(first, HALO), :] = value
        return carry

    lax.fori_loop(0, 2 * ITERS, build_outer, 0)

    inner_ref[...] = jnp.zeros(inner_ref.shape, BF16)
    for step in range(ITERS):
        skip = HALO * step
        count = inside - 2 * skip
        begin = HALO + skip
        weights = jnp.concatenate(
            [stencil[kind, skip:inside - skip, :] for kind in range(TYPES)], axis=0
        )

        def read(part, tile, block):
            if step == 0:
                return field_ref[part, tile, block, :]
            return inner_ref[step - 1, part, tile, block, :]

        for tile in range(tiles):
            every = slice(0, rows)
            for part, half in enumerate(
                gathered(weights, read(0, tile, every), read(1, tile, every))
            ):
                for kind in range(TYPES):
                    buckets[part, kind, tile * count:(tile + 1) * count, :] = (
                        half[kind * count:(kind + 1) * count]
                    )
        applied = mixed(buckets, mixer_ref, tiles * count)
        block = slice(begin, begin + count)
        for tile in range(tiles):
            here = read(0, tile, block).astype(F32) + read(1, tile, block).astype(F32)
            value = applied[tile * count:(tile + 1) * count] + (MASS_SHIFT - shift) * here
            for part, half in enumerate(halves(value)):
                inner_ref[step, part, tile, block, :] = half


def sides_kernel(slots, before_ref, after_ref, field_ref, inner_ref, weights_ref, mixer_ref,
                 blocks_ref, geo_ref, basis_ref, moments_ref, v_refs, stencil, buckets):
    tiles, rows = field_ref.shape[1:3]
    width = tiles * TILE
    dof = blocks_ref.shape[1]
    cases = width // dof
    edge = ITERS * HALO
    span = rows + 2 * edge
    outer = edge - HALO
    count = edge
    shift = basis_shift(blocks_ref[...], slots)

    def build(chunk, carry):
        side = lax.div(chunk, jnp.int32(2))
        first = lax.rem(chunk, jnp.int32(2)) * HALO
        first = pl.multiple_of(first, HALO)
        place = pl.multiple_of(first + side * edge, HALO)
        meta = jnp.where(
            side == 0,
            before_ref[pl.ds(pl.multiple_of(first + HALO, HALO), HALO), width:],
            after_ref[pl.ds(first, HALO), width:],
        )
        spot = jnp.where(side == 0, first + HALO, first + rows - edge)
        for kind, value in enumerate(stencil_rows(meta, slots, spot)):
            stencil[side, kind, pl.ds(place, HALO), :] = value
        return carry

    lax.fori_loop(0, 4, build, 0)
    for kind in range(TYPES):
        stencil[0, kind, outer:, :] = weights_ref[0, kind]
        stencil[1, kind, :edge, :] = weights_ref[1, kind]

    for tile in range(tiles):
        lanes = slice(tile * TILE, (tile + 1) * TILE)
        for start, source in ((0, before_ref), (edge + rows, after_ref)):
            for part, half in enumerate(halves(source[:, lanes])):
                v_refs[0, part, tile, start:start + edge, :] = half
        for part in range(2):
            v_refs[0, part, tile, edge:edge + rows, :] = field_ref[part, tile]
            for step in range(1, ITERS + 1):
                begin = HALO * step
                v_refs[step, part, tile, edge + begin:edge + rows - begin, :] = (
                    inner_ref[step - 1, part, tile, begin:rows - begin, :]
                )
                if step < ITERS:
                    blank = jnp.zeros((begin, TILE), BF16)
                    v_refs[step, part, tile, :begin, :] = blank
                    v_refs[step, part, tile, span - begin:, :] = blank

    for step in range(ITERS):
        starts = (HALO * (step + 1), span - HALO * (step + 1) - count)
        for side in range(2):
            offset = HALO * step if side == 0 else outer - HALO * step
            weights = jnp.concatenate(
                [stencil[side, kind, offset:offset + count, :] for kind in range(TYPES)], axis=0
            )
            window = slice(0, TILE) if side == 0 else slice(span - TILE, span)
            for tile in range(tiles):
                row = (side * tiles + tile) * count
                for part, half in enumerate(
                    gathered(
                        weights, v_refs[step, 0, tile, window, :], v_refs[step, 1, tile, window, :]
                    )
                ):
                    for kind in range(TYPES):
                        buckets[part, kind, row:row + count, :] = (
                            half[kind * count:(kind + 1) * count]
                        )
        applied = mixed(buckets, mixer_ref, 2 * tiles * count)
        for side in range(2):
            block = slice(starts[side], starts[side] + count)
            for tile in range(tiles):
                row = (side * tiles + tile) * count
                here = (
                    v_refs[step, 0, tile, block, :].astype(F32)
                    + v_refs[step, 1, tile, block, :].astype(F32)
                )
                value = applied[row:row + count] + (MASS_SHIFT - shift) * here
                for part, half in enumerate(halves(value)):
                    v_refs[step + 1, part, tile, block, :] = half

    own = slice(edge, edge + rows)
    for step in range(1, ITERS + 1):

        def piece(tile, part):
            lanes = slice(part * META, (part + 1) * META)
            return (
                v_refs[step, 0, tile, own, lanes].astype(F32)
                + v_refs[step, 1, tile, own, lanes].astype(F32)
            )

        for number, value in enumerate(swap_blocks(piece)):
            lanes = slice(number % 2 * META, (number % 2 + 1) * META)
            for part, half in enumerate(halves(value)):
                basis_ref[step - 1, part, number // 2, :, lanes] = half

    def tall(step, part):
        if step == 0:
            return jnp.concatenate([geo_ref[part, tile] for tile in range(tiles)], axis=0)
        return jnp.concatenate([basis_ref[step - 1, part, tile] for tile in range(tiles)], axis=0)

    same_dof = iota((TILE, TILE), 0) % 16 == iota((TILE, TILE), 1) % 16
    sums = []
    for step in range(ITERS):
        high = dot_tn(
            tall(step, 0),
            jnp.concatenate([tall(step + k, part) for k in range(2) for part in range(2)], axis=1),
        )
        low = dot_tn(tall(step, 1), jnp.concatenate([tall(step + k, 0) for k in range(2)], axis=1))
        for k in range(2):
            gram = (
                high[:, 2 * k * TILE:(2 * k + 1) * TILE]
                + high[:, (2 * k + 1) * TILE:(2 * k + 2) * TILE]
                + low[:, k * TILE:(k + 1) * TILE]
            )
            gram = jnp.where(same_dof, gram, 0.0)
            sums.append(jnp.sum(gram.reshape(cases, TILE // cases, TILE), axis=1))
    rest = jnp.concatenate(sums, axis=0)
    pieces = []
    for _ in range(3):
        pieces.append(rest.astype(BF16))
        rest = rest - pieces[-1].astype(F32)
    collect = one_hot(iota((TILE, META), 0) // 16 == iota((TILE, META), 1) % 16)
    folded = dot(jnp.concatenate(pieces, axis=1), jnp.concatenate([collect] * 3, axis=0))
    group = iota((cases, META), 1) // cases
    moments = jnp.zeros((cases, META), F32)
    for number in range(2 * ITERS):
        part = folded[number * cases:(number + 1) * cases]
        moments = jnp.where(group == number, part, moments)
    for device in range(moments_ref.shape[0]):
        moments_ref[device] = moments


def finish_kernel(slots, moments_ref, blocks_ref, geo_ref, basis_ref, solution_ref, residual_ref):
    rows, width = solution_ref.shape
    dof = blocks_ref.shape[1]
    cases = width // dof
    tiles = width // TILE
    shift = basis_shift(blocks_ref[...], slots)
    moments = moments_ref[0]
    for device in range(1, moments_ref.shape[0]):
        moments = moments + moments_ref[device]
    group = iota((cases, META), 1) // cases
    system = []
    for row in range(ITERS):
        plain = moments if row == 0 else pltpu.roll(moments, META - cases * row, 1)
        ahead = pltpu.roll(moments, META - cases * (row + 1), 1)
        target = pltpu.roll(moments, cases * (ITERS - row), 1)
        system.append(jnp.where(group < ITERS, ahead + shift * plain, target))
    system = jnp.concatenate(system, axis=0)
    size = ITERS * cases
    index = iota((size, 1), 0)
    for pivot in range(size):
        column = jnp.broadcast_to(system[:, pivot:pivot + 1], (size, META))
        line = system[pivot:pivot + 1, :] / column[pivot:pivot + 1, :]
        system = jnp.where(index == pivot, line, system - column * line)

    unit = jnp.where(iota((cases, META), 1) % cases == iota((cases, META), 0), 1.0, 0.0)
    answers = []
    for row in range(ITERS):
        part = jnp.where(group == ITERS, system[row * cases:(row + 1) * cases], 0.0)
        step = cases
        while step < META:
            part = part + pltpu.roll(part, step, 1)
            step *= 2
        answers.append(part)
    left_over = [unit - shift * answers[0]]
    for row in range(1, ITERS):
        left_over.append(-(answers[row - 1] + shift * answers[row]))
    left_over.append(-answers[ITERS - 1])

    meets = iota((TILE, TILE), 0) % 16 == iota((TILE, TILE), 1) // 16

    def spread(parts):
        highs, lows = [], []
        for part in parts:
            tall = jnp.broadcast_to(part[:, None, :], (cases, TILE // cases, META))
            tall = tall.reshape(TILE, META)
            wide = jnp.concatenate([tall] * (TILE // META), axis=1)
            high, low = halves(jnp.where(meets, wide, 0.0))
            highs.append(high)
            lows.append(low)
        return jnp.concatenate(highs + highs + lows, axis=0)

    def tall(term, part):
        if term == 0:
            return jnp.concatenate([geo_ref[part, tile] for tile in range(tiles)], axis=0)
        return jnp.concatenate([basis_ref[term - 1, part, tile] for tile in range(tiles)], axis=0)

    for out_ref, matrix in ((solution_ref, spread(answers)), (residual_ref, spread(left_over))):
        terms = matrix.shape[0] // (3 * TILE)
        highs = [tall(term, 0) for term in range(terms)]
        lows = [tall(term, 1) for term in range(terms)]
        value = dot(jnp.concatenate(highs + lows + highs, axis=1), matrix)
        for tile in range(tiles):
            out_ref[:, tile * TILE:(tile + 1) * TILE] = value[tile * rows:(tile + 1) * rows]


def on_device(loads, row_ids, densities, block_cols, block_types, ref_blocks):
    rows, width = loads.shape
    slots = densities.shape[1]
    cases = width // ref_blocks.shape[1]
    cap = rows // 4
    edge = ITERS * HALO
    span = rows + 2 * edge
    tiles = width // TILE
    devices = lax.axis_size("sub")
    position = lax.axis_index("sub").astype(jnp.int32).reshape(1, 1)
    shape = jax.ShapeDtypeStruct
    up = [(i, i + 1) for i in range(devices - 1)]
    down = [(i + 1, i) for i in range(devices - 1)]
    across = [(i, (i + devices // 2) % devices) for i in range(devices)]

    block = shape((cap, width + META), F32)
    to_left, to_right, to_partner, meta = pl.pallas_call(
        functools.partial(pack_kernel, devices),
        out_shape=(block, block, block, shape((META, rows), F32)),
        in_specs=[SMEM] + [HBM] * 5,
        out_specs=(VMEM,) * 4,
        scratch_shapes=[
            pltpu.VMEM((rows, width), F32),
            pltpu.VMEM((1, rows), jnp.int32),
            pltpu.VMEM((slots, rows), F32),
            pltpu.VMEM((slots, rows), jnp.int32),
            pltpu.VMEM((slots, rows), jnp.int32),
            pltpu.SemaphoreType.DMA((5,)),
        ],
        compiler_params=PACK_PARAMS,
        name="pack",
    )(position, loads, row_ids.reshape(1, rows), densities.T, block_cols.T, block_types.T)

    from_partner = lax.ppermute(to_partner, "sub", across)
    from_left = lax.ppermute(to_right, "sub", up)
    from_right = lax.ppermute(to_left, "sub", down)

    mixer_shape = shape((3 * TYPES * TILE, TILE), BF16)
    kept, kept_meta, mixer = pl.pallas_call(
        functools.partial(prepare_kernel, slots),
        out_shape=(shape((rows, width), F32), shape((rows, META), F32), mixer_shape),
        in_specs=[VMEM] * 3,
        out_specs=(VMEM,) * 3,
        compiler_params=PARAMS,
        cost_estimate=pl.CostEstimate(
            flops=4_000_000_000, bytes_accessed=4_000_000, transcendentals=0
        ),
        name="prepare",
    )(loads, meta, ref_blocks)

    border = shape((edge, width + META), F32)
    pair = shape((2, tiles, rows, TILE), BF16)
    geo, field, geo_meta, head, tail = pl.pallas_call(
        functools.partial(arrange_kernel, slots),
        out_shape=(pair, pair, shape((rows, META), F32), border, border),
        in_specs=[VMEM] * 5,
        out_specs=(VMEM,) * 5,
        compiler_params=PARAMS,
        name="arrange",
    )(kept, kept_meta, from_left, from_right, from_partner)

    after = lax.ppermute(head, "sub", down)
    before = lax.ppermute(tail, "sub", up)

    basis_shape = shape((ITERS, 2, tiles, rows, TILE), BF16)
    inner, weights = pl.pallas_call(
        functools.partial(interior_kernel, slots),
        out_shape=(basis_shape, shape((2, TYPES, edge, 3 * TILE), BF16)),
        in_specs=[VMEM] * 4,
        out_specs=(VMEM,) * 2,
        scratch_shapes=[
            pltpu.VMEM((TYPES, rows - 2 * HALO, 3 * TILE), BF16),
            pltpu.VMEM((2, TYPES, tiles * (rows - 2 * HALO), TILE), BF16),
        ],
        compiler_params=PARAMS,
        cost_estimate=pl.CostEstimate(
            flops=10_000_000_000, bytes_accessed=8_000_000, transcendentals=0
        ),
        name="interior",
    )(field, geo_meta, mixer, ref_blocks)

    basis, moments = pl.pallas_call(
        functools.partial(sides_kernel, slots),
        out_shape=(basis_shape, shape((devices, cases, META), F32)),
        in_specs=[VMEM] * 8,
        out_specs=(VMEM,) * 2,
        scratch_shapes=[
            pltpu.VMEM((ITERS + 1, 2, tiles, span, TILE), BF16),
            pltpu.VMEM((2, TYPES, 2 * edge - HALO, 3 * TILE), BF16),
            pltpu.VMEM((2, TYPES, 2 * tiles * edge, TILE), BF16),
        ],
        compiler_params=PARAMS,
        name="sides",
    )(before, after, field, inner, weights, mixer, ref_blocks, geo)

    moments = lax.all_to_all(moments, "sub", split_axis=0, concat_axis=0, tiled=True)

    return pl.pallas_call(
        functools.partial(finish_kernel, slots),
        out_shape=(shape((rows, width), F32), shape((rows, width), F32)),
        in_specs=[VMEM] * 4,
        out_specs=(VMEM,) * 2,
        compiler_params=PARAMS,
        name="finish",
    )(moments, ref_blocks, geo, basis)


def solution(mesh):
    placed = (
        P(("groups", "sub"), None),
        P(("groups", "sub")),
        P(("groups", "sub"), None),
        P(("groups", "sub"), None),
        P(("groups", "sub"), None),
        P(),
    )
    return jax.shard_map(
        on_device,
        mesh=mesh,
        in_specs=placed,
        out_specs=(P(("groups", "sub"), None), P(("groups", "sub"), None)),
        check_vma=False,
    )
```

time: 95 us -> 80.9 us (0.85)
  waiting for transfers between devices: 18.1 us -> 11.2 us
  blocking collectives: 19.1 us -> 13.3 us
  local copies, waits for them, and re-layouts: 5.28 us -> 3.02 us
  Pallas kernels: 38.2 us -> 39.2 us
    all_to_all x1, blocking collectives: 19.1 us -> 13.3 us  [on_device(): lax.all_to_all(moments, 'sub', split_axis=0, concat_axis=0, tiled=True)]
    ppermute x1, waiting for transfers between devices: 15.7 us -> 11.2 us  [on_device(): from_partner = lax.ppermute(to_partner, 'sub', across)]
    ppermute x1, waiting for transfers between devices: 2.31 us -> 0.01 us  [on_device(): after = lax.ppermute(head, 'sub', down)]
    unnamed x14 -> x8, local copies, waits for them, and re-layouts: 5.28 us -> 3.02 us
    pallas_call x1, Pallas kernels: 0.58 us -> 2.64 us  [on_device(): pl.pallas_call(functools.partial(pack_kernel, devices), out_shape=(block,...]
    pallas_call x2 -> x4, Pallas kernels: 29.1 us -> 27.8 us  [the longest x1 13.9 us: on_device(): pl.pallas_call(functools.partial(sides_kernel, slots), out_shape=(basis_s...]
  transfers between devices with their start and end apart: 5 -> 5, of which waited for: 3 -> 1; matrix products, arithmetic and copies ran while one was open for 0% -> 0% of each run, Pallas kernels for 0% -> 16%
where the time goes in v2:
time: 80.9 us; the launch traced here: 80.6 us
  Pallas kernels  39.2 us (48%)
  blocking collectives  13.3 us (16%)
  starting transfers between devices  13.2 us (16%)
  waiting for transfers between devices  11.2 us (14%)
  local copies, waits for them, and re-layouts  3.02 us (4%)
    pallas_call x1, Pallas kernels, on_device(): pl.pallas_call(functools.partial(sides_kernel, slots), out_shape=(basis_s...  13.9 us
    all_to_all x1, blocking collectives, on_device(): lax.all_to_all(moments, 'sub', split_axis=0, concat_axis=0, tiled=True)  13.3 us
    pallas_call x1, Pallas kernels, on_device(): pl.pallas_call(functools.partial(interior_kernel, slots), out_shape=(basi...  11.3 us
    ppermute x1, waiting for transfers between devices, on_device(): from_partner = lax.ppermute(to_partner, 'sub', across)  11.2 us
    pallas_call x1, Pallas kernels, on_device(): pl.pallas_call(functools.partial(finish_kernel, slots), out_shape=(shape(...  8.72 us
    ppermute x1, starting transfers between devices, on_device(): from_partner = lax.ppermute(to_partner, 'sub', across)  6.9 us
    unnamed x8, local copies, waits for them, and re-layouts  3.02 us
    pallas_call x1, Pallas kernels, on_device(): pl.pallas_call(functools.partial(pack_kernel, devices), out_shape=(block,...  2.64 us
  transfers between devices with their start and end apart: 5, of which 1 were waited for; matrix products, arithmetic and copies ran while one was open for 0% of the time, Pallas kernels for 16%

profile of v2, /device:TPU:0, one launch (start us, length us, event | category | flops | bytes accessed | tf_op | source)
XLA Modules:
  0.0 80.6 jit_solution(8998302598907780672)
XLA Ops:
  0.6 2.6 %pack.1 = (f32[64,1152]{1,0:T(8,128)}, f32[64,1152]{1,0:T(8,128)}, f32[64,1152]{1,0:T(8,128)}, f32[128,256]{1,0:T(8,128)}) custom-call(s32[1,1]{1,0:T(1,128)} %bitcast.pos_ref, f32[256,1024]{1,0:T(8,128)} %loads_ref.1, s32[1,256]{1,0:T(1,128)} %bitcast.8, f32[12,256]{1,0:T(8,128)} %bitcast.5, s32[12,256]{1,0:T(8,128)} %bitcast.6, s32[12,256]{1,0:T(8,128)} %bitcast.7), custom_call_target="tpu_custom_call" | custom-call | tf_op jit(solution)/shard_map/pack/pallas_call | solution.py:512
  3.3 2.4 %collective-permute-start = (f32[64,1152]{1,0:T(8,128)}, f32[64,1152]{1,0:T(8,128)S(1)}, u32[]{:S(2)}, u32[]{:S(2)}) collective-permute-start(f32[64,1152]{1,0:T(8,128)} %get-tuple-element.21), channel_id=1, source_target_pairs={{0,1},{1,2},{2,3},{3,4},{4,5},{5,6},{6,7},{7,8},{8,9},{9,10},{10,1... | collective-permute-start | bytes 884744 | tf_op jit(solution)/shard_map/ppermute | solution.py:530
  5.7 1.3 %collective-permute-start.1 = (f32[64,1152]{1,0:T(8,128)}, f32[64,1152]{1,0:T(8,128)S(1)}, u32[]{:S(2)}, u32[]{:S(2)}) collective-permute-start(f32[64,1152]{1,0:T(8,128)} %get-tuple-element.22), channel_id=1, source_target_pairs={{1,0},{2,1},{3,2},{4,3},{5,4},{6,5},{7,6},{8,7},{9,8},{10,9},{11,1... | collective-permute-start | bytes 884744 | tf_op jit(solution)/shard_map/ppermute | solution.py:531
  7.0 6.9 %collective-permute-start.2 = (f32[64,1152]{1,0:T(8,128)}, f32[64,1152]{1,0:T(8,128)S(1)}, u32[]{:S(2)}, u32[]{:S(2)}) collective-permute-start(f32[64,1152]{1,0:T(8,128)} %get-tuple-element.23), channel_id=1, source_target_pairs={{0,8},{1,9},{2,10},{3,11},{4,12},{5,13},{6,14},{7,15},{8,0},{9,1},... | collective-permute-start | bytes 884744 | tf_op jit(solution)/shard_map/ppermute | solution.py:529
  13.9 0.0 copy-start
  13.9 1.2 %copy-done = f32[256,1024]{1,0:T(8,128)S(1)} copy-done((f32[256,1024]{1,0:T(8,128)S(1)}, f32[256,1024]{1,0:T(8,128)}, u32[]{:S(2)}) %copy-start) | copy-done | bytes 1048600
  15.1 0.0 copy-start.1
  15.1 0.9 %copy-done.1 = f32[3,64,64]{2,1,0:T(8,128)S(1)} copy-done((f32[3,64,64]{2,1,0:T(8,128)S(1)}, f32[3,64,64]{2,1,0:T(8,128)}, u32[]{:S(2)}) %copy-start.1) | copy-done | bytes 49176
  16.0 0.0 copy-start.3
  16.0 0.9 %copy-done.3 = f32[128,256]{1,0:T(8,128)S(1)} copy-done((f32[128,256]{1,0:T(8,128)S(1)}, f32[128,256]{1,0:T(8,128)}, u32[]{:S(2)}) %copy-start.3) | copy-done | bytes 131096
  16.9 0.0 copy-start.2
  16.9 1.7 %prepare.1 = (f32[256,1024]{1,0:T(8,128)S(1)}, f32[256,128]{1,0:T(8,128)S(1)}, bf16[2304,256]{1,0:T(8,128)(2,1)S(1)}) custom-call(f32[256,1024]{1,0:T(8,128)S(1)} %copy-done, f32[128,256]{1,0:T(8,128)S(1)} %copy-done.3, f32[3,64,64]{2,1,0:T(8,128)S(1)} %copy-done.1), custom_call_target="tpu_custom_call" | custom-call | flops 4000000000 | bytes 4000000 | tf_op jit(solution)/shard_map/prepare/pallas_call | solution.py:534
  18.6 0.0 collective-permute-done.left_ref
  18.6 0.0 collective-permute-done.1.right_ref
  18.6 11.2 %collective-permute-done.2.partner_ref = f32[64,1152]{1,0:T(8,128)S(1)} collective-permute-done((f32[64,1152]{1,0:T(8,128)}, f32[64,1152]{1,0:T(8,128)S(1)}, u32[]{:S(2)}, u32[]{:S(2)}) %collective-permute-start.2) | collective-permute-done | bytes 294944 | tf_op jit(solution)/shard_map/ppermute | solution.py:529
  29.8 0.9 %arrange.1 = (bf16[2,4,256,256]{3,2,1,0:T(8,128)(2,1)S(1)}, bf16[2,4,256,256]{3,2,1,0:T(8,128)(2,1)S(1)}, f32[256,128]{1,0:T(8,128)S(1)}, f32[96,1152]{1,0:T(8,128)S(1)}, f32[96,1152]{1,0:T(8,128)S(1)}) custom-call(f32[256,1024]{1,0:T(8,128)S(1)} %get-tuple-element.19.kept_ref, f32[256,128]{1,0:T(8,128)S(1)} %get-tuple-element.20.kept_meta_ref, ...), custom_call_target="tpu_custom_call" | custom-call | tf_op jit(solution)/shard_map/arrange/pallas_call | solution.py:548
  30.7 1.3 %collective-permute-start.3 = (f32[96,1152]{1,0:T(8,128)S(1)}, f32[96,1152]{1,0:T(8,128)S(1)}, u32[]{:S(2)}, u32[]{:S(2)}) collective-permute-start(f32[96,1152]{1,0:T(8,128)S(1)} %get-tuple-element.24), channel_id=1, source_target_pairs={{0,1},{1,2},{2,3},{3,4},{4,5},{5,6},{6,7},{7,8},{8,9},{9,10},{10,1... | collective-permute-start | bytes 1327112 | tf_op jit(solution)/shard_map/ppermute | solution.py:558
  32.1 1.3 %collective-permute-start.4 = (f32[96,1152]{1,0:T(8,128)S(1)}, f32[96,1152]{1,0:T(8,128)S(1)}, u32[]{:S(2)}, u32[]{:S(2)}) collective-permute-start(f32[96,1152]{1,0:T(8,128)S(1)} %get-tuple-element.25), channel_id=1, source_target_pairs={{1,0},{2,1},{3,2},{4,3},{5,4},{6,5},{7,6},{8,7},{9,8},{10,9},{11,1... | collective-permute-start | bytes 1327112 | tf_op jit(solution)/shard_map/ppermute | solution.py:557
  33.4 0.0 copy-done.2
  33.4 11.3 %interior.1 = (bf16[3,2,4,256,256]{4,3,2,1,0:T(8,128)(2,1)S(1)}, bf16[2,3,96,768]{3,2,1,0:T(8,128)(2,1)S(1)}) custom-call(bf16[2,4,256,256]{3,2,1,0:T(8,128)(2,1)S(1)} %get-tuple-element.26.field_ref, f32[256,128]{1,0:T(8,128)S(1)} %get-tuple-element.27.meta_ref, bf16[2304,256]{1,0:T(8,128)(2,1)S(1)} %get-tuple-element.28.mixer_ref, f32[3,64,64]{2,1,0:T(8,128)S(1)} %copy-done.2), custom_call_target="tpu_custom_call" | custom-call | flops 10000000000 | bytes 8000000 | tf_op jit(solution)/shard_map/interior/pallas_call | solution.py:561
  44.6 0.0 collective-permute-done.3.before_ref
  44.7 0.0 collective-permute-done.4.after_ref
  44.7 13.9 %sides.1 = (bf16[3,2,4,256,256]{4,3,2,1,0:T(8,128)(2,1)S(1)}, f32[16,16,128]{2,1,0:T(8,128)S(1)}) custom-call(f32[96,1152]{1,0:T(8,128)S(1)} %collective-permute-done.3.before_ref, f32[96,1152]{1,0:T(8,128)S(1)} %collective-permute-done.4.after_ref, bf16[2,4,256,256]{3,2,1,0:T(8,128)(2,1)S(1)} %get-tuple-element.26.field_ref, ...), custom_call_target="tpu_custom_call" | custom-call | tf_op jit(solution)/shard_map/sides/pallas_call | solution.py:577
  58.6 13.3 %all_to_all.5.moments_ref = f32[16,16,128]{2,1,0:T(8,128)S(1)} all-to-all(f32[16,16,128]{2,1,0:T(8,128)S(1)} %get-tuple-element.32), channel_id=1, replica_groups=mesh['groups'=2,'sub'=16] {'sub'}, dimensions={0} | all-to-all | bytes 262144 | tf_op jit(solution)/shard_map/all_to_all | solution.py:591
  71.9 8.7 %finish.1 = (f32[256,1024]{1,0:T(8,128)}, f32[256,1024]{1,0:T(8,128)}) custom-call(f32[16,16,128]{2,1,0:T(8,128)S(1)} %all_to_all.5.moments_ref, f32[3,64,64]{2,1,0:T(8,128)S(1)} %copy-done.2, bf16[2,4,256,256]{3,2,1,0:T(8,128)(2,1)S(1)} %get-tuple-element.31.geo_ref, bf16[3,2,4,256,256]{4,3,2,1,0:T(8,128)(2,1)S(1)} %get-tuple-element.33.basis_ref), custom_call_target="tpu_custom_call" | custom-call | tf_op jit(solution)/shard_map/finish/pallas_call | solution.py:593
Async XLA Ops:
  3.3 15.3 %collective-permute-start = (f32[64,1152]{1,0:T(8,128)}, f32[64,1152]{1,0:T(8,128)S(1)}, u32[]{:S(2)}, u32[]{:S(2)}) collective-permute-start(f32[64,1152]{1,0:T(8,128)} %get-tuple-element.21), channel_id=1, source_target_pairs={{0,1},{1,2},{2,3},{3,4},{4,5},{5,6},{6,7},{7,8},{8,9},{9,10},{10,1... | collective-permute-start | bytes 884744 | tf_op jit(solution)/shard_map/ppermute | solution.py:530
  5.7 12.9 %collective-permute-start.1 = (f32[64,1152]{1,0:T(8,128)}, f32[64,1152]{1,0:T(8,128)S(1)}, u32[]{:S(2)}, u32[]{:S(2)}) collective-permute-start(f32[64,1152]{1,0:T(8,128)} %get-tuple-element.22), channel_id=1, source_target_pairs={{1,0},{2,1},{3,2},{4,3},{5,4},{6,5},{7,6},{8,7},{9,8},{10,9},{11,1... | collective-permute-start | bytes 884744 | tf_op jit(solution)/shard_map/ppermute | solution.py:531
  7.0 22.8 %collective-permute-start.2 = (f32[64,1152]{1,0:T(8,128)}, f32[64,1152]{1,0:T(8,128)S(1)}, u32[]{:S(2)}, u32[]{:S(2)}) collective-permute-start(f32[64,1152]{1,0:T(8,128)} %get-tuple-element.23), channel_id=1, source_target_pairs={{0,8},{1,9},{2,10},{3,11},{4,12},{5,13},{6,14},{7,15},{8,0},{9,1},... | collective-permute-start | bytes 884744 | tf_op jit(solution)/shard_map/ppermute | solution.py:529
  13.9 1.2 %copy-start = (f32[256,1024]{1,0:T(8,128)S(1)}, f32[256,1024]{1,0:T(8,128)}, u32[]{:S(2)}) copy-start(f32[256,1024]{1,0:T(8,128)} %loads_ref.1) | copy-start | bytes 3145732
  15.1 0.9 %copy-start.1 = (f32[3,64,64]{2,1,0:T(8,128)S(1)}, f32[3,64,64]{2,1,0:T(8,128)}, u32[]{:S(2)}) copy-start(f32[3,64,64]{2,1,0:T(8,128)} %blocks_ref.7) | copy-start | bytes 147460
  16.0 0.9 %copy-start.3 = (f32[128,256]{1,0:T(8,128)S(1)}, f32[128,256]{1,0:T(8,128)}, u32[]{:S(2)}) copy-start(f32[128,256]{1,0:T(8,128)} %get-tuple-element.18.meta_ref) | copy-start | bytes 393220
  16.9 16.5 %copy-start.2 = (f32[3,64,64]{2,1,0:T(8,128)S(1)}, f32[3,64,64]{2,1,0:T(8,128)}, u32[]{:S(2)}) copy-start(f32[3,64,64]{2,1,0:T(8,128)} %blocks_ref.7) | copy-start | bytes 147460
  30.7 13.9 %collective-permute-start.3 = (f32[96,1152]{1,0:T(8,128)S(1)}, f32[96,1152]{1,0:T(8,128)S(1)}, u32[]{:S(2)}, u32[]{:S(2)}) collective-permute-start(f32[96,1152]{1,0:T(8,128)S(1)} %get-tuple-element.24), channel_id=1, source_target_pairs={{0,1},{1,2},{2,3},{3,4},{4,5},{5,6},{6,7},{7,8},{8,9},{9,10},{10,1... | collective-permute-start | bytes 1327112 | tf_op jit(solution)/shard_map/ppermute | solution.py:558
  32.1 12.6 %collective-permute-start.4 = (f32[96,1152]{1,0:T(8,128)S(1)}, f32[96,1152]{1,0:T(8,128)S(1)}, u32[]{:S(2)}, u32[]{:S(2)}) collective-permute-start(f32[96,1152]{1,0:T(8,128)S(1)} %get-tuple-element.25), channel_id=1, source_target_pairs={{1,0},{2,1},{3,2},{4,3},{5,4},{6,5},{7,6},{8,7},{9,8},{10,9},{11,1... | collective-permute-start | bytes 1327112 | tf_op jit(solution)/shard_map/ppermute | solution.py:557

commit v3 on v2

--- a/solution.py
+++ b/solution.py
@@ -78,9 +78,45 @@
     return one_hot((target // 16 == source % 16) & (target % 16 == source // 16))
 
 
-def pack_kernel(devices, pos_ref, loads_hbm, rows_hbm, dens_hbm, cols_hbm, types_hbm,
-                left_ref, right_ref, partner_ref, meta_ref,
-                loads_ref, rows_ref, dens_ref, cols_ref, types_ref, sems):
+def peers(pos, devices):
+    odd = lax.rem(pos, jnp.int32(2))
+    return (
+        pos + 1 - 2 * odd,
+        pos - 1 + 2 * odd,
+        lax.rem(pos + devices // 2, jnp.int32(devices)),
+    )
+
+
+def targets(pos, ids, rows, devices):
+    cap = rows // 4
+    owner = lax.div(ids, jnp.int32(rows))
+    goes = []
+    for peer in peers(pos, devices):
+        here = owner == peer
+        for other in goes:
+            here = here & ~other
+        goes.append(here)
+    flags = jnp.concatenate(
+        [jnp.where(g, 1.0, 0.0) for g in goes] + [jnp.zeros((5, rows), F32)], axis=0
+    )
+    before = one_hot(iota((rows, rows), 0) < iota((rows, rows), 1))
+    rank = dot(flags.astype(BF16), before).astype(jnp.int32)
+    target = jnp.full((1, rows), -1, jnp.int32)
+    for side in range(3):
+        target = jnp.where(goes[side], rank[side:side + 1] + side * cap, target)
+    return target
+
+
+def fill_block(pick, loads, meta, out_ref):
+    width = loads.shape[1]
+    twice = jnp.concatenate([pick, pick], axis=1)
+    out_ref[:, width:] = dot_nt(twice, jnp.concatenate(halves(meta), axis=1))
+    out_ref[:, :width] = dot(twice, jnp.concatenate(halves(loads), axis=0))
+
+
+def pack_far_kernel(devices, pos_ref, loads_hbm, rows_hbm, dens_hbm, cols_hbm, types_hbm,
+                    far_ref, meta_ref, target_ref,
+                    loads_ref, rows_ref, dens_ref, cols_ref, types_ref, sems):
     pairs = (
         (rows_hbm, rows_ref), (dens_hbm, dens_ref), (cols_hbm, cols_ref),
         (types_hbm, types_ref), (loads_hbm, loads_ref),
@@ -93,26 +129,15 @@
         copy.start()
     for copy in copies[:4]:
         copy.wait()
-    rows, width = loads_ref.shape
+    rows = loads_ref.shape[0]
     slots = dens_ref.shape[0]
     cap = rows // 4
     pos = pos_ref[0, 0]
     ids = rows_ref[...]
     owner = lax.div(ids, jnp.int32(rows))
     local = (ids - owner * rows + 1).astype(F32)
-    kept = owner == pos
-    opposite = lax.rem(pos + devices // 2, jnp.int32(devices))
-    goes = [owner == pos - 1, owner == pos + 1]
-    goes.append((owner == opposite) & ~goes[0] & ~goes[1])
-    flags = jnp.concatenate(
-        [jnp.where(g, 1.0, 0.0) for g in goes] + [jnp.zeros((5, rows), F32)], axis=0
-    )
-    before = one_hot(iota((rows, rows), 0) < iota((rows, rows), 1))
-    rank = dot(flags.astype(BF16), before).astype(jnp.int32)
-    target = jnp.full((1, rows), -1, jnp.int32)
-    for side in range(3):
-        target = jnp.where(goes[side], rank[side:side + 1] + side * cap, target)
-    pick = one_hot(iota((3 * cap, rows), 0) == target)
+    target = targets(pos, ids, rows, devices)
+    target_ref[...] = jnp.broadcast_to(target, target_ref.shape)
 
     density = dens_ref[...]
     kinds = types_ref[...]
@@ -121,15 +146,29 @@
     meta_ref[3 * slots:4 * slots, :] = (cols_ref[...] - ids).astype(F32)
     meta_ref[4 * slots:, :] = jnp.zeros((META - 4 * slots, rows), F32)
     meta_ref[4 * slots:4 * slots + 1, :] = local
-    meta_ref[4 * slots + 1:4 * slots + 2, :] = jnp.where(kept, local, 0.0)
-
-    twice = jnp.concatenate([pick, pick], axis=1)
-    meta = dot_nt(twice, jnp.concatenate(halves(meta_ref[...]), axis=1))
+    meta_ref[4 * slots + 1:4 * slots + 2, :] = jnp.where(owner == pos, local, 0.0)
+
     copies[4].wait()
-    body = dot(twice, jnp.concatenate(halves(loads_ref[...]), axis=0))
-    for side, out_ref in enumerate((left_ref, right_ref, partner_ref)):
-        out_ref[:, :width] = body[side * cap:(side + 1) * cap]
-        out_ref[:, width:] = meta[side * cap:(side + 1) * cap]
+    pick = one_hot(iota((cap, rows), 0) + 2 * cap == target)
+    fill_block(pick, loads_ref[...], meta_ref[...], far_ref)
+
+
+def pack_near_kernel(target_hbm, meta_hbm, loads_hbm, core_ref, chip_ref,
+                     target_ref, meta_ref, loads_ref, sems):
+    pairs = ((target_hbm, target_ref), (meta_hbm, meta_ref), (loads_hbm, loads_ref))
+    copies = [
+        pltpu.make_async_copy(source, target, sems.at[number])
+        for number, (source, target) in enumerate(pairs)
+    ]
+    for copy in copies:
+        copy.start()
+    for copy in copies:
+        copy.wait()
+    rows = loads_ref.shape[0]
+    cap = rows // 4
+    for side, out_ref in enumerate((core_ref, chip_ref)):
+        pick = one_hot(iota((cap, rows), 0) + side * cap == target_ref[0:1, :])
+        fill_block(pick, loads_ref[...], meta_ref[...], out_ref)
 
 
 def reorder(parts, tiles):
@@ -169,12 +208,13 @@
                 mixer_ref[start:start + TILE, :] = wide
 
 
-def arrange_kernel(slots, kept_ref, kept_meta_ref, left_ref, right_ref, partner_ref,
-                   geo_ref, field_ref, meta_ref, head_ref, tail_ref):
+def arrange_kernel(slots, pos_ref, kept_ref, kept_meta_ref, core_ref, chip_ref, far_ref,
+                   geo_ref, field_ref, meta_ref, to_core_ref, to_chip_ref):
     rows, width = kept_ref.shape
     tiles = width // TILE
-    edge = head_ref.shape[0]
-    arrived = jnp.concatenate([left_ref[...], right_ref[...], partner_ref[...]], axis=0)
+    edge = to_core_ref.shape[0]
+    even = lax.rem(pos_ref[0, 0], jnp.int32(2)) == 0
+    arrived = jnp.concatenate([core_ref[...], chip_ref[...], far_ref[...]], axis=0)
     count = arrived.shape[0]
     arrived_meta = arrived[:, width:]
     unit = one_hot(iota((8, META), 1) == 4 * slots)
@@ -185,8 +225,13 @@
     geo = kept_ref[...] + dot(twice, jnp.concatenate(moved, axis=0))
     meta = kept_meta_ref[...] + dot(twice, jnp.concatenate(halves(arrived_meta), axis=0))
     meta_ref[...] = meta
-    head_ref[:, width:] = meta[:edge]
-    tail_ref[:, width:] = meta[rows - edge:]
+
+    def send(lanes, value):
+        head, tail = value[:edge], value[rows - edge:]
+        to_core_ref[:, lanes] = jnp.where(even, tail, head)
+        to_chip_ref[:, lanes] = jnp.where(even, head, tail)
+
+    send(slice(width, None), meta)
 
     def piece(tile, part):
         start = tile * TILE + part * META
@@ -194,8 +239,7 @@
 
     for number, value in enumerate(swap_blocks(piece)):
         lanes = slice(number * META, (number + 1) * META)
-        head_ref[:, lanes] = value[:edge]
-        tail_ref[:, lanes] = value[rows - edge:]
+        send(lanes, value)
         inner = slice(number % 2 * META, (number % 2 + 1) * META)
         for part, half in enumerate(halves(value)):
             field_ref[part, number // 2, :, inner] = half
@@ -263,7 +307,13 @@
 
     lax.fori_loop(0, 2 * ITERS, build_outer, 0)
 
-    inner_ref[...] = jnp.zeros(inner_ref.shape, BF16)
+    for step in range(ITERS - 1):
+        begin = HALO * (step + 1)
+        blank = jnp.zeros((begin, TILE), BF16)
+        for part in range(2):
+            for tile in range(tiles):
+                inner_ref[step, part, tile, :begin, :] = blank
+                inner_ref[step, part, tile, rows - begin:, :] = blank
     for step in range(ITERS):
         skip = HALO * step
         count = inside - 2 * skip
@@ -295,96 +345,111 @@
                 inner_ref[step, part, tile, block, :] = half
 
 
-def sides_kernel(slots, before_ref, after_ref, field_ref, inner_ref, weights_ref, mixer_ref,
-                 blocks_ref, geo_ref, basis_ref, moments_ref, v_refs, stencil, buckets):
+def sides_kernel(slots, pos_ref, core_ref, chip_ref, field_ref, inner_ref, weights_ref, mixer_ref,
+                 blocks_ref, geo_ref, basis_ref, moments_ref, v_refs, meta_refs, stencil, buckets):
     tiles, rows = field_ref.shape[1:3]
     width = tiles * TILE
     dof = blocks_ref.shape[1]
     cases = width // dof
     edge = ITERS * HALO
-    span = rows + 2 * edge
     outer = edge - HALO
     count = edge
+    rest = TILE - edge
     shift = basis_shift(blocks_ref[...], slots)
+    even = lax.rem(pos_ref[0, 0], jnp.int32(2)) == 0
+
+    for tile in range(tiles + 1):
+        lanes = slice(tile * TILE, (tile + 1) * TILE) if tile < tiles else slice(width, None)
+        core, chip = core_ref[:, lanes], chip_ref[:, lanes]
+        for side, value in enumerate((jnp.where(even, chip, core), jnp.where(even, core, chip))):
+            if tile == tiles:
+                meta_refs[side] = value
+            else:
+                for part, half in enumerate(halves(value)):
+                    v_refs[0, side, part, tile] = half
 
     def build(chunk, carry):
         side = lax.div(chunk, jnp.int32(2))
-        first = lax.rem(chunk, jnp.int32(2)) * HALO
-        first = pl.multiple_of(first, HALO)
-        place = pl.multiple_of(first + side * edge, HALO)
-        meta = jnp.where(
-            side == 0,
-            before_ref[pl.ds(pl.multiple_of(first + HALO, HALO), HALO), width:],
-            after_ref[pl.ds(first, HALO), width:],
-        )
+        first = pl.multiple_of(lax.rem(chunk, jnp.int32(2)) * HALO, HALO)
+        start = pl.multiple_of(first + HALO * (1 - side), HALO)
         spot = jnp.where(side == 0, first + HALO, first + rows - edge)
-        for kind, value in enumerate(stencil_rows(meta, slots, spot)):
-            stencil[side, kind, pl.ds(place, HALO), :] = value
+        for kind, value in enumerate(
+            stencil_rows(meta_refs[side, pl.ds(start, HALO), :], slots, spot)
+        ):
+            stencil[side, kind, pl.ds(first, HALO), :] = value
         return carry
 
     lax.fori_loop(0, 4, build, 0)
-    for kind in range(TYPES):
-        stencil[0, kind, outer:, :] = weights_ref[0, kind]
-        stencil[1, kind, :edge, :] = weights_ref[1, kind]
-
-    for tile in range(tiles):
-        lanes = slice(tile * TILE, (tile + 1) * TILE)
-        for start, source in ((0, before_ref), (edge + rows, after_ref)):
-            for part, half in enumerate(halves(source[:, lanes])):
-                v_refs[0, part, tile, start:start + edge, :] = half
-        for part in range(2):
-            v_refs[0, part, tile, edge:edge + rows, :] = field_ref[part, tile]
-            for step in range(1, ITERS + 1):
-                begin = HALO * step
-                v_refs[step, part, tile, edge + begin:edge + rows - begin, :] = (
-                    inner_ref[step - 1, part, tile, begin:rows - begin, :]
-                )
-                if step < ITERS:
-                    blank = jnp.zeros((begin, TILE), BF16)
-                    v_refs[step, part, tile, :begin, :] = blank
-                    v_refs[step, part, tile, span - begin:, :] = blank
+
+    def window(step, side, part, tile):
+        near = v_refs[step, side, part, tile]
+        if step == 0:
+            if side == 0:
+                return jnp.concatenate([near, field_ref[part, tile, :rest, :]], axis=0)
+            return jnp.concatenate([field_ref[part, tile, rows - rest:, :], near], axis=0)
+        blank = jnp.zeros((HALO * step, TILE), BF16)
+        begin = HALO * step
+        if side == 0:
+            far = inner_ref[step - 1, part, tile, begin:rest, :]
+            return jnp.concatenate([blank, near, far], axis=0)
+        far = inner_ref[step - 1, part, tile, rows - rest:rows - begin, :]
+        return jnp.concatenate([far, near, blank], axis=0)
+
+    def weight_rows(step, side, kind):
+        keep = outer - HALO * step
+        if side == 0:
+            pieces = [weights_ref[0, kind, :count - keep, :]]
+            if keep:
+                pieces.insert(0, stencil[0, kind, outer - keep:, :])
+        else:
+            pieces = [weights_ref[1, kind, keep:, :]]
+            if keep:
+                pieces.append(stencil[1, kind, :keep, :])
+        return jnp.concatenate(pieces, axis=0)
 
     for step in range(ITERS):
-        starts = (HALO * (step + 1), span - HALO * (step + 1) - count)
+        centres = []
         for side in range(2):
-            offset = HALO * step if side == 0 else outer - HALO * step
             weights = jnp.concatenate(
-                [stencil[side, kind, offset:offset + count, :] for kind in range(TYPES)], axis=0
+                [weight_rows(step, side, kind) for kind in range(TYPES)], axis=0
             )
-            window = slice(0, TILE) if side == 0 else slice(span - TILE, span)
             for tile in range(tiles):
                 row = (side * tiles + tile) * count
-                for part, half in enumerate(
-                    gathered(
-                        weights, v_refs[step, 0, tile, window, :], v_refs[step, 1, tile, window, :]
-                    )
-                ):
+                near, fine = (window(step, side, part, tile) for part in range(2))
+                first = HALO * (step + 1) if side == 0 else TILE - HALO * (step + 1) - count
+                centres.append((near[first:first + count], fine[first:first + count]))
+                for part, half in enumerate(gathered(weights, near, fine)):
                     for kind in range(TYPES):
                         buckets[part, kind, row:row + count, :] = (
                             half[kind * count:(kind + 1) * count]
                         )
         applied = mixed(buckets, mixer_ref, 2 * tiles * count)
         for side in range(2):
-            block = slice(starts[side], starts[side] + count)
             for tile in range(tiles):
-                row = (side * tiles + tile) * count
-                here = (
-                    v_refs[step, 0, tile, block, :].astype(F32)
-                    + v_refs[step, 1, tile, block, :].astype(F32)
-                )
-                value = applied[row:row + count] + (MASS_SHIFT - shift) * here
+                number = side * tiles + tile
+                near, fine = centres[number]
+                here = near.astype(F32) + fine.astype(F32)
+                value = applied[number * count:(number + 1) * count] + (MASS_SHIFT - shift) * here
                 for part, half in enumerate(halves(value)):
-                    v_refs[step + 1, part, tile, block, :] = half
-
-    own = slice(edge, edge + rows)
+                    v_refs[step + 1, side, part, tile] = half
+
     for step in range(1, ITERS + 1):
+        begin = HALO * step
 
         def piece(tile, part):
             lanes = slice(part * META, (part + 1) * META)
-            return (
-                v_refs[step, 0, tile, own, lanes].astype(F32)
-                + v_refs[step, 1, tile, own, lanes].astype(F32)
+            high, low = (
+                jnp.concatenate(
+                    [
+                        v_refs[step, 0, half, tile, count - begin:, lanes],
+                        inner_ref[step - 1, half, tile, begin:rows - begin, lanes],
+                        v_refs[step, 1, half, tile, :begin, lanes],
+                    ],
+                    axis=0,
+                )
+                for half in range(2)
             )
+            return high.astype(F32) + low.astype(F32)
 
         for number, value in enumerate(swap_blocks(piece)):
             lanes = slice(number % 2 * META, (number % 2 + 1) * META)
@@ -412,11 +477,11 @@
             )
             gram = jnp.where(same_dof, gram, 0.0)
             sums.append(jnp.sum(gram.reshape(cases, TILE // cases, TILE), axis=1))
-    rest = jnp.concatenate(sums, axis=0)
+    remainder = jnp.concatenate(sums, axis=0)
     pieces = []
     for _ in range(3):
-        pieces.append(rest.astype(BF16))
-        rest = rest - pieces[-1].astype(F32)
+        pieces.append(remainder.astype(BF16))
+        remainder = remainder - pieces[-1].astype(F32)
     collect = one_hot(iota((TILE, META), 0) // 16 == iota((TILE, META), 1) % 16)
     folded = dot(jnp.concatenate(pieces, axis=1), jnp.concatenate([collect] * 3, axis=0))
     group = iota((cases, META), 1) // cases
@@ -424,8 +489,14 @@
     for number in range(2 * ITERS):
         part = folded[number * cases:(number + 1) * cases]
         moments = jnp.where(group == number, part, moments)
-    for device in range(moments_ref.shape[0]):
-        moments_ref[device] = moments
+    moments_ref[...] = moments
+
+
+def refined_reciprocal(value):
+    guess = pl.reciprocal(value, approx=True)
+    for _ in range(2):
+        guess = guess * (2.0 - value * guess)
+    return guess
 
 
 def finish_kernel(slots, moments_ref, blocks_ref, geo_ref, basis_ref, solution_ref, residual_ref):
@@ -447,10 +518,19 @@
     system = jnp.concatenate(system, axis=0)
     size = ITERS * cases
     index = iota((size, 1), 0)
-    for pivot in range(size):
-        column = jnp.broadcast_to(system[:, pivot:pivot + 1], (size, META))
-        line = system[pivot:pivot + 1, :] / column[pivot:pivot + 1, :]
-        system = jnp.where(index == pivot, line, system - column * line)
+    for pivot in range(0, size, 2):
+        column_a = jnp.broadcast_to(system[:, pivot:pivot + 1], (size, META))
+        column_b = jnp.broadcast_to(system[:, pivot + 1:pivot + 2], (size, META))
+        line_a = system[pivot:pivot + 1, :]
+        line_b = system[pivot + 1:pivot + 2, :]
+        above = column_b[pivot:pivot + 1, :]
+        inverse = refined_reciprocal(column_a[pivot:pivot + 1, :])
+        factor = column_a[pivot + 1:pivot + 2, :] * inverse
+        corner = column_b[pivot + 1:pivot + 2, :] - factor * above
+        line_b = (line_b - factor * line_a) * refined_reciprocal(corner)
+        line_a = (line_a - above * line_b) * inverse
+        update = system - column_a * line_a - column_b * line_b
+        system = jnp.where(index == pivot, line_a, jnp.where(index == pivot + 1, line_b, update))
 
     unit = jnp.where(iota((cases, META), 1) % cases == iota((cases, META), 0), 1.0, 0.0)
     answers = []
@@ -499,21 +579,21 @@
     cases = width // ref_blocks.shape[1]
     cap = rows // 4
     edge = ITERS * HALO
-    span = rows + 2 * edge
     tiles = width // TILE
     devices = lax.axis_size("sub")
     position = lax.axis_index("sub").astype(jnp.int32).reshape(1, 1)
     shape = jax.ShapeDtypeStruct
-    up = [(i, i + 1) for i in range(devices - 1)]
-    down = [(i + 1, i) for i in range(devices - 1)]
+    same_chip = [(i, i ^ 1) for i in range(devices)]
+    next_chip = [(i, i + 1) for i in range(1, devices - 1, 2)]
+    next_chip += [(i + 1, i) for i in range(1, devices - 1, 2)]
     across = [(i, (i + devices // 2) % devices) for i in range(devices)]
 
     block = shape((cap, width + META), F32)
-    to_left, to_right, to_partner, meta = pl.pallas_call(
-        functools.partial(pack_kernel, devices),
-        out_shape=(block, block, block, shape((META, rows), F32)),
+    to_far, meta, target = pl.pallas_call(
+        functools.partial(pack_far_kernel, devices),
+        out_shape=(block, shape((META, rows), F32), shape((8, rows), jnp.int32)),
         in_specs=[SMEM] + [HBM] * 5,
-        out_specs=(VMEM,) * 4,
+        out_specs=(VMEM,) * 3,
         scratch_shapes=[
             pltpu.VMEM((rows, width), F32),
             pltpu.VMEM((1, rows), jnp.int32),
@@ -523,12 +603,26 @@
             pltpu.SemaphoreType.DMA((5,)),
         ],
         compiler_params=PACK_PARAMS,
-        name="pack",
+        name="pack_far",
     )(position, loads, row_ids.reshape(1, rows), densities.T, block_cols.T, block_types.T)
-
-    from_partner = lax.ppermute(to_partner, "sub", across)
-    from_left = lax.ppermute(to_right, "sub", up)
-    from_right = lax.ppermute(to_left, "sub", down)
+    from_far = lax.ppermute(to_far, "sub", across)
+
+    to_core, to_chip = pl.pallas_call(
+        pack_near_kernel,
+        out_shape=(block, block),
+        in_specs=[HBM] * 3,
+        out_specs=(VMEM,) * 2,
+        scratch_shapes=[
+            pltpu.VMEM((8, rows), jnp.int32),
+            pltpu.VMEM((META, rows), F32),
+            pltpu.VMEM((rows, width), F32),
+            pltpu.SemaphoreType.DMA((3,)),
+        ],
+        compiler_params=PACK_PARAMS,
+        name="pack_near",
+    )(target, meta, loads)
+    from_chip = lax.ppermute(to_chip, "sub", next_chip)
+    from_core = lax.ppermute(to_core, "sub", same_chip)
 
     mixer_shape = shape((3 * TYPES * TILE, TILE), BF16)
     kept, kept_meta, mixer = pl.pallas_call(
@@ -545,17 +639,17 @@
 
     border = shape((edge, width + META), F32)
     pair = shape((2, tiles, rows, TILE), BF16)
-    geo, field, geo_meta, head, tail = pl.pallas_call(
+    geo, field, geo_meta, to_core, to_chip = pl.pallas_call(
         functools.partial(arrange_kernel, slots),
         out_shape=(pair, pair, shape((rows, META), F32), border, border),
-        in_specs=[VMEM] * 5,
+        in_specs=[SMEM] + [VMEM] * 5,
         out_specs=(VMEM,) * 5,
         compiler_params=PARAMS,
         name="arrange",
-    )(kept, kept_meta, from_left, from_right, from_partner)
-
-    after = lax.ppermute(head, "sub", down)
-    before = lax.ppermute(tail, "sub", up)
+    )(position, kept, kept_meta, from_core, from_chip, from_far)
+
+    halo_chip = lax.ppermute(to_chip, "sub", next_chip)
+    halo_core = lax.ppermute(to_core, "sub", same_chip)
 
     basis_shape = shape((ITERS, 2, tiles, rows, TILE), BF16)
     inner, weights = pl.pallas_call(
@@ -576,19 +670,20 @@
 
     basis, moments = pl.pallas_call(
         functools.partial(sides_kernel, slots),
-        out_shape=(basis_shape, shape((devices, cases, META), F32)),
-        in_specs=[VMEM] * 8,
+        out_shape=(basis_shape, shape((cases, META), F32)),
+        in_specs=[SMEM] + [VMEM] * 8,
         out_specs=(VMEM,) * 2,
         scratch_shapes=[
-            pltpu.VMEM((ITERS + 1, 2, tiles, span, TILE), BF16),
-            pltpu.VMEM((2, TYPES, 2 * edge - HALO, 3 * TILE), BF16),
+            pltpu.VMEM((ITERS + 1, 2, 2, tiles, edge, TILE), BF16),
+            pltpu.VMEM((2, edge, META), F32),
+            pltpu.VMEM((2, TYPES, edge - HALO, 3 * TILE), BF16),
             pltpu.VMEM((2, TYPES, 2 * tiles * edge, TILE), BF16),
         ],
         compiler_params=PARAMS,
         name="sides",
-    )(before, after, field, inner, weights, mixer, ref_blocks, geo)
-
-    moments = lax.all_to_all(moments, "sub", split_axis=0, concat_axis=0, tiled=True)
+    )(position, halo_core, halo_chip, field, inner, weights, mixer, ref_blocks, geo)
+
+    moments = lax.all_gather(moments, "sub")
 
     return pl.pallas_call(
         functools.partial(finish_kernel, slots),

time: 80.9 us -> 82.3 us (1.017)
  blocking collectives: 13.3 us -> 26 us
  starting transfers between devices: 13.2 us -> 5.61 us
  waiting for transfers between devices: 11.2 us -> 5.55 us
  Pallas kernels: 39.2 us -> 41 us
    all_gather x0 -> x1, blocking collectives: none -> 26 us  [on_device(): moments = lax.all_gather(moments, 'sub')]
    all_to_all x1 -> x0, blocking collectives: 13.3 us -> none  [on_device(): lax.all_to_all(moments, 'sub', split_axis=0, concat_axis=0, tiled=True)]
    ppermute x5, starting transfers between devices: 13.2 us -> 5.61 us  [the longest x1 4.1 us: on_device(): from_far = lax.ppermute(to_far, 'sub', across)]
    ppermute x5, waiting for transfers between devices: 11.2 us -> 5.55 us  [the longest x1 5.54 us: on_device(): from_far = lax.ppermute(to_far, 'sub', across)]
    pallas_call x1 -> x2, Pallas kernels: 2.64 us -> 5.06 us  [the longest x1 2.63 us: on_device(): pl.pallas_call(pack_near_kernel, out_shape=(block, block), in_specs=[HBM]...]
    pallas_call x1, Pallas kernels: 8.72 us -> 7.86 us  [on_device(): pl.pallas_call(functools.partial(finish_kernel, slots), out_shape=(shape(...]
  transfers between devices with their start and end apart: 5 -> 5, of which waited for: 1 -> 1; matrix products, arithmetic and copies ran while one was open for 0% -> 0% of each run, Pallas kernels for 16% -> 19%
where the time goes in v3:
time: 82.3 us; the launch traced here: 82 us
  Pallas kernels  41 us (50%)
  blocking collectives  26 us (32%)
  starting transfers between devices  5.61 us (7%)
  waiting for transfers between devices  5.55 us (7%)
  local copies, waits for them, and re-layouts  3.02 us (4%)
    all_gather x1, blocking collectives, on_device(): moments = lax.all_gather(moments, 'sub')  26 us
    pallas_call x1, Pallas kernels, on_device(): pl.pallas_call(functools.partial(sides_kernel, slots), out_shape=(basis_s...  14.1 us
    pallas_call x1, Pallas kernels, on_device(): pl.pallas_call(functools.partial(interior_kernel, slots), out_shape=(basi...  11.3 us
    pallas_call x1, Pallas kernels, on_device(): pl.pallas_call(functools.partial(finish_kernel, slots), out_shape=(shape(...  7.86 us
    ppermute x1, waiting for transfers between devices, on_device(): from_far = lax.ppermute(to_far, 'sub', across)  5.54 us
    ppermute x1, starting transfers between devices, on_device(): from_far = lax.ppermute(to_far, 'sub', across)  4.1 us
    unnamed x8, local copies, waits for them, and re-layouts  3.02 us
    pallas_call x1, Pallas kernels, on_device(): pl.pallas_call(pack_near_kernel, out_shape=(block, block), in_specs=[HBM]...  2.63 us
  transfers between devices with their start and end apart: 5, of which 1 were waited for; matrix products, arithmetic and copies ran while one was open for 0% of the time, Pallas kernels for 19%

profile of v3, /device:TPU:0, one launch (start us, length us, event | category | flops | bytes accessed | tf_op | source)
XLA Modules:
  0.0 82.0 jit_solution(15291247136126371068)
XLA Ops:
  0.6 2.4 %pack_far.1 = (f32[64,1152]{1,0:T(8,128)}, f32[128,256]{1,0:T(8,128)}, s32[8,256]{1,0:T(8,128)}) custom-call(s32[1,1]{1,0:T(1,128)} %bitcast.pos_ref, f32[256,1024]{1,0:T(8,128)} %loads_hbm.3, s32[1,256]{1,0:T(1,128)} %bitcast.10, f32[12,256]{1,0:T(8,128)} %bitcast.7, s32[12,256]{1,0:T(8,128)} %bitcast.8, s32[12,256]{1,0:T(8,128)} %bitcast.9), custom_call_target="tpu_custom_call" | custom-call | tf_op jit(solution)/shard_map/pack_far/pallas_call | solution.py:592
  3.1 4.1 %collective-permute-start.2 = (f32[64,1152]{1,0:T(8,128)}, f32[64,1152]{1,0:T(8,128)S(1)}, u32[]{:S(2)}, u32[]{:S(2)}) collective-permute-start(f32[64,1152]{1,0:T(8,128)} %get-tuple-element.25), channel_id=1, source_target_pairs={{0,8},{1,9},{2,10},{3,11},{4,12},{5,13},{6,14},{7,15},{8,0},{9,1},... | collective-permute-start | bytes 884744 | tf_op jit(solution)/shard_map/ppermute | solution.py:608
  7.2 2.6 %pack_near.1 = (f32[64,1152]{1,0:T(8,128)}, f32[64,1152]{1,0:T(8,128)}) custom-call(s32[8,256]{1,0:T(8,128)} %get-tuple-element.22.target_hbm, f32[128,256]{1,0:T(8,128)} %get-tuple-element.19.meta_ref.meta_hbm, f32[256,1024]{1,0:T(8,128)} %loads_hbm.3), custom_call_target="tpu_custom_call" | custom-call | tf_op jit(solution)/shard_map/pack_near/pallas_call | solution.py:610
  9.8 0.1 collective-permute-start
  9.9 0.7 collective-permute-start.1
  10.6 0.0 copy-start
  10.6 1.2 %copy-done = f32[256,1024]{1,0:T(8,128)S(1)} copy-done((f32[256,1024]{1,0:T(8,128)S(1)}, f32[256,1024]{1,0:T(8,128)}, u32[]{:S(2)}) %copy-start) | copy-done | bytes 1048600
  11.8 0.0 copy-start.1
  11.8 0.9 %copy-done.1 = f32[3,64,64]{2,1,0:T(8,128)S(1)} copy-done((f32[3,64,64]{2,1,0:T(8,128)S(1)}, f32[3,64,64]{2,1,0:T(8,128)}, u32[]{:S(2)}) %copy-start.1) | copy-done | bytes 49176
  12.7 0.0 copy-start.3
  12.7 0.9 %copy-done.3 = f32[128,256]{1,0:T(8,128)S(1)} copy-done((f32[128,256]{1,0:T(8,128)S(1)}, f32[128,256]{1,0:T(8,128)}, u32[]{:S(2)}) %copy-start.3) | copy-done | bytes 131096
  13.6 0.0 copy-start.2
  13.6 1.7 %prepare.1 = (f32[256,1024]{1,0:T(8,128)S(1)}, f32[256,128]{1,0:T(8,128)S(1)}, bf16[2304,256]{1,0:T(8,128)(2,1)S(1)}) custom-call(f32[256,1024]{1,0:T(8,128)S(1)} %copy-done, f32[128,256]{1,0:T(8,128)S(1)} %copy-done.3, f32[3,64,64]{2,1,0:T(8,128)S(1)} %copy-done.1), custom_call_target="tpu_custom_call" | custom-call | flops 4000000000 | bytes 4000000 | tf_op jit(solution)/shard_map/prepare/pallas_call | solution.py:628
  15.3 5.5 %collective-permute-done.2.far_ref = f32[64,1152]{1,0:T(8,128)S(1)} collective-permute-done((f32[64,1152]{1,0:T(8,128)}, f32[64,1152]{1,0:T(8,128)S(1)}, u32[]{:S(2)}, u32[]{:S(2)}) %collective-permute-start.2) | collective-permute-done | bytes 294944 | tf_op jit(solution)/shard_map/ppermute | solution.py:608
  20.8 0.0 collective-permute-done.core_ref
  20.8 0.0 collective-permute-done.1.chip_ref
  20.8 1.0 %arrange.1 = (bf16[2,4,256,256]{3,2,1,0:T(8,128)(2,1)S(1)}, bf16[2,4,256,256]{3,2,1,0:T(8,128)(2,1)S(1)}, f32[256,128]{1,0:T(8,128)S(1)}, f32[96,1152]{1,0:T(8,128)S(1)}, f32[96,1152]{1,0:T(8,128)S(1)}) custom-call(s32[1,1]{1,0:T(1,128)} %bitcast.pos_ref, f32[256,1024]{1,0:T(8,128)S(1)} %get-tuple-element.20.kept_ref, ...), custom_call_target="tpu_custom_call" | custom-call | tf_op jit(solution)/shard_map/arrange/pallas_call | solution.py:642
  21.8 0.1 collective-permute-start.3
  21.9 0.7 collective-permute-start.4
  22.6 0.0 copy-done.2
  22.6 11.3 %interior.1 = (bf16[3,2,4,256,256]{4,3,2,1,0:T(8,128)(2,1)S(1)}, bf16[2,3,96,768]{3,2,1,0:T(8,128)(2,1)S(1)}) custom-call(bf16[2,4,256,256]{3,2,1,0:T(8,128)(2,1)S(1)} %get-tuple-element.28.field_ref, f32[256,128]{1,0:T(8,128)S(1)} %get-tuple-element.29.meta_ref, bf16[2304,256]{1,0:T(8,128)(2,1)S(1)} %get-tuple-element.30.mixer_ref, f32[3,64,64]{2,1,0:T(8,128)S(1)} %copy-done.2), custom_call_target="tpu_custom_call" | custom-call | flops 10000000000 | bytes 8000000 | tf_op jit(solution)/shard_map/interior/pallas_call | solution.py:655
  33.9 0.0 collective-permute-done.3.core_ref
  33.9 0.0 collective-permute-done.4.chip_ref
  33.9 14.1 %sides.1 = (bf16[3,2,4,256,256]{4,3,2,1,0:T(8,128)(2,1)S(1)}, f32[16,128]{1,0:T(8,128)S(1)}) custom-call(s32[1,1]{1,0:T(1,128)} %bitcast.pos_ref, f32[96,1152]{1,0:T(8,128)S(1)} %collective-permute-done.3.core_ref, f32[96,1152]{1,0:T(8,128)S(1)} %collective-permute-done.4.chip_ref, bf16[2,4,256,256]{3,2,1,0:T(8,128)(2,1)S(1)} %get-tuple-element.28.field_ref, ...), custom_call_target="tpu_custom_call" | custom-call | tf_op jit(solution)/shard_map/sides/pallas_call | solution.py:671
  48.1 26.0 %all-gather = f32[256,128]{1,0:T(8,128)S(1)} all-gather(f32[16,128]{1,0:T(8,128)S(1)} %get-tuple-element.34), channel_id=2, replica_groups=mesh['groups'=2,'sub'=16] {'sub'}, dimensions={0}, use_global_device_ids=true | all-gather | bytes 139264 | tf_op jit(solution)/shard_map/all_gather | solution.py:686
  74.1 7.9 %finish.1 = (f32[256,1024]{1,0:T(8,128)}, f32[256,1024]{1,0:T(8,128)}) custom-call(f32[16,16,128]{2,1,0:T(8,128)S(1)} %bitcast.6, f32[3,64,64]{2,1,0:T(8,128)S(1)} %copy-done.2, bf16[2,4,256,256]{3,2,1,0:T(8,128)(2,1)S(1)} %get-tuple-element.33.geo_ref, bf16[3,2,4,256,256]{4,3,2,1,0:T(8,128)(2,1)S(1)} %get-tuple-element.35.basis_ref), custom_call_target="tpu_custom_call" | custom-call | tf_op jit(solution)/shard_map/finish/pallas_call | solution.py:688
Async XLA Ops:
  3.1 17.7 %collective-permute-start.2 = (f32[64,1152]{1,0:T(8,128)}, f32[64,1152]{1,0:T(8,128)S(1)}, u32[]{:S(2)}, u32[]{:S(2)}) collective-permute-start(f32[64,1152]{1,0:T(8,128)} %get-tuple-element.25), channel_id=1, source_target_pairs={{0,8},{1,9},{2,10},{3,11},{4,12},{5,13},{6,14},{7,15},{8,0},{9,1},... | collective-permute-start | bytes 884744 | tf_op jit(solution)/shard_map/ppermute | solution.py:608
  9.8 11.0 %collective-permute-start = (f32[64,1152]{1,0:T(8,128)}, f32[64,1152]{1,0:T(8,128)S(1)}, u32[]{:S(2)}, u32[]{:S(2)}) collective-permute-start(f32[64,1152]{1,0:T(8,128)} %get-tuple-element.23), channel_id=1, source_target_pairs={{0,1},{1,0},{2,3},{3,2},{4,5},{5,4},{6,7},{7,6},{8,9},{9,8},{10,11... | collective-permute-start | bytes 884744 | tf_op jit(solution)/shard_map/ppermute | solution.py:625
  9.9 10.9 %collective-permute-start.1 = (f32[64,1152]{1,0:T(8,128)}, f32[64,1152]{1,0:T(8,128)S(1)}, u32[]{:S(2)}, u32[]{:S(2)}) collective-permute-start(f32[64,1152]{1,0:T(8,128)} %get-tuple-element.24), channel_id=1, source_target_pairs={{1,2},{3,4},{5,6},{7,8},{9,10},{11,12},{13,14},{2,1},{4,3},{6,5},{... | collective-permute-start | bytes 884744 | tf_op jit(solution)/shard_map/ppermute | solution.py:624
  10.6 1.2 %copy-start = (f32[256,1024]{1,0:T(8,128)S(1)}, f32[256,1024]{1,0:T(8,128)}, u32[]{:S(2)}) copy-start(f32[256,1024]{1,0:T(8,128)} %loads_hbm.3) | copy-start | bytes 3145732
  11.8 0.9 %copy-start.1 = (f32[3,64,64]{2,1,0:T(8,128)S(1)}, f32[3,64,64]{2,1,0:T(8,128)}, u32[]{:S(2)}) copy-start(f32[3,64,64]{2,1,0:T(8,128)} %blocks_ref.7) | copy-start | bytes 147460
  12.7 0.9 %copy-start.3 = (f32[128,256]{1,0:T(8,128)S(1)}, f32[128,256]{1,0:T(8,128)}, u32[]{:S(2)}) copy-start(f32[128,256]{1,0:T(8,128)} %get-tuple-element.19.meta_ref.meta_hbm) | copy-start | bytes 393220
  13.6 9.0 %copy-start.2 = (f32[3,64,64]{2,1,0:T(8,128)S(1)}, f32[3,64,64]{2,1,0:T(8,128)}, u32[]{:S(2)}) copy-start(f32[3,64,64]{2,1,0:T(8,128)} %blocks_ref.7) | copy-start | bytes 147460
  21.8 12.1 %collective-permute-start.3 = (f32[96,1152]{1,0:T(8,128)S(1)}, f32[96,1152]{1,0:T(8,128)S(1)}, u32[]{:S(2)}, u32[]{:S(2)}) collective-permute-start(f32[96,1152]{1,0:T(8,128)S(1)} %get-tuple-element.26), channel_id=1, source_target_pairs={{0,1},{1,0},{2,3},{3,2},{4,5},{5,4},{6,7},{7,6},{8,9},{9,8},{10,11... | collective-permute-start | bytes 1327112 | tf_op jit(solution)/shard_map/ppermute | solution.py:652
  21.9 12.0 %collective-permute-start.4 = (f32[96,1152]{1,0:T(8,128)S(1)}, f32[96,1152]{1,0:T(8,128)S(1)}, u32[]{:S(2)}, u32[]{:S(2)}) collective-permute-start(f32[96,1152]{1,0:T(8,128)S(1)} %get-tuple-element.27), channel_id=1, source_target_pairs={{1,2},{3,4},{5,6},{7,8},{9,10},{11,12},{13,14},{2,1},{4,3},{6,5},{... | collective-permute-start | bytes 1327112 | tf_op jit(solution)/shard_map/ppermute | solution.py:651

commit v4 on v3

--- a/solution.py
+++ b/solution.py
@@ -109,9 +109,23 @@
 
 def fill_block(pick, loads, meta, out_ref):
     width = loads.shape[1]
+    cap = pick.shape[0]
     twice = jnp.concatenate([pick, pick], axis=1)
-    out_ref[:, width:] = dot_nt(twice, jnp.concatenate(halves(meta), axis=1))
-    out_ref[:, :width] = dot(twice, jnp.concatenate(halves(loads), axis=0))
+    notes = dot_nt(twice, jnp.concatenate(halves(meta), axis=1))
+    body = dot(twice, jnp.concatenate(halves(loads), axis=0))
+    parts = width // META
+    for part in range(parts):
+        out_ref[part * cap:(part + 1) * cap, :] = body[:, part * META:(part + 1) * META]
+    out_ref[parts * cap:, :] = notes[:cap // 2] + pltpu.roll(notes[cap // 2:], META // 2, 1)
+
+
+def read_block(ref, width):
+    parts = width // META
+    cap = ref.shape[0] * 2 // (2 * parts + 1)
+    body = jnp.concatenate([ref[part * cap:(part + 1) * cap, :] for part in range(parts)], axis=1)
+    notes = ref[parts * cap:, :]
+    notes = jnp.concatenate([notes, pltpu.roll(notes, META // 2, 1)], axis=0)
+    return body, jnp.where(iota(notes.shape, 1) < META // 2, notes, 0.0)
 
 
 def pack_far_kernel(devices, pos_ref, loads_hbm, rows_hbm, dens_hbm, cols_hbm, types_hbm,
@@ -183,14 +197,30 @@
     ]
 
 
-def prepare_kernel(slots, loads_ref, meta_ref, blocks_ref, kept_ref, kept_meta_ref, mixer_ref):
+def stacked_tiles(value, tiles):
+    return jnp.concatenate([value[:, t * TILE:(t + 1) * TILE] for t in range(tiles)], axis=0)
+
+
+def folded_rows(gram, cases):
+    same_dof = iota((TILE, TILE), 0) % 16 == iota((TILE, TILE), 1) % 16
+    gram = jnp.where(same_dof, gram, 0.0)
+    return jnp.sum(gram.reshape(cases, TILE // cases, TILE), axis=1)
+
+
+def prepare_kernel(slots, loads_ref, meta_ref, blocks_ref,
+                   kept_ref, kept_meta_ref, mixer_ref, first_ref):
     rows, width = loads_ref.shape
     dof = blocks_ref.shape[1]
     tiles = width // TILE
     place = iota((rows, rows), 0) + 1
     own = one_hot(place == meta_ref[4 * slots + 1:4 * slots + 2, :].astype(jnp.int32))
     twice = jnp.concatenate([own, own], axis=1)
-    kept_ref[...] = dot(twice, jnp.concatenate(reorder(halves(loads_ref[...]), tiles), axis=0))
+    moved = reorder(halves(loads_ref[...]), tiles)
+    kept_ref[...] = dot(twice, jnp.concatenate(moved, axis=0))
+    high, low = (stacked_tiles(part, tiles) for part in moved)
+    gram = dot_tn(high, jnp.concatenate([high, low], axis=1))
+    cross = gram[:, TILE:]
+    first_ref[...] = folded_rows(gram[:, :TILE] + cross + cross.T, width // dof)
     kept_meta_ref[...] = dot_nt(twice, jnp.concatenate(halves(meta_ref[...]), axis=1))
 
     def dof_of(lane):
@@ -214,14 +244,15 @@
     tiles = width // TILE
     edge = to_core_ref.shape[0]
     even = lax.rem(pos_ref[0, 0], jnp.int32(2)) == 0
-    arrived = jnp.concatenate([core_ref[...], chip_ref[...], far_ref[...]], axis=0)
+    blocks = [read_block(ref, width) for ref in (core_ref, chip_ref, far_ref)]
+    arrived = jnp.concatenate([block[0] for block in blocks], axis=0)
+    arrived_meta = jnp.concatenate([block[1] for block in blocks], axis=0)
     count = arrived.shape[0]
-    arrived_meta = arrived[:, width:]
     unit = one_hot(iota((8, META), 1) == 4 * slots)
     tags = dot_nt(unit, arrived_meta.astype(BF16))[0:1]
     other = one_hot(iota((rows, count), 0) + 1 == tags.astype(jnp.int32))
     twice = jnp.concatenate([other, other], axis=1)
-    moved = reorder(halves(arrived[:, :width]), tiles)
+    moved = reorder(halves(arrived), tiles)
     geo = kept_ref[...] + dot(twice, jnp.concatenate(moved, axis=0))
     meta = kept_meta_ref[...] + dot(twice, jnp.concatenate(halves(arrived_meta), axis=0))
     meta_ref[...] = meta
@@ -346,7 +377,7 @@
 
 
 def sides_kernel(slots, pos_ref, core_ref, chip_ref, field_ref, inner_ref, weights_ref, mixer_ref,
-                 blocks_ref, geo_ref, basis_ref, moments_ref, v_refs, meta_refs, stencil, buckets):
+                 blocks_ref, geo_ref, first_ref, basis_ref, moments_ref, v_refs, meta_refs, stencil, buckets):
     tiles, rows = field_ref.shape[1:3]
     width = tiles * TILE
     dof = blocks_ref.shape[1]
@@ -461,22 +492,17 @@
             return jnp.concatenate([geo_ref[part, tile] for tile in range(tiles)], axis=0)
         return jnp.concatenate([basis_ref[step - 1, part, tile] for tile in range(tiles)], axis=0)
 
-    same_dof = iota((TILE, TILE), 0) % 16 == iota((TILE, TILE), 1) % 16
-    sums = []
+    sums = [first_ref[...]]
     for step in range(ITERS):
-        high = dot_tn(
-            tall(step, 0),
-            jnp.concatenate([tall(step + k, part) for k in range(2) for part in range(2)], axis=1),
-        )
-        low = dot_tn(tall(step, 1), jnp.concatenate([tall(step + k, 0) for k in range(2)], axis=1))
-        for k in range(2):
-            gram = (
-                high[:, 2 * k * TILE:(2 * k + 1) * TILE]
-                + high[:, (2 * k + 1) * TILE:(2 * k + 2) * TILE]
-                + low[:, k * TILE:(k + 1) * TILE]
-            )
-            gram = jnp.where(same_dof, gram, 0.0)
-            sums.append(jnp.sum(gram.reshape(cases, TILE // cases, TILE), axis=1))
+        others = [tall(step + 1, 0), tall(step + 1, 1)]
+        if step > 0:
+            others += [tall(step, 0), tall(step, 1)]
+        high = dot_tn(tall(step, 0), jnp.concatenate(others, axis=1))
+        if step > 0:
+            cross = high[:, 3 * TILE:]
+            sums.append(folded_rows(high[:, 2 * TILE:3 * TILE] + cross + cross.T, cases))
+        low = dot_tn(tall(step, 1), tall(step + 1, 0))
+        sums.append(folded_rows(high[:, :TILE] + high[:, TILE:2 * TILE] + low, cases))
     remainder = jnp.concatenate(sums, axis=0)
     pieces = []
     for _ in range(3):
@@ -499,15 +525,17 @@
     return guess
 
 
-def finish_kernel(slots, moments_ref, blocks_ref, geo_ref, basis_ref, solution_ref, residual_ref):
-    rows, width = solution_ref.shape
+def finish_kernel(slots, blocks_ref, geo_ref, basis_ref, *refs):
+    moment_refs = refs[:-4]
+    solution_hbm, residual_hbm, out_refs, sems = refs[-4:]
+    rows, width = out_refs.shape[1:]
     dof = blocks_ref.shape[1]
     cases = width // dof
     tiles = width // TILE
     shift = basis_shift(blocks_ref[...], slots)
-    moments = moments_ref[0]
-    for device in range(1, moments_ref.shape[0]):
-        moments = moments + moments_ref[device]
+    moments = moment_refs[0][...]
+    for ref in moment_refs[1:]:
+        moments = moments + ref[...]
     group = iota((cases, META), 1) // cases
     system = []
     for row in range(ITERS):
@@ -564,13 +592,22 @@
             return jnp.concatenate([geo_ref[part, tile] for tile in range(tiles)], axis=0)
         return jnp.concatenate([basis_ref[term - 1, part, tile] for tile in range(tiles)], axis=0)
 
-    for out_ref, matrix in ((solution_ref, spread(answers)), (residual_ref, spread(left_over))):
+    copies = []
+    for number, (out_hbm, parts) in enumerate(
+        ((solution_hbm, answers), (residual_hbm, left_over))
+    ):
+        matrix = spread(parts)
         terms = matrix.shape[0] // (3 * TILE)
         highs = [tall(term, 0) for term in range(terms)]
         lows = [tall(term, 1) for term in range(terms)]
         value = dot(jnp.concatenate(highs + lows + highs, axis=1), matrix)
         for tile in range(tiles):
-            out_ref[:, tile * TILE:(tile + 1) * TILE] = value[tile * rows:(tile + 1) * rows]
+            lanes = slice(tile * TILE, (tile + 1) * TILE)
+            out_refs[number, :, lanes] = value[tile * rows:(tile + 1) * rows]
+        copies.append(pltpu.make_async_copy(out_refs.at[number], out_hbm, sems.at[number]))
+        copies[number].start()
+    for copy in copies:
+        copy.wait()
 
 
 def on_device(loads, row_ids, densities, block_cols, block_types, ref_blocks):
@@ -588,7 +625,7 @@
     next_chip += [(i + 1, i) for i in range(1, devices - 1, 2)]
     across = [(i, (i + devices // 2) % devices) for i in range(devices)]
 
-    block = shape((cap, width + META), F32)
+    block = shape((cap * width // META + cap // 2, META), F32)
     to_far, meta, target = pl.pallas_call(
         functools.partial(pack_far_kernel, devices),
         out_shape=(block, shape((META, rows), F32), shape((8, rows), jnp.int32)),
@@ -625,11 +662,16 @@
     from_core = lax.ppermute(to_core, "sub", same_chip)
 
     mixer_shape = shape((3 * TYPES * TILE, TILE), BF16)
-    kept, kept_meta, mixer = pl.pallas_call(
+    kept, kept_meta, mixer, first = pl.pallas_call(
         functools.partial(prepare_kernel, slots),
-        out_shape=(shape((rows, width), F32), shape((rows, META), F32), mixer_shape),
+        out_shape=(
+            shape((rows, width), F32),
+            shape((rows, META), F32),
+            mixer_shape,
+            shape((cases, TILE), F32),
+        ),
         in_specs=[VMEM] * 3,
-        out_specs=(VMEM,) * 3,
+        out_specs=(VMEM,) * 4,
         compiler_params=PARAMS,
         cost_estimate=pl.CostEstimate(
             flops=4_000_000_000, bytes_accessed=4_000_000, transcendentals=0
@@ -671,7 +713,7 @@
     basis, moments = pl.pallas_call(
         functools.partial(sides_kernel, slots),
         out_shape=(basis_shape, shape((cases, META), F32)),
-        in_specs=[SMEM] + [VMEM] * 8,
+        in_specs=[SMEM] + [VMEM] * 9,
         out_specs=(VMEM,) * 2,
         scratch_shapes=[
             pltpu.VMEM((ITERS + 1, 2, 2, tiles, edge, TILE), BF16),
@@ -681,18 +723,26 @@
         ],
         compiler_params=PARAMS,
         name="sides",
-    )(position, halo_core, halo_chip, field, inner, weights, mixer, ref_blocks, geo)
-
-    moments = lax.all_gather(moments, "sub")
+    )(position, halo_core, halo_chip, field, inner, weights, mixer, ref_blocks, geo, first)
+
+    bits = devices.bit_length() - 1
+    gathered_moments = [moments]
+    for low, high in ((0, bits // 2), (bits // 2, bits)):
+        partial = sum(gathered_moments[1:], gathered_moments[0])
+        gathered_moments = [partial]
+        for mask in range(1, 1 << (high - low)):
+            swap = [(i, i ^ (mask << low)) for i in range(devices)]
+            gathered_moments.append(lax.ppermute(partial, "sub", swap))
 
     return pl.pallas_call(
         functools.partial(finish_kernel, slots),
         out_shape=(shape((rows, width), F32), shape((rows, width), F32)),
-        in_specs=[VMEM] * 4,
-        out_specs=(VMEM,) * 2,
+        in_specs=[VMEM] * (3 + len(gathered_moments)),
+        out_specs=(HBM,) * 2,
+        scratch_shapes=[pltpu.VMEM((2, rows, width), F32), pltpu.SemaphoreType.DMA((2,))],
         compiler_params=PARAMS,
         name="finish",
-    )(moments, ref_blocks, geo, basis)
+    )(ref_blocks, geo, basis, *gathered_moments)
 
 
 def solution(mesh):

time: 82.3 us -> 73.5 us (0.89)
  blocking collectives: 26 us -> 0 us
  starting transfers between devices: 5.61 us -> 18.5 us
  waiting for transfers between devices: 5.55 us -> 10.1 us
    all_gather x1 -> x0, blocking collectives: 26 us -> none  [on_device(): moments = lax.all_gather(moments, 'sub')]
    ppermute x0 -> x6, starting transfers between devices: none -> 12.9 us  [on_device(): gathered_moments.append(lax.ppermute(partial, 'sub', swap))]
    ppermute x0 -> x6, waiting for transfers between devices: none -> 5.46 us  [on_device(): gathered_moments.append(lax.ppermute(partial, 'sub', swap))]
    ppermute x1, waiting for transfers between devices: 5.54 us -> 4.59 us  [on_device(): from_far = lax.ppermute(to_far, 'sub', across)]
  transfers between devices with their start and end apart: 5 -> 11, of which waited for: 1 -> 4; matrix products, arithmetic and copies ran while one was open for 0% -> 0% of each run, Pallas kernels for 19% -> 22%
where the time goes in v4:
time: 73.5 us; the launch traced here: 73.2 us
  Pallas kernels  40.7 us (55%)
  starting transfers between devices  18.5 us (25%)
  waiting for transfers between devices  10.1 us (14%)
  local copies, waits for them, and re-layouts  3.02 us (4%)
  between operations  0.92 us (1%)
    pallas_call x1, Pallas kernels, on_device(): pl.pallas_call(functools.partial(sides_kernel, slots), out_shape=(basis_s...  13.7 us
    ppermute x6, starting transfers between devices, on_device(): gathered_moments.append(lax.ppermute(partial, 'sub', swap))  12.9 us
    pallas_call x1, Pallas kernels, on_device(): pl.pallas_call(functools.partial(interior_kernel, slots), out_shape=(basi...  11.3 us
    pallas_call x1, Pallas kernels, on_device(): pl.pallas_call(functools.partial(finish_kernel, slots), out_shape=(shape(...  7.66 us
    ppermute x6, waiting for transfers between devices, on_device(): gathered_moments.append(lax.ppermute(partial, 'sub', swap))  5.46 us
    ppermute x1, waiting for transfers between devices, on_device(): from_far = lax.ppermute(to_far, 'sub', across)  4.59 us
    ppermute x1, starting transfers between devices, on_device(): from_far = lax.ppermute(to_far, 'sub', across)  4.1 us
    unnamed x8, local copies, waits for them, and re-layouts  3.02 us
  transfers between devices with their start and end apart: 11, of which 4 were waited for; matrix products, arithmetic and copies ran while one was open for 0% of the time, Pallas kernels for 22%

profile of v4, /device:TPU:0, one launch (start us, length us, event | category | flops | bytes accessed | tf_op | source)
XLA Modules:
  0.0 73.2 jit_solution(8150290393294242893)
XLA Ops:
  0.6 2.4 %pack_far.1 = (f32[544,128]{1,0:T(8,128)}, f32[128,256]{1,0:T(8,128)}, s32[8,256]{1,0:T(8,128)}) custom-call(s32[1,1]{1,0:T(1,128)} %bitcast.pos_ref, f32[256,1024]{1,0:T(8,128)} %loads_hbm.3, s32[1,256]{1,0:T(1,128)} %bitcast.8, f32[12,256]{1,0:T(8,128)} %bitcast.5, s32[12,256]{1,0:T(8,128)} %bitcast.6, s32[12,256]{1,0:T(8,128)} %bitcast.7), custom_call_target="tpu_custom_call" | custom-call | tf_op jit(solution)/shard_map/pack_far/pallas_call | solution.py:629
  3.1 4.1 %collective-permute-start.2 = (f32[544,128]{1,0:T(8,128)}, f32[544,128]{1,0:T(8,128)S(1)}, u32[]{:S(2)}, u32[]{:S(2)}) collective-permute-start(f32[544,128]{1,0:T(8,128)} %get-tuple-element.26), channel_id=1, source_target_pairs={{0,8},{1,9},{2,10},{3,11},{4,12},{5,13},{6,14},{7,15},{8,0},{9,1},... | collective-permute-start | bytes 835592 | tf_op jit(solution)/shard_map/ppermute | solution.py:645
  7.2 2.6 %pack_near.1 = (f32[544,128]{1,0:T(8,128)}, f32[544,128]{1,0:T(8,128)}) custom-call(s32[8,256]{1,0:T(8,128)} %get-tuple-element.23.target_hbm, f32[128,256]{1,0:T(8,128)} %get-tuple-element.20.meta_ref.meta_hbm, f32[256,1024]{1,0:T(8,128)} %loads_hbm.3), custom_call_target="tpu_custom_call" | custom-call | tf_op jit(solution)/shard_map/pack_near/pallas_call | solution.py:647
  9.8 0.1 collective-permute-start
  9.9 0.7 collective-permute-start.1
  10.6 0.0 copy-start
  10.6 1.2 %copy-done = f32[256,1024]{1,0:T(8,128)S(1)} copy-done((f32[256,1024]{1,0:T(8,128)S(1)}, f32[256,1024]{1,0:T(8,128)}, u32[]{:S(2)}) %copy-start) | copy-done | bytes 1048600
  11.8 0.0 copy-start.1
  11.8 0.9 %copy-done.1 = f32[3,64,64]{2,1,0:T(8,128)S(1)} copy-done((f32[3,64,64]{2,1,0:T(8,128)S(1)}, f32[3,64,64]{2,1,0:T(8,128)}, u32[]{:S(2)}) %copy-start.1) | copy-done | bytes 49176
  12.7 0.0 copy-start.3
  12.7 0.9 %copy-done.3 = f32[128,256]{1,0:T(8,128)S(1)} copy-done((f32[128,256]{1,0:T(8,128)S(1)}, f32[128,256]{1,0:T(8,128)}, u32[]{:S(2)}) %copy-start.3) | copy-done | bytes 131096
  13.6 0.0 copy-start.2
  13.6 1.9 %prepare.1 = (f32[256,1024]{1,0:T(8,128)S(1)}, f32[256,128]{1,0:T(8,128)S(1)}, bf16[2304,256]{1,0:T(8,128)(2,1)S(1)}, f32[16,256]{1,0:T(8,128)S(1)}) custom-call(f32[256,1024]{1,0:T(8,128)S(1)} %copy-done, f32[128,256]{1,0:T(8,128)S(1)} %copy-done.3, f32[3,64,64]{2,1,0:T(8,128)S(1)} %copy-done.1), custom_call_target="tpu_custom_call" | custom-call | flops 4000000000 | bytes 4000000 | tf_op jit(solution)/shard_map/prepare/pallas_call | solution.py:665
  15.5 4.6 %collective-permute-done.2.far_ref = f32[544,128]{1,0:T(8,128)S(1)} collective-permute-done((f32[544,128]{1,0:T(8,128)}, f32[544,128]{1,0:T(8,128)S(1)}, u32[]{:S(2)}, u32[]{:S(2)}) %collective-permute-start.2) | collective-permute-done | bytes 278560 | tf_op jit(solution)/shard_map/ppermute | solution.py:645
  20.1 0.0 collective-permute-done.core_ref
  20.1 0.0 collective-permute-done.1.chip_ref
  20.1 1.1 %arrange.1 = (bf16[2,4,256,256]{3,2,1,0:T(8,128)(2,1)S(1)}, bf16[2,4,256,256]{3,2,1,0:T(8,128)(2,1)S(1)}, f32[256,128]{1,0:T(8,128)S(1)}, f32[96,1152]{1,0:T(8,128)S(1)}, f32[96,1152]{1,0:T(8,128)S(1)}) custom-call(s32[1,1]{1,0:T(1,128)} %bitcast.pos_ref, f32[256,1024]{1,0:T(8,128)S(1)} %get-tuple-element.21.kept_ref, ...), custom_call_target="tpu_custom_call" | custom-call | tf_op jit(solution)/shard_map/arrange/pallas_call | solution.py:684
  21.2 0.1 collective-permute-start.3
  21.3 0.7 collective-permute-start.4
  22.0 0.0 copy-done.2
  22.0 11.3 %interior.1 = (bf16[3,2,4,256,256]{4,3,2,1,0:T(8,128)(2,1)S(1)}, bf16[2,3,96,768]{3,2,1,0:T(8,128)(2,1)S(1)}) custom-call(bf16[2,4,256,256]{3,2,1,0:T(8,128)(2,1)S(1)} %get-tuple-element.30.field_ref, f32[256,128]{1,0:T(8,128)S(1)} %get-tuple-element.31.meta_ref, bf16[2304,256]{1,0:T(8,128)(2,1)S(1)} %get-tuple-element.32.mixer_ref, f32[3,64,64]{2,1,0:T(8,128)S(1)} %copy-done.2), custom_call_target="tpu_custom_call" | custom-call | flops 10000000000 | bytes 8000000 | tf_op jit(solution)/shard_map/interior/pallas_call | solution.py:697
  33.3 0.0 collective-permute-done.3.core_ref
  33.3 0.0 collective-permute-done.4.chip_ref
  33.3 13.7 %sides.1 = (bf16[3,2,4,256,256]{4,3,2,1,0:T(8,128)(2,1)S(1)}, f32[16,128]{1,0:T(8,128)S(1)}) custom-call(s32[1,1]{1,0:T(1,128)} %bitcast.pos_ref, f32[96,1152]{1,0:T(8,128)S(1)} %collective-permute-done.3.core_ref, f32[96,1152]{1,0:T(8,128)S(1)} %collective-permute-done.4.chip_ref, bf16[2,4,256,256]{3,2,1,0:T(8,128)(2,1)S(1)} %get-tuple-element.30.field_ref, ...), custom_call_target="tpu_custom_call" | custom-call | tf_op jit(solution)/shard_map/sides/pallas_call | solution.py:713
  47.0 5.3 %collective-permute-start.7 = (f32[16,128]{1,0:T(8,128)S(1)}, f32[16,128]{1,0:T(8,128)S(1)}, u32[]{:S(2)}, u32[]{:S(2)}) collective-permute-start(f32[16,128]{1,0:T(8,128)S(1)} %get-tuple-element.37), channel_id=1, source_target_pairs={{0,3},{1,2},{2,1},{3,0},{4,7},{5,6},{6,5},{7,4},{8,11},{9,10},{10,... | collective-permute-start | bytes 24584 | tf_op jit(solution)/shard_map/ppermute | solution.py:735
  52.4 1.8 %collective-permute-start.6 = (f32[16,128]{1,0:T(8,128)S(1)}, f32[16,128]{1,0:T(8,128)S(1)}, u32[]{:S(2)}, u32[]{:S(2)}) collective-permute-start(f32[16,128]{1,0:T(8,128)S(1)} %get-tuple-element.37), channel_id=1, source_target_pairs={{0,2},{1,3},{2,0},{3,1},{4,6},{5,7},{6,4},{7,5},{8,10},{9,11},{10,... | collective-permute-start | bytes 24584 | tf_op jit(solution)/shard_map/ppermute | solution.py:735
  54.2 0.0 collective-permute-start.5
  54.2 0.0 collective-permute-done.7
  54.2 1.8 %collective-permute-done.6 = f32[16,128]{1,0:T(8,128)S(1)} collective-permute-done((f32[16,128]{1,0:T(8,128)S(1)}, f32[16,128]{1,0:T(8,128)S(1)}, u32[]{:S(2)}, u32[]{:S(2)}) %collective-permute-start.6) | collective-permute-done | bytes 8224 | tf_op jit(solution)/shard_map/ppermute | solution.py:735
  56.0 0.0 collective-permute-done.5
  56.0 3.4 %collective-permute-start.10 = (f32[16,128]{1,0:T(8,128)S(1)}, f32[16,128]{1,0:T(8,128)S(1)}, u32[]{:S(2)}, u32[]{:S(2)}) collective-permute-start(f32[16,128]{1,0:T(8,128)S(1)} %add_add_fusion.refs_0_), channel_id=1, source_target_pairs={{0,12},{1,13},{2,14},{3,15},{4,8},{5,9},{6,10},{7,11},{8,4},{9,5},... | collective-permute-start | bytes 24584 | tf_op jit(solution)/shard_map/ppermute | solution.py:735
  59.4 2.4 %collective-permute-start.9 = (f32[16,128]{1,0:T(8,128)S(1)}, f32[16,128]{1,0:T(8,128)S(1)}, u32[]{:S(2)}, u32[]{:S(2)}) collective-permute-start(f32[16,128]{1,0:T(8,128)S(1)} %add_add_fusion.refs_0_), channel_id=1, source_target_pairs={{0,8},{1,9},{2,10},{3,11},{4,12},{5,13},{6,14},{7,15},{8,0},{9,1},... | collective-permute-start | bytes 24584 | tf_op jit(solution)/shard_map/ppermute | solution.py:735
  61.8 0.0 collective-permute-start.8
  61.8 0.0 collective-permute-done.10.refs_3_
  61.8 2.2 %collective-permute-done.9.refs_2_ = f32[16,128]{1,0:T(8,128)S(1)} collective-permute-done((f32[16,128]{1,0:T(8,128)S(1)}, f32[16,128]{1,0:T(8,128)S(1)}, u32[]{:S(2)}, u32[]{:S(2)}) %collective-permute-start.9) | collective-permute-done | bytes 8224 | tf_op jit(solution)/shard_map/ppermute | solution.py:735
  64.0 1.5 %collective-permute-done.8.refs_1_ = f32[16,128]{1,0:T(8,128)S(1)} collective-permute-done((f32[16,128]{1,0:T(8,128)S(1)}, f32[16,128]{1,0:T(8,128)S(1)}, u32[]{:S(2)}, u32[]{:S(2)}) %collective-permute-start.8) | collective-permute-done | bytes 8224 | tf_op jit(solution)/shard_map/ppermute | solution.py:735
  65.4 7.7 %finish.1 = (f32[256,1024]{1,0:T(8,128)}, f32[256,1024]{1,0:T(8,128)}) custom-call(f32[3,64,64]{2,1,0:T(8,128)S(1)} %copy-done.2, bf16[2,4,256,256]{3,2,1,0:T(8,128)(2,1)S(1)} %get-tuple-element.27.geo_ref, bf16[3,2,4,256,256]{4,3,2,1,0:T(8,128)(2,1)S(1)} %get-tuple-element.36.basis_ref, f32[16,128]{1,0:T(8,128)S(1)} %add_add_fusion.refs_0_, ...), custom_call_target="tpu_custom_call" | custom-call | tf_op jit(solution)/shard_map/finish/pallas_call | solution.py:737
  (1 shorter events, 0.0 us)
Async XLA Ops:
  3.1 17.0 %collective-permute-start.2 = (f32[544,128]{1,0:T(8,128)}, f32[544,128]{1,0:T(8,128)S(1)}, u32[]{:S(2)}, u32[]{:S(2)}) collective-permute-start(f32[544,128]{1,0:T(8,128)} %get-tuple-element.26), channel_id=1, source_target_pairs={{0,8},{1,9},{2,10},{3,11},{4,12},{5,13},{6,14},{7,15},{8,0},{9,1},... | collective-permute-start | bytes 835592 | tf_op jit(solution)/shard_map/ppermute | solution.py:645
  9.8 10.3 %collective-permute-start = (f32[544,128]{1,0:T(8,128)}, f32[544,128]{1,0:T(8,128)S(1)}, u32[]{:S(2)}, u32[]{:S(2)}) collective-permute-start(f32[544,128]{1,0:T(8,128)} %get-tuple-element.24), channel_id=1, source_target_pairs={{0,1},{1,0},{2,3},{3,2},{4,5},{5,4},{6,7},{7,6},{8,9},{9,8},{10,11... | collective-permute-start | bytes 835592 | tf_op jit(solution)/shard_map/ppermute | solution.py:662
  9.9 10.2 %collective-permute-start.1 = (f32[544,128]{1,0:T(8,128)}, f32[544,128]{1,0:T(8,128)S(1)}, u32[]{:S(2)}, u32[]{:S(2)}) collective-permute-start(f32[544,128]{1,0:T(8,128)} %get-tuple-element.25), channel_id=1, source_target_pairs={{1,2},{3,4},{5,6},{7,8},{9,10},{11,12},{13,14},{2,1},{4,3},{6,5},{... | collective-permute-start | bytes 835592 | tf_op jit(solution)/shard_map/ppermute | solution.py:661
  10.6 1.2 %copy-start = (f32[256,1024]{1,0:T(8,128)S(1)}, f32[256,1024]{1,0:T(8,128)}, u32[]{:S(2)}) copy-start(f32[256,1024]{1,0:T(8,128)} %loads_hbm.3) | copy-start | bytes 3145732
  11.8 0.9 %copy-start.1 = (f32[3,64,64]{2,1,0:T(8,128)S(1)}, f32[3,64,64]{2,1,0:T(8,128)}, u32[]{:S(2)}) copy-start(f32[3,64,64]{2,1,0:T(8,128)} %blocks_ref.7) | copy-start | bytes 147460
  12.7 0.9 %copy-start.3 = (f32[128,256]{1,0:T(8,128)S(1)}, f32[128,256]{1,0:T(8,128)}, u32[]{:S(2)}) copy-start(f32[128,256]{1,0:T(8,128)} %get-tuple-element.20.meta_ref.meta_hbm) | copy-start | bytes 393220
  13.6 8.4 %copy-start.2 = (f32[3,64,64]{2,1,0:T(8,128)S(1)}, f32[3,64,64]{2,1,0:T(8,128)}, u32[]{:S(2)}) copy-start(f32[3,64,64]{2,1,0:T(8,128)} %blocks_ref.7) | copy-start | bytes 147460
  21.2 12.1 %collective-permute-start.3 = (f32[96,1152]{1,0:T(8,128)S(1)}, f32[96,1152]{1,0:T(8,128)S(1)}, u32[]{:S(2)}, u32[]{:S(2)}) collective-permute-start(f32[96,1152]{1,0:T(8,128)S(1)} %get-tuple-element.28), channel_id=1, source_target_pairs={{0,1},{1,0},{2,3},{3,2},{4,5},{5,4},{6,7},{7,6},{8,9},{9,8},{10,11... | collective-permute-start | bytes 1327112 | tf_op jit(solution)/shard_map/ppermute | solution.py:694
  21.3 12.0 %collective-permute-start.4 = (f32[96,1152]{1,0:T(8,128)S(1)}, f32[96,1152]{1,0:T(8,128)S(1)}, u32[]{:S(2)}, u32[]{:S(2)}) collective-permute-start(f32[96,1152]{1,0:T(8,128)S(1)} %get-tuple-element.29), channel_id=1, source_target_pairs={{1,2},{3,4},{5,6},{7,8},{9,10},{11,12},{13,14},{2,1},{4,3},{6,5},{... | collective-permute-start | bytes 1327112 | tf_op jit(solution)/shard_map/ppermute | solution.py:693
  47.0 7.2 %collective-permute-start.7 = (f32[16,128]{1,0:T(8,128)S(1)}, f32[16,128]{1,0:T(8,128)S(1)}, u32[]{:S(2)}, u32[]{:S(2)}) collective-permute-start(f32[16,128]{1,0:T(8,128)S(1)} %get-tuple-element.37), channel_id=1, source_target_pairs={{0,3},{1,2},{2,1},{3,0},{4,7},{5,6},{6,5},{7,4},{8,11},{9,10},{10,... | collective-permute-start | bytes 24584 | tf_op jit(solution)/shard_map/ppermute | solution.py:735
  52.4 3.7 %collective-permute-start.6 = (f32[16,128]{1,0:T(8,128)S(1)}, f32[16,128]{1,0:T(8,128)S(1)}, u32[]{:S(2)}, u32[]{:S(2)}) collective-permute-start(f32[16,128]{1,0:T(8,128)S(1)} %get-tuple-element.37), channel_id=1, source_target_pairs={{0,2},{1,3},{2,0},{3,1},{4,6},{5,7},{6,4},{7,5},{8,10},{9,11},{10,... | collective-permute-start | bytes 24584 | tf_op jit(solution)/shard_map/ppermute | solution.py:735
  54.2 1.8 %collective-permute-start.5 = (f32[16,128]{1,0:T(8,128)S(1)}, f32[16,128]{1,0:T(8,128)S(1)}, u32[]{:S(2)}, u32[]{:S(2)}) collective-permute-start(f32[16,128]{1,0:T(8,128)S(1)} %get-tuple-element.37), channel_id=1, source_target_pairs={{0,1},{1,0},{2,3},{3,2},{4,5},{5,4},{6,7},{7,6},{8,9},{9,8},{10,11... | collective-permute-start | bytes 24584 | tf_op jit(solution)/shard_map/ppermute | solution.py:735
  56.0 5.8 %collective-permute-start.10 = (f32[16,128]{1,0:T(8,128)S(1)}, f32[16,128]{1,0:T(8,128)S(1)}, u32[]{:S(2)}, u32[]{:S(2)}) collective-permute-start(f32[16,128]{1,0:T(8,128)S(1)} %add_add_fusion.refs_0_), channel_id=1, source_target_pairs={{0,12},{1,13},{2,14},{3,15},{4,8},{5,9},{6,10},{7,11},{8,4},{9,5},... | collective-permute-start | bytes 24584 | tf_op jit(solution)/shard_map/ppermute | solution.py:735
  59.4 4.5 %collective-permute-start.9 = (f32[16,128]{1,0:T(8,128)S(1)}, f32[16,128]{1,0:T(8,128)S(1)}, u32[]{:S(2)}, u32[]{:S(2)}) collective-permute-start(f32[16,128]{1,0:T(8,128)S(1)} %add_add_fusion.refs_0_), channel_id=1, source_target_pairs={{0,8},{1,9},{2,10},{3,11},{4,12},{5,13},{6,14},{7,15},{8,0},{9,1},... | collective-permute-start | bytes 24584 | tf_op jit(solution)/shard_map/ppermute | solution.py:735
  61.8 3.7 %collective-permute-start.8 = (f32[16,128]{1,0:T(8,128)S(1)}, f32[16,128]{1,0:T(8,128)S(1)}, u32[]{:S(2)}, u32[]{:S(2)}) collective-permute-start(f32[16,128]{1,0:T(8,128)S(1)} %add_add_fusion.refs_0_), channel_id=1, source_target_pairs={{0,4},{1,5},{2,6},{3,7},{4,0},{5,1},{6,2},{7,3},{8,12},{9,13},{10,... | collective-permute-start | bytes 24584 | tf_op jit(solution)/shard_map/ppermute | solution.py:735

commit v5 on v4

--- a/solution.py
+++ b/solution.py
@@ -85,6 +85,12 @@
         pos - 1 + 2 * odd,
         lax.rem(pos + devices // 2, jnp.int32(devices)),
     )
+
+
+def far_first(pos, devices):
+    half = devices // 2
+    group = (pos % half + 1) // 2 % max(half // 2, 1)
+    return group % 2 == 1
 
 
 def targets(pos, ids, rows, devices):
@@ -128,9 +134,9 @@
     return body, jnp.where(iota(notes.shape, 1) < META // 2, notes, 0.0)
 
 
-def pack_far_kernel(devices, pos_ref, loads_hbm, rows_hbm, dens_hbm, cols_hbm, types_hbm,
-                    far_ref, meta_ref, target_ref,
-                    loads_ref, rows_ref, dens_ref, cols_ref, types_ref, sems):
+def pack_first_kernel(devices, pos_ref, loads_hbm, rows_hbm, dens_hbm, cols_hbm, types_hbm,
+                      first_ref, meta_ref, target_ref,
+                      loads_ref, rows_ref, dens_ref, cols_ref, types_ref, sems):
     pairs = (
         (rows_hbm, rows_ref), (dens_hbm, dens_ref), (cols_hbm, cols_ref),
         (types_hbm, types_ref), (loads_hbm, loads_ref),
@@ -163,12 +169,13 @@
     meta_ref[4 * slots + 1:4 * slots + 2, :] = jnp.where(owner == pos, local, 0.0)
 
     copies[4].wait()
-    pick = one_hot(iota((cap, rows), 0) + 2 * cap == target)
-    fill_block(pick, loads_ref[...], meta_ref[...], far_ref)
-
-
-def pack_near_kernel(target_hbm, meta_hbm, loads_hbm, core_ref, chip_ref,
-                     target_ref, meta_ref, loads_ref, sems):
+    side = jnp.where(far_first(pos, devices), 2, 1)
+    pick = one_hot(iota((cap, rows), 0) + side * cap == target)
+    fill_block(pick, loads_ref[...], meta_ref[...], first_ref)
+
+
+def pack_second_kernel(devices, pos_ref, target_hbm, meta_hbm, loads_hbm, core_ref, second_ref,
+                       target_ref, meta_ref, loads_ref, sems):
     pairs = ((target_hbm, target_ref), (meta_hbm, meta_ref), (loads_hbm, loads_ref))
     copies = [
         pltpu.make_async_copy(source, target, sems.at[number])
@@ -180,7 +187,8 @@
         copy.wait()
     rows = loads_ref.shape[0]
     cap = rows // 4
-    for side, out_ref in enumerate((core_ref, chip_ref)):
+    late = jnp.where(far_first(pos_ref[0, 0], devices), 1, 2)
+    for side, out_ref in ((late, second_ref), (0, core_ref)):
         pick = one_hot(iota((cap, rows), 0) + side * cap == target_ref[0:1, :])
         fill_block(pick, loads_ref[...], meta_ref[...], out_ref)
 
@@ -238,13 +246,13 @@
                 mixer_ref[start:start + TILE, :] = wide
 
 
-def arrange_kernel(slots, pos_ref, kept_ref, kept_meta_ref, core_ref, chip_ref, far_ref,
+def arrange_kernel(slots, pos_ref, kept_ref, kept_meta_ref, core_ref, first_ref, second_ref,
                    geo_ref, field_ref, meta_ref, to_core_ref, to_chip_ref):
     rows, width = kept_ref.shape
     tiles = width // TILE
     edge = to_core_ref.shape[0]
     even = lax.rem(pos_ref[0, 0], jnp.int32(2)) == 0
-    blocks = [read_block(ref, width) for ref in (core_ref, chip_ref, far_ref)]
+    blocks = [read_block(ref, width) for ref in (core_ref, first_ref, second_ref)]
     arrived = jnp.concatenate([block[0] for block in blocks], axis=0)
     arrived_meta = jnp.concatenate([block[1] for block in blocks], axis=0)
     count = arrived.shape[0]
@@ -327,16 +335,12 @@
 
     lax.fori_loop(0, inside // HALO, build, 0)
 
-    def build_outer(chunk, carry):
-        side = lax.div(chunk, jnp.int32(ITERS))
-        first = pl.multiple_of(lax.rem(chunk, jnp.int32(ITERS)) * HALO, HALO)
-        start = pl.multiple_of(first + side * (rows - edge), HALO)
-        spot = jnp.where(side == 0, first + edge, first + rows - 2 * edge)
-        for kind, value in enumerate(stencil_rows(meta_ref[pl.ds(start, HALO), :], slots, spot)):
-            weights_ref[side, kind, pl.ds(first, HALO), :] = value
-        return carry
-
-    lax.fori_loop(0, 2 * ITERS, build_outer, 0)
+    def build_outer(side, chunk):
+        first = chunk * HALO
+        start = first + side * (rows - edge)
+        spot = first + edge if side == 0 else first + rows - 2 * edge
+        for kind, value in enumerate(stencil_rows(meta_ref[start:start + HALO, :], slots, spot)):
+            weights_ref[side, kind, first:first + HALO, :] = value
 
     for step in range(ITERS - 1):
         begin = HALO * (step + 1)
@@ -367,6 +371,8 @@
                     buckets[part, kind, tile * count:(tile + 1) * count, :] = (
                         half[kind * count:(kind + 1) * count]
                     )
+        for side in range(2):
+            build_outer(side, step)
         applied = mixed(buckets, mixer_ref, tiles * count)
         block = slice(begin, begin + count)
         for tile in range(tiles):
@@ -399,18 +405,14 @@
                 for part, half in enumerate(halves(value)):
                     v_refs[0, side, part, tile] = half
 
-    def build(chunk, carry):
-        side = lax.div(chunk, jnp.int32(2))
-        first = pl.multiple_of(lax.rem(chunk, jnp.int32(2)) * HALO, HALO)
-        start = pl.multiple_of(first + HALO * (1 - side), HALO)
-        spot = jnp.where(side == 0, first + HALO, first + rows - edge)
-        for kind, value in enumerate(
-            stencil_rows(meta_refs[side, pl.ds(start, HALO), :], slots, spot)
-        ):
-            stencil[side, kind, pl.ds(first, HALO), :] = value
-        return carry
-
-    lax.fori_loop(0, 4, build, 0)
+    def build(side):
+        for first in range(0, outer, HALO):
+            start = first + HALO * (1 - side)
+            spot = first + HALO if side == 0 else first + rows - edge
+            for kind, value in enumerate(
+                stencil_rows(meta_refs[side, start:start + HALO, :], slots, spot)
+            ):
+                stencil[side, kind, first:first + HALO, :] = value
 
     def window(step, side, part, tile):
         near = v_refs[step, side, part, tile]
@@ -438,9 +440,43 @@
                 pieces.append(stencil[1, kind, :keep, :])
         return jnp.concatenate(pieces, axis=0)
 
+    def convert(step):
+        begin = HALO * step
+        for half in range(2):
+
+            def piece(tile, part):
+                lanes = slice(part * META, (part + 1) * META)
+                return jnp.concatenate(
+                    [
+                        v_refs[step, 0, half, tile, count - begin:, lanes],
+                        inner_ref[step - 1, half, tile, begin:rows - begin, lanes],
+                        v_refs[step, 1, half, tile, :begin, lanes],
+                    ],
+                    axis=0,
+                )
+
+            for number, value in enumerate(swap_blocks(piece)):
+                lanes = slice(number % 2 * META, (number % 2 + 1) * META)
+                basis_ref[step - 1, half, number // 2, :, lanes] = value
+
+    def tall(step, part):
+        if step == 0:
+            return jnp.concatenate([geo_ref[part, tile] for tile in range(tiles)], axis=0)
+        return jnp.concatenate([basis_ref[step - 1, part, tile] for tile in range(tiles)], axis=0)
+
+    def mixed_gram(high, low):
+        return folded_rows(high[:, :TILE] + high[:, TILE:] + low, cases)
+
+    def even_gram(high):
+        cross = high[:, TILE:]
+        return folded_rows(high[:, :TILE] + cross + cross.T, cases)
+
+    sums = [first_ref[...]]
     for step in range(ITERS):
         centres = []
         for side in range(2):
+            if step == 0:
+                build(side)
             weights = jnp.concatenate(
                 [weight_rows(step, side, kind) for kind in range(TYPES)], axis=0
             )
@@ -464,45 +500,21 @@
                 for part, half in enumerate(halves(value)):
                     v_refs[step + 1, side, part, tile] = half
 
-    for step in range(1, ITERS + 1):
-        begin = HALO * step
-
-        def piece(tile, part):
-            lanes = slice(part * META, (part + 1) * META)
-            high, low = (
-                jnp.concatenate(
-                    [
-                        v_refs[step, 0, half, tile, count - begin:, lanes],
-                        inner_ref[step - 1, half, tile, begin:rows - begin, lanes],
-                        v_refs[step, 1, half, tile, :begin, lanes],
-                    ],
-                    axis=0,
-                )
-                for half in range(2)
-            )
-            return high.astype(F32) + low.astype(F32)
-
-        for number, value in enumerate(swap_blocks(piece)):
-            lanes = slice(number % 2 * META, (number % 2 + 1) * META)
-            for part, half in enumerate(halves(value)):
-                basis_ref[step - 1, part, number // 2, :, lanes] = half
-
-    def tall(step, part):
-        if step == 0:
-            return jnp.concatenate([geo_ref[part, tile] for tile in range(tiles)], axis=0)
-        return jnp.concatenate([basis_ref[step - 1, part, tile] for tile in range(tiles)], axis=0)
-
-    sums = [first_ref[...]]
-    for step in range(ITERS):
-        others = [tall(step + 1, 0), tall(step + 1, 1)]
-        if step > 0:
-            others += [tall(step, 0), tall(step, 1)]
-        high = dot_tn(tall(step, 0), jnp.concatenate(others, axis=1))
-        if step > 0:
-            cross = high[:, 3 * TILE:]
-            sums.append(folded_rows(high[:, 2 * TILE:3 * TILE] + cross + cross.T, cases))
-        low = dot_tn(tall(step, 1), tall(step + 1, 0))
-        sums.append(folded_rows(high[:, :TILE] + high[:, TILE:2 * TILE] + low, cases))
+        convert(step + 1)
+        if step == 1:
+            others = [tall(k, part) for k in range(3) for part in range(2)]
+            high = dot_tn(tall(1, 0), jnp.concatenate(others, axis=1))
+            low = dot_tn(tall(1, 1), jnp.concatenate([others[0], others[4]], axis=1))
+            sums.append(mixed_gram(high[:, :2 * TILE], low[:, :TILE]))
+            sums.append(even_gram(high[:, 2 * TILE:4 * TILE]))
+            sums.append(mixed_gram(high[:, 4 * TILE:], low[:, TILE:]))
+        elif step == 2:
+            others = [tall(k, part) for k in range(2, 4) for part in range(2)]
+            high = dot_tn(tall(2, 0), jnp.concatenate(others, axis=1))
+            low = dot_tn(tall(2, 1), others[2])
+            sums.append(even_gram(high[:, :2 * TILE]))
+            sums.append(mixed_gram(high[:, 2 * TILE:], low))
+
     remainder = jnp.concatenate(sums, axis=0)
     pieces = []
     for _ in range(3):
@@ -623,11 +635,17 @@
     same_chip = [(i, i ^ 1) for i in range(devices)]
     next_chip = [(i, i + 1) for i in range(1, devices - 1, 2)]
     next_chip += [(i + 1, i) for i in range(1, devices - 1, 2)]
-    across = [(i, (i + devices // 2) % devices) for i in range(devices)]
+    neighbour = dict(next_chip)
+    rounds = [[], []]
+    for i in range(devices):
+        early = 0 if far_first(i, devices) else 1
+        rounds[early].append((i, (i + devices // 2) % devices))
+        if i in neighbour:
+            rounds[1 - early].append((i, neighbour[i]))
 
     block = shape((cap * width // META + cap // 2, META), F32)
-    to_far, meta, target = pl.pallas_call(
-        functools.partial(pack_far_kernel, devices),
+    to_first, meta, target = pl.pallas_call(
+        functools.partial(pack_first_kernel, devices),
         out_shape=(block, shape((META, rows), F32), shape((8, rows), jnp.int32)),
         in_specs=[SMEM] + [HBM] * 5,
         out_specs=(VMEM,) * 3,
@@ -640,14 +658,14 @@
             pltpu.SemaphoreType.DMA((5,)),
         ],
         compiler_params=PACK_PARAMS,
-        name="pack_far",
+        name="pack_first",
     )(position, loads, row_ids.reshape(1, rows), densities.T, block_cols.T, block_types.T)
-    from_far = lax.ppermute(to_far, "sub", across)
-
-    to_core, to_chip = pl.pallas_call(
-        pack_near_kernel,
+    from_first = lax.ppermute(to_first, "sub", rounds[0])
+
+    to_core, to_second = pl.pallas_call(
+        functools.partial(pack_second_kernel, devices),
         out_shape=(block, block),
-        in_specs=[HBM] * 3,
+        in_specs=[SMEM] + [HBM] * 3,
         out_specs=(VMEM,) * 2,
         scratch_shapes=[
             pltpu.VMEM((8, rows), jnp.int32),
@@ -656,9 +674,9 @@
             pltpu.SemaphoreType.DMA((3,)),
         ],
         compiler_params=PACK_PARAMS,
-        name="pack_near",
-    )(target, meta, loads)
-    from_chip = lax.ppermute(to_chip, "sub", next_chip)
+        name="pack_second",
+    )(position, target, meta, loads)
+    from_second = lax.ppermute(to_second, "sub", rounds[1])
     from_core = lax.ppermute(to_core, "sub", same_chip)
 
     mixer_shape = shape((3 * TYPES * TILE, TILE), BF16)
@@ -688,7 +706,7 @@
         out_specs=(VMEM,) * 5,
         compiler_params=PARAMS,
         name="arrange",
-    )(position, kept, kept_meta, from_core, from_chip, from_far)
+    )(position, kept, kept_meta, from_core, from_first, from_second)
 
     halo_chip = lax.ppermute(to_chip, "sub", next_chip)
     halo_core = lax.ppermute(to_core, "sub", same_chip)

time: 73.5 us -> 71.8 us (0.977)
  Pallas kernels: 40.7 us -> 38.8 us
  waiting for transfers between devices: 10.1 us -> 11.8 us
  starting transfers between devices: 18.5 us -> 16.9 us
    ppermute x1, starting transfers between devices: 0.07 us -> 4.89 us  [on_device(): from_core = lax.ppermute(to_core, 'sub', same_chip)]
    ppermute x6, starting transfers between devices: 12.9 us -> 9.24 us  [on_device(): gathered_moments.append(lax.ppermute(partial, 'sub', swap))]
    ppermute x2, starting transfers between devices: 4.78 us -> 2.05 us  [the longest x1 1.37 us: on_device(): from_second = lax.ppermute(to_second, 'sub', rounds[1])]
    ppermute x2, waiting for transfers between devices: 4.59 us -> 7.21 us  [the longest x1 7.2 us: on_device(): from_second = lax.ppermute(to_second, 'sub', rounds[1])]
    pallas_call x1, Pallas kernels: 11.3 us -> 9.39 us  [on_device(): pl.pallas_call(functools.partial(interior_kernel, slots), out_shape=(basi...]
    ppermute x6, waiting for transfers between devices: 5.46 us -> 4.57 us  [on_device(): gathered_moments.append(lax.ppermute(partial, 'sub', swap))]
  transfers between devices with their start and end apart: 11 -> 11, of which waited for: 4 -> 4; matrix products, arithmetic and copies ran while one was open for 0% -> 0% of each run, Pallas kernels for 22% -> 19%
where the time goes in v5:
time: 71.8 us; the launch traced here: 71.5 us
  Pallas kernels  38.8 us (54%)
  starting transfers between devices  16.9 us (24%)
  waiting for transfers between devices  11.8 us (16%)
  local copies, waits for them, and re-layouts  3.02 us (4%)
  between operations  0.94 us (1%)
    pallas_call x1, Pallas kernels, on_device(): pl.pallas_call(functools.partial(sides_kernel, slots), out_shape=(basis_s...  13.7 us
    pallas_call x1, Pallas kernels, on_device(): pl.pallas_call(functools.partial(interior_kernel, slots), out_shape=(basi...  9.39 us
    ppermute x6, starting transfers between devices, on_device(): gathered_moments.append(lax.ppermute(partial, 'sub', swap))  9.24 us
    pallas_call x1, Pallas kernels, on_device(): pl.pallas_call(functools.partial(finish_kernel, slots), out_shape=(shape(...  7.66 us
    ppermute x1, waiting for transfers between devices, on_device(): from_second = lax.ppermute(to_second, 'sub', rounds[1])  7.2 us
    ppermute x1, starting transfers between devices, on_device(): from_core = lax.ppermute(to_core, 'sub', same_chip)  4.89 us
    ppermute x6, waiting for transfers between devices, on_device(): gathered_moments.append(lax.ppermute(partial, 'sub', swap))  4.57 us
    unnamed x8, local copies, waits for them, and re-layouts  3.02 us
  transfers between devices with their start and end apart: 11, of which 4 were waited for; matrix products, arithmetic and copies ran while one was open for 0% of the time, Pallas kernels for 19%

profile of v5, /device:TPU:0, one launch (start us, length us, event | category | flops | bytes accessed | tf_op | source)
XLA Modules:
  0.0 71.5 jit_solution(11362322764860552242)
XLA Ops:
  0.6 2.4 %pack_first.1 = (f32[544,128]{1,0:T(8,128)}, f32[128,256]{1,0:T(8,128)}, s32[8,256]{1,0:T(8,128)}) custom-call(s32[1,1]{1,0:T(1,128)} %bitcast.pos_ref, f32[256,1024]{1,0:T(8,128)} %loads_hbm.3, s32[1,256]{1,0:T(1,128)} %bitcast.8, f32[12,256]{1,0:T(8,128)} %bitcast.5, s32[12,256]{1,0:T(8,128)} %bitcast.6, s32[12,256]{1,0:T(8,128)} %bitcast.7), custom_call_target="tpu_custom_call" | custom-call | tf_op jit(solution)/shard_map/pack_first/pallas_call | solution.py:647
  3.1 0.7 collective-permute-start.1
  3.8 2.6 %pack_second.1 = (f32[544,128]{1,0:T(8,128)}, f32[544,128]{1,0:T(8,128)}) custom-call(s32[1,1]{1,0:T(1,128)} %bitcast.pos_ref, s32[8,256]{1,0:T(8,128)} %get-tuple-element.23.target_hbm, f32[128,256]{1,0:T(8,128)} %get-tuple-element.20.meta_ref.meta_hbm, f32[256,1024]{1,0:T(8,128)} %loads_hbm.3), custom_call_target="tpu_custom_call" | custom-call | tf_op jit(solution)/shard_map/pack_second/pallas_call | solution.py:665
  6.4 4.9 %collective-permute-start = (f32[544,128]{1,0:T(8,128)}, f32[544,128]{1,0:T(8,128)S(1)}, u32[]{:S(2)}, u32[]{:S(2)}) collective-permute-start(f32[544,128]{1,0:T(8,128)} %get-tuple-element.24), channel_id=1, source_target_pairs={{0,1},{1,0},{2,3},{3,2},{4,5},{5,4},{6,7},{7,6},{8,9},{9,8},{10,11... | collective-permute-start | bytes 835592 | tf_op jit(solution)/shard_map/ppermute | solution.py:680
  11.3 1.4 %collective-permute-start.2 = (f32[544,128]{1,0:T(8,128)}, f32[544,128]{1,0:T(8,128)S(1)}, u32[]{:S(2)}, u32[]{:S(2)}) collective-permute-start(f32[544,128]{1,0:T(8,128)} %get-tuple-element.26), channel_id=1, source_target_pairs={{0,8},{1,2},{2,1},{3,11},{4,12},{5,6},{6,5},{7,15},{8,0},{9,10},{1... | collective-permute-start | bytes 835592 | tf_op jit(solution)/shard_map/ppermute | solution.py:679
  12.7 0.0 copy-start
  12.7 1.2 %copy-done = f32[256,1024]{1,0:T(8,128)S(1)} copy-done((f32[256,1024]{1,0:T(8,128)S(1)}, f32[256,1024]{1,0:T(8,128)}, u32[]{:S(2)}) %copy-start) | copy-done | bytes 1048600
  13.9 0.0 copy-start.1
  13.9 0.9 %copy-done.1 = f32[3,64,64]{2,1,0:T(8,128)S(1)} copy-done((f32[3,64,64]{2,1,0:T(8,128)S(1)}, f32[3,64,64]{2,1,0:T(8,128)}, u32[]{:S(2)}) %copy-start.1) | copy-done | bytes 49176
  14.8 0.0 copy-start.3
  14.8 0.9 %copy-done.3 = f32[128,256]{1,0:T(8,128)S(1)} copy-done((f32[128,256]{1,0:T(8,128)S(1)}, f32[128,256]{1,0:T(8,128)}, u32[]{:S(2)}) %copy-start.3) | copy-done | bytes 131096
  15.7 0.0 copy-start.2
  15.7 1.9 %prepare.1 = (f32[256,1024]{1,0:T(8,128)S(1)}, f32[256,128]{1,0:T(8,128)S(1)}, bf16[2304,256]{1,0:T(8,128)(2,1)S(1)}, f32[16,256]{1,0:T(8,128)S(1)}) custom-call(f32[256,1024]{1,0:T(8,128)S(1)} %copy-done, f32[128,256]{1,0:T(8,128)S(1)} %copy-done.3, f32[3,64,64]{2,1,0:T(8,128)S(1)} %copy-done.1), custom_call_target="tpu_custom_call" | custom-call | flops 4000000000 | bytes 4000000 | tf_op jit(solution)/shard_map/prepare/pallas_call | solution.py:683
  17.6 0.0 collective-permute-done.1.first_ref
  17.6 0.0 collective-permute-done.core_ref
  17.6 7.2 %collective-permute-done.2.second_ref = f32[544,128]{1,0:T(8,128)S(1)} collective-permute-done((f32[544,128]{1,0:T(8,128)}, f32[544,128]{1,0:T(8,128)S(1)}, u32[]{:S(2)}, u32[]{:S(2)}) %collective-permute-start.2) | collective-permute-done | bytes 278560 | tf_op jit(solution)/shard_map/ppermute | solution.py:679
  24.8 1.1 %arrange.1 = (bf16[2,4,256,256]{3,2,1,0:T(8,128)(2,1)S(1)}, bf16[2,4,256,256]{3,2,1,0:T(8,128)(2,1)S(1)}, f32[256,128]{1,0:T(8,128)S(1)}, f32[96,1152]{1,0:T(8,128)S(1)}, f32[96,1152]{1,0:T(8,128)S(1)}) custom-call(s32[1,1]{1,0:T(1,128)} %bitcast.pos_ref, f32[256,1024]{1,0:T(8,128)S(1)} %get-tuple-element.21.kept_ref, ...), custom_call_target="tpu_custom_call" | custom-call | tf_op jit(solution)/shard_map/arrange/pallas_call | solution.py:702
  25.9 0.1 collective-permute-start.3
  26.0 0.7 collective-permute-start.4
  26.7 0.0 copy-done.2
  26.7 9.4 %interior.1 = (bf16[3,2,4,256,256]{4,3,2,1,0:T(8,128)(2,1)S(1)}, bf16[2,3,96,768]{3,2,1,0:T(8,128)(2,1)S(1)}) custom-call(bf16[2,4,256,256]{3,2,1,0:T(8,128)(2,1)S(1)} %get-tuple-element.30.field_ref, f32[256,128]{1,0:T(8,128)S(1)} %get-tuple-element.31.meta_ref, bf16[2304,256]{1,0:T(8,128)(2,1)S(1)} %get-tuple-element.32.mixer_ref, f32[3,64,64]{2,1,0:T(8,128)S(1)} %copy-done.2), custom_call_target="tpu_custom_call" | custom-call | flops 10000000000 | bytes 8000000 | tf_op jit(solution)/shard_map/interior/pallas_call | solution.py:715
  36.1 0.0 collective-permute-done.3.core_ref
  36.1 0.0 collective-permute-done.4.chip_ref
  36.1 13.7 %sides.1 = (bf16[3,2,4,256,256]{4,3,2,1,0:T(8,128)(2,1)S(1)}, f32[16,128]{1,0:T(8,128)S(1)}) custom-call(s32[1,1]{1,0:T(1,128)} %bitcast.pos_ref, f32[96,1152]{1,0:T(8,128)S(1)} %collective-permute-done.3.core_ref, f32[96,1152]{1,0:T(8,128)S(1)} %collective-permute-done.4.chip_ref, bf16[2,4,256,256]{3,2,1,0:T(8,128)(2,1)S(1)} %get-tuple-element.30.field_ref, ...), custom_call_target="tpu_custom_call" | custom-call | tf_op jit(solution)/shard_map/sides/pallas_call | solution.py:731
  49.8 0.4 collective-permute-start.7
  50.3 4.3 %collective-permute-start.6 = (f32[16,128]{1,0:T(8,128)S(1)}, f32[16,128]{1,0:T(8,128)S(1)}, u32[]{:S(2)}, u32[]{:S(2)}) collective-permute-start(f32[16,128]{1,0:T(8,128)S(1)} %get-tuple-element.37), channel_id=1, source_target_pairs={{0,2},{1,3},{2,0},{3,1},{4,6},{5,7},{6,4},{7,5},{8,10},{9,11},{10,... | collective-permute-start | bytes 24584 | tf_op jit(solution)/shard_map/ppermute | solution.py:753
  54.6 0.0 collective-permute-start.5
  54.6 0.0 collective-permute-done.7
  54.6 1.6 %collective-permute-done.6 = f32[16,128]{1,0:T(8,128)S(1)} collective-permute-done((f32[16,128]{1,0:T(8,128)S(1)}, f32[16,128]{1,0:T(8,128)S(1)}, u32[]{:S(2)}, u32[]{:S(2)}) %collective-permute-start.6) | collective-permute-done | bytes 8224 | tf_op jit(solution)/shard_map/ppermute | solution.py:753
  56.2 0.0 collective-permute-done.5
  56.2 2.9 %collective-permute-start.10 = (f32[16,128]{1,0:T(8,128)S(1)}, f32[16,128]{1,0:T(8,128)S(1)}, u32[]{:S(2)}, u32[]{:S(2)}) collective-permute-start(f32[16,128]{1,0:T(8,128)S(1)} %add_add_fusion.refs_0_), channel_id=1, source_target_pairs={{0,12},{1,13},{2,14},{3,15},{4,8},{5,9},{6,10},{7,11},{8,4},{9,5},... | collective-permute-start | bytes 24584 | tf_op jit(solution)/shard_map/ppermute | solution.py:753
  59.1 0.3 collective-permute-start.9
  59.4 1.3 %collective-permute-start.8 = (f32[16,128]{1,0:T(8,128)S(1)}, f32[16,128]{1,0:T(8,128)S(1)}, u32[]{:S(2)}, u32[]{:S(2)}) collective-permute-start(f32[16,128]{1,0:T(8,128)S(1)} %add_add_fusion.refs_0_), channel_id=1, source_target_pairs={{0,4},{1,5},{2,6},{3,7},{4,0},{5,1},{6,2},{7,3},{8,12},{9,13},{10,... | collective-permute-start | bytes 24584 | tf_op jit(solution)/shard_map/ppermute | solution.py:753
  60.7 1.1 %collective-permute-done.10.refs_3_ = f32[16,128]{1,0:T(8,128)S(1)} collective-permute-done((f32[16,128]{1,0:T(8,128)S(1)}, f32[16,128]{1,0:T(8,128)S(1)}, u32[]{:S(2)}, u32[]{:S(2)}) %collective-permute-start.10) | collective-permute-done | bytes 8224 | tf_op jit(solution)/shard_map/ppermute | solution.py:753
  61.8 1.9 %collective-permute-done.9.refs_2_ = f32[16,128]{1,0:T(8,128)S(1)} collective-permute-done((f32[16,128]{1,0:T(8,128)S(1)}, f32[16,128]{1,0:T(8,128)S(1)}, u32[]{:S(2)}, u32[]{:S(2)}) %collective-permute-start.9) | collective-permute-done | bytes 8224 | tf_op jit(solution)/shard_map/ppermute | solution.py:753
  63.6 0.0 collective-permute-done.8.refs_1_
  63.7 7.7 %finish.1 = (f32[256,1024]{1,0:T(8,128)}, f32[256,1024]{1,0:T(8,128)}) custom-call(f32[3,64,64]{2,1,0:T(8,128)S(1)} %copy-done.2, bf16[2,4,256,256]{3,2,1,0:T(8,128)(2,1)S(1)} %get-tuple-element.27.geo_ref, bf16[3,2,4,256,256]{4,3,2,1,0:T(8,128)(2,1)S(1)} %get-tuple-element.36.basis_ref, f32[16,128]{1,0:T(8,128)S(1)} %add_add_fusion.refs_0_, ...), custom_call_target="tpu_custom_call" | custom-call | tf_op jit(solution)/shard_map/finish/pallas_call | solution.py:755
  (1 shorter events, 0.0 us)
Async XLA Ops:
  3.1 14.5 %collective-permute-start.1 = (f32[544,128]{1,0:T(8,128)}, f32[544,128]{1,0:T(8,128)S(1)}, u32[]{:S(2)}, u32[]{:S(2)}) collective-permute-start(f32[544,128]{1,0:T(8,128)} %get-tuple-element.25), channel_id=1, source_target_pairs={{1,9},{2,10},{3,4},{4,3},{5,13},{6,14},{7,8},{8,7},{9,1},{10,2},{1... | collective-permute-start | bytes 835592 | tf_op jit(solution)/shard_map/ppermute | solution.py:663
  6.4 11.2 %collective-permute-start = (f32[544,128]{1,0:T(8,128)}, f32[544,128]{1,0:T(8,128)S(1)}, u32[]{:S(2)}, u32[]{:S(2)}) collective-permute-start(f32[544,128]{1,0:T(8,128)} %get-tuple-element.24), channel_id=1, source_target_pairs={{0,1},{1,0},{2,3},{3,2},{4,5},{5,4},{6,7},{7,6},{8,9},{9,8},{10,11... | collective-permute-start | bytes 835592 | tf_op jit(solution)/shard_map/ppermute | solution.py:680
  11.3 13.5 %collective-permute-start.2 = (f32[544,128]{1,0:T(8,128)}, f32[544,128]{1,0:T(8,128)S(1)}, u32[]{:S(2)}, u32[]{:S(2)}) collective-permute-start(f32[544,128]{1,0:T(8,128)} %get-tuple-element.26), channel_id=1, source_target_pairs={{0,8},{1,2},{2,1},{3,11},{4,12},{5,6},{6,5},{7,15},{8,0},{9,10},{1... | collective-permute-start | bytes 835592 | tf_op jit(solution)/shard_map/ppermute | solution.py:679
  12.7 1.2 %copy-start = (f32[256,1024]{1,0:T(8,128)S(1)}, f32[256,1024]{1,0:T(8,128)}, u32[]{:S(2)}) copy-start(f32[256,1024]{1,0:T(8,128)} %loads_hbm.3) | copy-start | bytes 3145732
  13.9 0.9 %copy-start.1 = (f32[3,64,64]{2,1,0:T(8,128)S(1)}, f32[3,64,64]{2,1,0:T(8,128)}, u32[]{:S(2)}) copy-start(f32[3,64,64]{2,1,0:T(8,128)} %blocks_ref.7) | copy-start | bytes 147460
  14.8 0.9 %copy-start.3 = (f32[128,256]{1,0:T(8,128)S(1)}, f32[128,256]{1,0:T(8,128)}, u32[]{:S(2)}) copy-start(f32[128,256]{1,0:T(8,128)} %get-tuple-element.20.meta_ref.meta_hbm) | copy-start | bytes 393220
  15.7 11.0 %copy-start.2 = (f32[3,64,64]{2,1,0:T(8,128)S(1)}, f32[3,64,64]{2,1,0:T(8,128)}, u32[]{:S(2)}) copy-start(f32[3,64,64]{2,1,0:T(8,128)} %blocks_ref.7) | copy-start | bytes 147460
  25.9 10.2 %collective-permute-start.3 = (f32[96,1152]{1,0:T(8,128)S(1)}, f32[96,1152]{1,0:T(8,128)S(1)}, u32[]{:S(2)}, u32[]{:S(2)}) collective-permute-start(f32[96,1152]{1,0:T(8,128)S(1)} %get-tuple-element.28), channel_id=1, source_target_pairs={{0,1},{1,0},{2,3},{3,2},{4,5},{5,4},{6,7},{7,6},{8,9},{9,8},{10,11... | collective-permute-start | bytes 1327112 | tf_op jit(solution)/shard_map/ppermute | solution.py:712
  26.0 10.1 %collective-permute-start.4 = (f32[96,1152]{1,0:T(8,128)S(1)}, f32[96,1152]{1,0:T(8,128)S(1)}, u32[]{:S(2)}, u32[]{:S(2)}) collective-permute-start(f32[96,1152]{1,0:T(8,128)S(1)} %get-tuple-element.29), channel_id=1, source_target_pairs={{1,2},{3,4},{5,6},{7,8},{9,10},{11,12},{13,14},{2,1},{4,3},{6,5},{... | collective-permute-start | bytes 1327112 | tf_op jit(solution)/shard_map/ppermute | solution.py:711
  49.8 4.8 %collective-permute-start.7 = (f32[16,128]{1,0:T(8,128)S(1)}, f32[16,128]{1,0:T(8,128)S(1)}, u32[]{:S(2)}, u32[]{:S(2)}) collective-permute-start(f32[16,128]{1,0:T(8,128)S(1)} %get-tuple-element.37), channel_id=1, source_target_pairs={{0,3},{1,2},{2,1},{3,0},{4,7},{5,6},{6,5},{7,4},{8,11},{9,10},{10,... | collective-permute-start | bytes 24584 | tf_op jit(solution)/shard_map/ppermute | solution.py:753
  50.3 6.0 %collective-permute-start.6 = (f32[16,128]{1,0:T(8,128)S(1)}, f32[16,128]{1,0:T(8,128)S(1)}, u32[]{:S(2)}, u32[]{:S(2)}) collective-permute-start(f32[16,128]{1,0:T(8,128)S(1)} %get-tuple-element.37), channel_id=1, source_target_pairs={{0,2},{1,3},{2,0},{3,1},{4,6},{5,7},{6,4},{7,5},{8,10},{9,11},{10,... | collective-permute-start | bytes 24584 | tf_op jit(solution)/shard_map/ppermute | solution.py:753
  54.6 1.6 %collective-permute-start.5 = (f32[16,128]{1,0:T(8,128)S(1)}, f32[16,128]{1,0:T(8,128)S(1)}, u32[]{:S(2)}, u32[]{:S(2)}) collective-permute-start(f32[16,128]{1,0:T(8,128)S(1)} %get-tuple-element.37), channel_id=1, source_target_pairs={{0,1},{1,0},{2,3},{3,2},{4,5},{5,4},{6,7},{7,6},{8,9},{9,8},{10,11... | collective-permute-start | bytes 24584 | tf_op jit(solution)/shard_map/ppermute | solution.py:753
  56.2 5.5 %collective-permute-start.10 = (f32[16,128]{1,0:T(8,128)S(1)}, f32[16,128]{1,0:T(8,128)S(1)}, u32[]{:S(2)}, u32[]{:S(2)}) collective-permute-start(f32[16,128]{1,0:T(8,128)S(1)} %add_add_fusion.refs_0_), channel_id=1, source_target_pairs={{0,12},{1,13},{2,14},{3,15},{4,8},{5,9},{6,10},{7,11},{8,4},{9,5},... | collective-permute-start | bytes 24584 | tf_op jit(solution)/shard_map/ppermute | solution.py:753
  59.1 4.5 %collective-permute-start.9 = (f32[16,128]{1,0:T(8,128)S(1)}, f32[16,128]{1,0:T(8,128)S(1)}, u32[]{:S(2)}, u32[]{:S(2)}) collective-permute-start(f32[16,128]{1,0:T(8,128)S(1)} %add_add_fusion.refs_0_), channel_id=1, source_target_pairs={{0,8},{1,9},{2,10},{3,11},{4,12},{5,13},{6,14},{7,15},{8,0},{9,1},... | collective-permute-start | bytes 24584 | tf_op jit(solution)/shard_map/ppermute | solution.py:753
  59.4 4.2 %collective-permute-start.8 = (f32[16,128]{1,0:T(8,128)S(1)}, f32[16,128]{1,0:T(8,128)S(1)}, u32[]{:S(2)}, u32[]{:S(2)}) collective-permute-start(f32[16,128]{1,0:T(8,128)S(1)} %add_add_fusion.refs_0_), channel_id=1, source_target_pairs={{0,4},{1,5},{2,6},{3,7},{4,0},{5,1},{6,2},{7,3},{8,12},{9,13},{10,... | collective-permute-start | bytes 24584 | tf_op jit(solution)/shard_map/ppermute | solution.py:753

commit v6 on v5

--- a/solution.py
+++ b/solution.py
@@ -113,30 +113,37 @@
     return target
 
 
-def fill_block(pick, loads, meta, out_ref):
+def fill_block(pick, loads, meta, out_refs):
     width = loads.shape[1]
     cap = pick.shape[0]
     twice = jnp.concatenate([pick, pick], axis=1)
     notes = dot_nt(twice, jnp.concatenate(halves(meta), axis=1))
+    notes = notes[:cap // 2] + pltpu.roll(notes[cap // 2:], META // 2, 1)
     body = dot(twice, jnp.concatenate(halves(loads), axis=0))
-    parts = width // META
-    for part in range(parts):
-        out_ref[part * cap:(part + 1) * cap, :] = body[:, part * META:(part + 1) * META]
-    out_ref[parts * cap:, :] = notes[:cap // 2] + pltpu.roll(notes[cap // 2:], META // 2, 1)
-
-
-def read_block(ref, width):
-    parts = width // META
-    cap = ref.shape[0] * 2 // (2 * parts + 1)
-    body = jnp.concatenate([ref[part * cap:(part + 1) * cap, :] for part in range(parts)], axis=1)
-    notes = ref[parts * cap:, :]
+    parts = width // META // len(out_refs)
+    few = cap // 2 // len(out_refs)
+    for number, out_ref in enumerate(out_refs):
+        for part in range(parts):
+            start = (number * parts + part) * META
+            out_ref[part * cap:(part + 1) * cap, :] = body[:, start:start + META]
+        out_ref[parts * cap:, :] = notes[number * few:(number + 1) * few]
+
+
+def read_block(refs, width):
+    parts = width // META // len(refs)
+    few = refs[0].shape[0] // (2 * parts * len(refs) + 1)
+    cap = 2 * few * len(refs)
+    body = jnp.concatenate(
+        [ref[part * cap:(part + 1) * cap, :] for ref in refs for part in range(parts)], axis=1
+    )
+    notes = jnp.concatenate([ref[parts * cap:, :] for ref in refs], axis=0)
     notes = jnp.concatenate([notes, pltpu.roll(notes, META // 2, 1)], axis=0)
     return body, jnp.where(iota(notes.shape, 1) < META // 2, notes, 0.0)
 
 
-def pack_first_kernel(devices, pos_ref, loads_hbm, rows_hbm, dens_hbm, cols_hbm, types_hbm,
-                      first_ref, meta_ref, target_ref,
-                      loads_ref, rows_ref, dens_ref, cols_ref, types_ref, sems):
+def pack_kernel(devices, pos_ref, loads_hbm, rows_hbm, dens_hbm, cols_hbm, types_hbm,
+                first_a, first_b, second_a, second_b, core_ref, meta_ref,
+                loads_ref, rows_ref, dens_ref, cols_ref, types_ref, sems):
     pairs = (
         (rows_hbm, rows_ref), (dens_hbm, dens_ref), (cols_hbm, cols_ref),
         (types_hbm, types_ref), (loads_hbm, loads_ref),
@@ -157,7 +164,6 @@
     owner = lax.div(ids, jnp.int32(rows))
     local = (ids - owner * rows + 1).astype(F32)
     target = targets(pos, ids, rows, devices)
-    target_ref[...] = jnp.broadcast_to(target, target_ref.shape)
 
     density = dens_ref[...]
     kinds = types_ref[...]
@@ -169,28 +175,10 @@
     meta_ref[4 * slots + 1:4 * slots + 2, :] = jnp.where(owner == pos, local, 0.0)
 
     copies[4].wait()
-    side = jnp.where(far_first(pos, devices), 2, 1)
-    pick = one_hot(iota((cap, rows), 0) + side * cap == target)
-    fill_block(pick, loads_ref[...], meta_ref[...], first_ref)
-
-
-def pack_second_kernel(devices, pos_ref, target_hbm, meta_hbm, loads_hbm, core_ref, second_ref,
-                       target_ref, meta_ref, loads_ref, sems):
-    pairs = ((target_hbm, target_ref), (meta_hbm, meta_ref), (loads_hbm, loads_ref))
-    copies = [
-        pltpu.make_async_copy(source, target, sems.at[number])
-        for number, (source, target) in enumerate(pairs)
-    ]
-    for copy in copies:
-        copy.start()
-    for copy in copies:
-        copy.wait()
-    rows = loads_ref.shape[0]
-    cap = rows // 4
-    late = jnp.where(far_first(pos_ref[0, 0], devices), 1, 2)
-    for side, out_ref in ((late, second_ref), (0, core_ref)):
-        pick = one_hot(iota((cap, rows), 0) + side * cap == target_ref[0:1, :])
-        fill_block(pick, loads_ref[...], meta_ref[...], out_ref)
+    early = jnp.where(far_first(pos, devices), 2, 1)
+    for side, refs in ((early, (first_a, first_b)), (3 - early, (second_a, second_b)), (0, (core_ref,))):
+        pick = one_hot(iota((cap, rows), 0) + side * cap == target)
+        fill_block(pick, loads_ref[...], meta_ref[...], refs)
 
 
 def reorder(parts, tiles):
@@ -246,13 +234,14 @@
                 mixer_ref[start:start + TILE, :] = wide
 
 
-def arrange_kernel(slots, pos_ref, kept_ref, kept_meta_ref, core_ref, first_ref, second_ref,
-                   geo_ref, field_ref, meta_ref, to_core_ref, to_chip_ref):
+def arrange_kernel(slots, pos_ref, first_a, first_b, second_a, second_b, core_ref,
+                   kept_ref, kept_meta_ref, geo_ref, field_ref, meta_ref, to_core_ref, to_chip_ref):
     rows, width = kept_ref.shape
     tiles = width // TILE
     edge = to_core_ref.shape[0]
     even = lax.rem(pos_ref[0, 0], jnp.int32(2)) == 0
-    blocks = [read_block(ref, width) for ref in (core_ref, first_ref, second_ref)]
+    groups = ((first_a, first_b), (second_a, second_b), (core_ref,))
+    blocks = [read_block(refs, width) for refs in groups]
     arrived = jnp.concatenate([block[0] for block in blocks], axis=0)
     arrived_meta = jnp.concatenate([block[1] for block in blocks], axis=0)
     count = arrived.shape[0]
@@ -308,7 +297,11 @@
 
 
 def gathered(weights, near, fine):
-    return halves(dot(weights, jnp.concatenate([near, fine, near], axis=0)))
+    parts = [near, fine, near]
+    spare = weights.shape[1] - 3 * near.shape[0]
+    if spare:
+        parts.append(jnp.zeros((spare, near.shape[1]), BF16))
+    return halves(dot(weights, jnp.concatenate(parts, axis=0)))
 
 
 def mixed(buckets, mixer_ref, count):
@@ -414,19 +407,20 @@
             ):
                 stencil[side, kind, first:first + HALO, :] = value
 
+    reach = count + 2 * HALO
+
     def window(step, side, part, tile):
         near = v_refs[step, side, part, tile]
-        if step == 0:
-            if side == 0:
-                return jnp.concatenate([near, field_ref[part, tile, :rest, :]], axis=0)
-            return jnp.concatenate([field_ref[part, tile, rows - rest:, :], near], axis=0)
-        blank = jnp.zeros((HALO * step, TILE), BF16)
         begin = HALO * step
         if side == 0:
-            far = inner_ref[step - 1, part, tile, begin:rest, :]
-            return jnp.concatenate([blank, near, far], axis=0)
-        far = inner_ref[step - 1, part, tile, rows - rest:rows - begin, :]
-        return jnp.concatenate([far, near, blank], axis=0)
+            block = slice(begin, begin + reach - count)
+        else:
+            block = slice(rows - begin - (reach - count), rows - begin)
+        if step == 0:
+            far = field_ref[part, tile, block, :]
+        else:
+            far = inner_ref[step - 1, part, tile, block, :]
+        return jnp.concatenate([near, far] if side == 0 else [far, near], axis=0)
 
     def weight_rows(step, side, kind):
         keep = outer - HALO * step
@@ -438,7 +432,12 @@
             pieces = [weights_ref[1, kind, keep:, :]]
             if keep:
                 pieces.append(stencil[1, kind, :keep, :])
-        return jnp.concatenate(pieces, axis=0)
+        rows_all = jnp.concatenate(pieces, axis=0)
+        first = HALO * step if side == 0 else TILE - reach - HALO * step
+        high = rows_all[:, first:first + reach]
+        low = rows_all[:, 2 * TILE + first:2 * TILE + first + reach]
+        blank = jnp.zeros((count, 2 * TILE - 3 * reach), BF16)
+        return jnp.concatenate([high, high, low, blank], axis=1)
 
     def convert(step):
         begin = HALO * step
@@ -463,9 +462,6 @@
         if step == 0:
             return jnp.concatenate([geo_ref[part, tile] for tile in range(tiles)], axis=0)
         return jnp.concatenate([basis_ref[step - 1, part, tile] for tile in range(tiles)], axis=0)
-
-    def mixed_gram(high, low):
-        return folded_rows(high[:, :TILE] + high[:, TILE:] + low, cases)
 
     def even_gram(high):
         cross = high[:, TILE:]
@@ -483,8 +479,7 @@
             for tile in range(tiles):
                 row = (side * tiles + tile) * count
                 near, fine = (window(step, side, part, tile) for part in range(2))
-                first = HALO * (step + 1) if side == 0 else TILE - HALO * (step + 1) - count
-                centres.append((near[first:first + count], fine[first:first + count]))
+                centres.append((near[HALO:HALO + count], fine[HALO:HALO + count]))
                 for part, half in enumerate(gathered(weights, near, fine)):
                     for kind in range(TYPES):
                         buckets[part, kind, row:row + count, :] = (
@@ -501,19 +496,25 @@
                     v_refs[step + 1, side, part, tile] = half
 
         convert(step + 1)
-        if step == 1:
-            others = [tall(k, part) for k in range(3) for part in range(2)]
-            high = dot_tn(tall(1, 0), jnp.concatenate(others, axis=1))
-            low = dot_tn(tall(1, 1), jnp.concatenate([others[0], others[4]], axis=1))
-            sums.append(mixed_gram(high[:, :2 * TILE], low[:, :TILE]))
-            sums.append(even_gram(high[:, 2 * TILE:4 * TILE]))
-            sums.append(mixed_gram(high[:, 4 * TILE:], low[:, TILE:]))
-        elif step == 2:
-            others = [tall(k, part) for k in range(2, 4) for part in range(2)]
-            high = dot_tn(tall(2, 0), jnp.concatenate(others, axis=1))
-            low = dot_tn(tall(2, 1), others[2])
-            sums.append(even_gram(high[:, :2 * TILE]))
-            sums.append(mixed_gram(high[:, 2 * TILE:], low))
+        if step == 0:
+            left = jnp.concatenate([tall(1, 0), tall(1, 1)], axis=1)
+            high = dot_tn(left, tall(0, 0))
+            fine = dot_tn(tall(1, 0), jnp.concatenate([tall(0, 1), tall(1, 0), tall(1, 1)], axis=1))
+            sums.append(folded_rows(high[:TILE] + high[TILE:] + fine[:, :TILE], cases))
+            sums.append(even_gram(fine[:, TILE:]))
+        elif step == 1:
+            left = jnp.concatenate([tall(1, 0), tall(2, 0), tall(1, 1)], axis=1)
+            high = dot_tn(left, tall(2, 0))
+            fine = dot_tn(left[:, :2 * TILE], tall(2, 1))
+            sums.append(folded_rows(high[:TILE] + high[2 * TILE:] + fine[:TILE], cases))
+            sums.append(
+                even_gram(jnp.concatenate([high[TILE:2 * TILE], fine[TILE:]], axis=1))
+            )
+        else:
+            left = jnp.concatenate([tall(2, 0), tall(2, 1)], axis=1)
+            high = dot_tn(left, tall(3, 0))
+            fine = dot_tn(tall(2, 0), tall(3, 1))
+            sums.append(folded_rows(high[:TILE] + high[TILE:] + fine, cases))
 
     remainder = jnp.concatenate(sums, axis=0)
     pieces = []
@@ -643,12 +644,13 @@
         if i in neighbour:
             rounds[1 - early].append((i, neighbour[i]))
 
-    block = shape((cap * width // META + cap // 2, META), F32)
-    to_first, meta, target = pl.pallas_call(
-        functools.partial(pack_first_kernel, devices),
-        out_shape=(block, shape((META, rows), F32), shape((8, rows), jnp.int32)),
+    length = cap * width // META + cap // 2
+    whole, piece = shape((length, META), F32), shape((length // 2, META), F32)
+    *outgoing, meta = pl.pallas_call(
+        functools.partial(pack_kernel, devices),
+        out_shape=(piece, piece, piece, piece, whole, shape((META, rows), F32)),
         in_specs=[SMEM] + [HBM] * 5,
-        out_specs=(VMEM,) * 3,
+        out_specs=(VMEM,) * 6,
         scratch_shapes=[
             pltpu.VMEM((rows, width), F32),
             pltpu.VMEM((1, rows), jnp.int32),
@@ -658,26 +660,10 @@
             pltpu.SemaphoreType.DMA((5,)),
         ],
         compiler_params=PACK_PARAMS,
-        name="pack_first",
+        name="pack",
     )(position, loads, row_ids.reshape(1, rows), densities.T, block_cols.T, block_types.T)
-    from_first = lax.ppermute(to_first, "sub", rounds[0])
-
-    to_core, to_second = pl.pallas_call(
-        functools.partial(pack_second_kernel, devices),
-        out_shape=(block, block),
-        in_specs=[SMEM] + [HBM] * 3,
-        out_specs=(VMEM,) * 2,
-        scratch_shapes=[
-            pltpu.VMEM((8, rows), jnp.int32),
-            pltpu.VMEM((META, rows), F32),
-            pltpu.VMEM((rows, width), F32),
-            pltpu.SemaphoreType.DMA((3,)),
-        ],
-        compiler_params=PACK_PARAMS,
-        name="pack_second",
-    )(position, target, meta, loads)
-    from_second = lax.ppermute(to_second, "sub", rounds[1])
-    from_core = lax.ppermute(to_core, "sub", same_chip)
+    routes = (rounds[0], rounds[0], rounds[1], rounds[1], same_chip)
+    incoming = [lax.ppermute(part, "sub", route) for part, route in zip(outgoing, routes)]
 
     mixer_shape = shape((3 * TYPES * TILE, TILE), BF16)
     kept, kept_meta, mixer, first = pl.pallas_call(
@@ -702,11 +688,11 @@
     geo, field, geo_meta, to_core, to_chip = pl.pallas_call(
         functools.partial(arrange_kernel, slots),
         out_shape=(pair, pair, shape((rows, META), F32), border, border),
-        in_specs=[SMEM] + [VMEM] * 5,
+        in_specs=[SMEM] + [VMEM] * 7,
         out_specs=(VMEM,) * 5,
         compiler_params=PARAMS,
         name="arrange",
-    )(position, kept, kept_meta, from_core, from_first, from_second)
+    )(position, *incoming, kept, kept_meta)
 
     halo_chip = lax.ppermute(to_chip, "sub", next_chip)
     halo_core = lax.ppermute(to_core, "sub", same_chip)

time: 71.8 us -> 73.3 us (1.021)
  starting transfers between devices: 16.9 us -> 20.6 us
  Pallas kernels: 38.8 us -> 37.6 us
  waiting for transfers between devices: 11.8 us -> 10.8 us
    ppermute x3 -> x5, starting transfers between devices: 6.93 us -> 10.6 us  [on_device(): lax.ppermute(part, 'sub', route)]
    pallas_call x2 -> x1, Pallas kernels: 5.06 us -> 2.88 us  [on_device(): pl.pallas_call(functools.partial(pack_kernel, devices), out_shape=(piece,...]
    ppermute x3 -> x5, waiting for transfers between devices: 7.21 us -> 6.13 us  [on_device(): lax.ppermute(part, 'sub', route)]
    pallas_call x1, Pallas kernels: 13.7 us -> 14.7 us  [on_device(): pl.pallas_call(functools.partial(sides_kernel, slots), out_shape=(basis_s...]
  transfers between devices with their start and end apart: 11 -> 13, of which waited for: 4 -> 5; matrix products, arithmetic and copies ran while one was open for 0% -> 0% of each run, Pallas kernels for 19% -> 15%
where the time goes in v6:
time: 73.3 us; the launch traced here: 73 us
  Pallas kernels  37.6 us (51%)
  starting transfers between devices  20.6 us (28%)
  waiting for transfers between devices  10.8 us (15%)
  local copies, waits for them, and re-layouts  3.02 us (4%)
  between operations  0.94 us (1%)
    pallas_call x1, Pallas kernels, on_device(): pl.pallas_call(functools.partial(sides_kernel, slots), out_shape=(basis_s...  14.7 us
    ppermute x5, starting transfers between devices, on_device(): lax.ppermute(part, 'sub', route)  10.6 us
    pallas_call x1, Pallas kernels, on_device(): pl.pallas_call(functools.partial(interior_kernel, slots), out_shape=(basi...  9.39 us
    ppermute x6, starting transfers between devices, on_device(): gathered_moments.append(lax.ppermute(partial, 'sub', swap))  9.24 us
    pallas_call x1, Pallas kernels, on_device(): pl.pallas_call(functools.partial(finish_kernel, slots), out_shape=(shape(...  7.66 us
    ppermute x5, waiting for transfers between devices, on_device(): lax.ppermute(part, 'sub', route)  6.13 us
    ppermute x6, waiting for transfers between devices, on_device(): gathered_moments.append(lax.ppermute(partial, 'sub', swap))  4.62 us
    unnamed x8, local copies, waits for them, and re-layouts  3.02 us
  transfers between devices with their start and end apart: 13, of which 5 were waited for; matrix products, arithmetic and copies ran while one was open for 0% of the time, Pallas kernels for 15%

profile of v6, /device:TPU:0, one launch (start us, length us, event | category | flops | bytes accessed | tf_op | source)
XLA Modules:
  0.0 73.0 jit_solution(18076516535595230168)
XLA Ops:
  0.6 2.9 %pack.1 = (f32[272,128]{1,0:T(8,128)}, f32[272,128]{1,0:T(8,128)}, f32[272,128]{1,0:T(8,128)}, f32[272,128]{1,0:T(8,128)}, f32[544,128]{1,0:T(8,128)}, /*index=5*/f32[128,256]{1,0:T(8,128)}) custom-call(s32[1,1]{1,0:T(1,128)} %bitcast.pos_ref, f32[256,1024]{1,0:T(8,128)} %loads_ref.1, s32[1,256]{1,0:T(1,128)} %bitcast.8, f32[12,256]{1,0:T(8,128)} %bitcast.5, ...), custom_call_target="tpu_custom_call" | custom-call | tf_op jit(solution)/shard_map/pack/pallas_call | solution.py:649
  3.5 0.7 collective-permute-start
  4.2 0.7 collective-permute-start.1
  4.9 9.2 %collective-permute-start.2 = (f32[272,128]{1,0:T(8,128)}, f32[272,128]{1,0:T(8,128)S(1)}, u32[]{:S(2)}, u32[]{:S(2)}) collective-permute-start(f32[272,128]{1,0:T(8,128)} %get-tuple-element.23), channel_id=1, source_target_pairs={{0,8},{1,2},{2,1},{3,11},{4,12},{5,6},{6,5},{7,15},{8,0},{9,10},{1... | collective-permute-start | bytes 417800 | tf_op jit(solution)/shard_map/ppermute | solution.py:666
  14.1 0.1 collective-permute-start.3
  14.2 0.0 collective-permute-start.4
  14.2 0.0 copy-start
  14.2 1.2 %copy-done = f32[256,1024]{1,0:T(8,128)S(1)} copy-done((f32[256,1024]{1,0:T(8,128)S(1)}, f32[256,1024]{1,0:T(8,128)}, u32[]{:S(2)}) %copy-start) | copy-done | bytes 1048600
  15.4 0.0 copy-start.1
  15.4 0.9 %copy-done.1 = f32[3,64,64]{2,1,0:T(8,128)S(1)} copy-done((f32[3,64,64]{2,1,0:T(8,128)S(1)}, f32[3,64,64]{2,1,0:T(8,128)}, u32[]{:S(2)}) %copy-start.1) | copy-done | bytes 49176
  16.3 0.0 copy-start.3
  16.3 0.9 %copy-done.3 = f32[128,256]{1,0:T(8,128)S(1)} copy-done((f32[128,256]{1,0:T(8,128)S(1)}, f32[128,256]{1,0:T(8,128)}, u32[]{:S(2)}) %copy-start.3) | copy-done | bytes 131096
  17.2 0.0 copy-start.2
  17.2 1.9 %prepare.1 = (f32[256,1024]{1,0:T(8,128)S(1)}, f32[256,128]{1,0:T(8,128)S(1)}, bf16[2304,256]{1,0:T(8,128)(2,1)S(1)}, f32[16,256]{1,0:T(8,128)S(1)}) custom-call(f32[256,1024]{1,0:T(8,128)S(1)} %copy-done, f32[128,256]{1,0:T(8,128)S(1)} %copy-done.3, f32[3,64,64]{2,1,0:T(8,128)S(1)} %copy-done.1), custom_call_target="tpu_custom_call" | custom-call | flops 4000000000 | bytes 4000000 | tf_op jit(solution)/shard_map/prepare/pallas_call | solution.py:669
  19.1 0.0 collective-permute-done.first_a
  19.1 0.0 collective-permute-done.1.first_b
  19.2 4.6 %collective-permute-done.2.second_a = f32[272,128]{1,0:T(8,128)S(1)} collective-permute-done((f32[272,128]{1,0:T(8,128)}, f32[272,128]{1,0:T(8,128)S(1)}, u32[]{:S(2)}, u32[]{:S(2)}) %collective-permute-start.2) | collective-permute-done | bytes 139296 | tf_op jit(solution)/shard_map/ppermute | solution.py:666
  23.8 1.5 %collective-permute-done.3.second_b = f32[272,128]{1,0:T(8,128)S(1)} collective-permute-done((f32[272,128]{1,0:T(8,128)}, f32[272,128]{1,0:T(8,128)S(1)}, u32[]{:S(2)}, u32[]{:S(2)}) %collective-permute-start.3) | collective-permute-done | bytes 139296 | tf_op jit(solution)/shard_map/ppermute | solution.py:666
  25.3 0.0 collective-permute-done.4.core_ref
  25.3 1.1 %arrange.1 = (bf16[2,4,256,256]{3,2,1,0:T(8,128)(2,1)S(1)}, bf16[2,4,256,256]{3,2,1,0:T(8,128)(2,1)S(1)}, f32[256,128]{1,0:T(8,128)S(1)}, f32[96,1152]{1,0:T(8,128)S(1)}, f32[96,1152]{1,0:T(8,128)S(1)}) custom-call(s32[1,1]{1,0:T(1,128)} %bitcast.pos_ref, f32[272,128]{1,0:T(8,128)S(1)} %collective-permute-done.first_a, ...), custom_call_target="tpu_custom_call" | custom-call | tf_op jit(solution)/shard_map/arrange/pallas_call | solution.py:688
  26.3 0.1 collective-permute-start.5
  26.4 0.7 collective-permute-start.6
  27.1 0.0 copy-done.2
  27.1 9.4 %interior.1 = (bf16[3,2,4,256,256]{4,3,2,1,0:T(8,128)(2,1)S(1)}, bf16[2,3,96,768]{3,2,1,0:T(8,128)(2,1)S(1)}) custom-call(bf16[2,4,256,256]{3,2,1,0:T(8,128)(2,1)S(1)} %get-tuple-element.32.field_ref, f32[256,128]{1,0:T(8,128)S(1)} %get-tuple-element.33.meta_ref, bf16[2304,256]{1,0:T(8,128)(2,1)S(1)} %get-tuple-element.34.mixer_ref, f32[3,64,64]{2,1,0:T(8,128)S(1)} %copy-done.2), custom_call_target="tpu_custom_call" | custom-call | flops 10000000000 | bytes 8000000 | tf_op jit(solution)/shard_map/interior/pallas_call | solution.py:701
  36.5 0.0 collective-permute-done.5.core_ref
  36.5 0.0 collective-permute-done.6.chip_ref
  36.6 14.7 %sides.1 = (bf16[3,2,4,256,256]{4,3,2,1,0:T(8,128)(2,1)S(1)}, f32[16,128]{1,0:T(8,128)S(1)}) custom-call(s32[1,1]{1,0:T(1,128)} %bitcast.pos_ref, f32[96,1152]{1,0:T(8,128)S(1)} %collective-permute-done.5.core_ref, f32[96,1152]{1,0:T(8,128)S(1)} %collective-permute-done.6.chip_ref, bf16[2,4,256,256]{3,2,1,0:T(8,128)(2,1)S(1)} %get-tuple-element.32.field_ref, ...), custom_call_target="tpu_custom_call" | custom-call | tf_op jit(solution)/shard_map/sides/pallas_call | solution.py:717
  51.3 1.1 %collective-permute-start.9 = (f32[16,128]{1,0:T(8,128)S(1)}, f32[16,128]{1,0:T(8,128)S(1)}, u32[]{:S(2)}, u32[]{:S(2)}) collective-permute-start(f32[16,128]{1,0:T(8,128)S(1)} %get-tuple-element.39), channel_id=1, source_target_pairs={{0,3},{1,2},{2,1},{3,0},{4,7},{5,6},{6,5},{7,4},{8,11},{9,10},{10,... | collective-permute-start | bytes 24584 | tf_op jit(solution)/shard_map/ppermute | solution.py:739
  52.4 3.6 %collective-permute-start.8 = (f32[16,128]{1,0:T(8,128)S(1)}, f32[16,128]{1,0:T(8,128)S(1)}, u32[]{:S(2)}, u32[]{:S(2)}) collective-permute-start(f32[16,128]{1,0:T(8,128)S(1)} %get-tuple-element.39), channel_id=1, source_target_pairs={{0,2},{1,3},{2,0},{3,1},{4,6},{5,7},{6,4},{7,5},{8,10},{9,11},{10,... | collective-permute-start | bytes 24584 | tf_op jit(solution)/shard_map/ppermute | solution.py:739
  56.0 0.0 collective-permute-start.7
  56.1 0.0 collective-permute-done.9
  56.1 1.6 %collective-permute-done.8 = f32[16,128]{1,0:T(8,128)S(1)} collective-permute-done((f32[16,128]{1,0:T(8,128)S(1)}, f32[16,128]{1,0:T(8,128)S(1)}, u32[]{:S(2)}, u32[]{:S(2)}) %collective-permute-start.8) | collective-permute-done | bytes 8224 | tf_op jit(solution)/shard_map/ppermute | solution.py:739
  57.7 0.0 collective-permute-done.7
  57.7 2.9 %collective-permute-start.12 = (f32[16,128]{1,0:T(8,128)S(1)}, f32[16,128]{1,0:T(8,128)S(1)}, u32[]{:S(2)}, u32[]{:S(2)}) collective-permute-start(f32[16,128]{1,0:T(8,128)S(1)} %add_add_fusion.refs_0_), channel_id=1, source_target_pairs={{0,12},{1,13},{2,14},{3,15},{4,8},{5,9},{6,10},{7,11},{8,4},{9,5},... | collective-permute-start | bytes 24584 | tf_op jit(solution)/shard_map/ppermute | solution.py:739
  60.6 0.3 collective-permute-start.11
  60.9 1.2 %collective-permute-start.10 = (f32[16,128]{1,0:T(8,128)S(1)}, f32[16,128]{1,0:T(8,128)S(1)}, u32[]{:S(2)}, u32[]{:S(2)}) collective-permute-start(f32[16,128]{1,0:T(8,128)S(1)} %add_add_fusion.refs_0_), channel_id=1, source_target_pairs={{0,4},{1,5},{2,6},{3,7},{4,0},{5,1},{6,2},{7,3},{8,12},{9,13},{10,... | collective-permute-start | bytes 24584 | tf_op jit(solution)/shard_map/ppermute | solution.py:739
  62.1 1.1 %collective-permute-done.12.refs_3_ = f32[16,128]{1,0:T(8,128)S(1)} collective-permute-done((f32[16,128]{1,0:T(8,128)S(1)}, f32[16,128]{1,0:T(8,128)S(1)}, u32[]{:S(2)}, u32[]{:S(2)}) %collective-permute-start.12) | collective-permute-done | bytes 8224 | tf_op jit(solution)/shard_map/ppermute | solution.py:739
  63.2 1.9 %collective-permute-done.11.refs_2_ = f32[16,128]{1,0:T(8,128)S(1)} collective-permute-done((f32[16,128]{1,0:T(8,128)S(1)}, f32[16,128]{1,0:T(8,128)S(1)}, u32[]{:S(2)}, u32[]{:S(2)}) %collective-permute-start.11) | collective-permute-done | bytes 8224 | tf_op jit(solution)/shard_map/ppermute | solution.py:739
  65.2 0.0 collective-permute-done.10.refs_1_
  65.2 7.7 %finish.1 = (f32[256,1024]{1,0:T(8,128)}, f32[256,1024]{1,0:T(8,128)}) custom-call(f32[3,64,64]{2,1,0:T(8,128)S(1)} %copy-done.2, bf16[2,4,256,256]{3,2,1,0:T(8,128)(2,1)S(1)} %get-tuple-element.29.geo_ref, bf16[3,2,4,256,256]{4,3,2,1,0:T(8,128)(2,1)S(1)} %get-tuple-element.38.basis_ref, f32[16,128]{1,0:T(8,128)S(1)} %add_add_fusion.refs_0_, ...), custom_call_target="tpu_custom_call" | custom-call | tf_op jit(solution)/shard_map/finish/pallas_call | solution.py:741
  (1 shorter events, 0.0 us)
Async XLA Ops:
  3.5 15.6 %collective-permute-start = (f32[272,128]{1,0:T(8,128)}, f32[272,128]{1,0:T(8,128)S(1)}, u32[]{:S(2)}, u32[]{:S(2)}) collective-permute-start(f32[272,128]{1,0:T(8,128)} %get-tuple-element.21), channel_id=1, source_target_pairs={{1,9},{2,10},{3,4},{4,3},{5,13},{6,14},{7,8},{8,7},{9,1},{10,2},{1... | collective-permute-start | bytes 417800 | tf_op jit(solution)/shard_map/ppermute | solution.py:666
  4.2 14.9 %collective-permute-start.1 = (f32[272,128]{1,0:T(8,128)}, f32[272,128]{1,0:T(8,128)S(1)}, u32[]{:S(2)}, u32[]{:S(2)}) collective-permute-start(f32[272,128]{1,0:T(8,128)} %get-tuple-element.22), channel_id=1, source_target_pairs={{1,9},{2,10},{3,4},{4,3},{5,13},{6,14},{7,8},{8,7},{9,1},{10,2},{1... | collective-permute-start | bytes 417800 | tf_op jit(solution)/shard_map/ppermute | solution.py:666
  4.9 18.9 %collective-permute-start.2 = (f32[272,128]{1,0:T(8,128)}, f32[272,128]{1,0:T(8,128)S(1)}, u32[]{:S(2)}, u32[]{:S(2)}) collective-permute-start(f32[272,128]{1,0:T(8,128)} %get-tuple-element.23), channel_id=1, source_target_pairs={{0,8},{1,2},{2,1},{3,11},{4,12},{5,6},{6,5},{7,15},{8,0},{9,10},{1... | collective-permute-start | bytes 417800 | tf_op jit(solution)/shard_map/ppermute | solution.py:666
  14.1 11.2 %collective-permute-start.3 = (f32[272,128]{1,0:T(8,128)}, f32[272,128]{1,0:T(8,128)S(1)}, u32[]{:S(2)}, u32[]{:S(2)}) collective-permute-start(f32[272,128]{1,0:T(8,128)} %get-tuple-element.24), channel_id=1, source_target_pairs={{0,8},{1,2},{2,1},{3,11},{4,12},{5,6},{6,5},{7,15},{8,0},{9,10},{1... | collective-permute-start | bytes 417800 | tf_op jit(solution)/shard_map/ppermute | solution.py:666
  14.2 11.1 %collective-permute-start.4 = (f32[544,128]{1,0:T(8,128)}, f32[544,128]{1,0:T(8,128)S(1)}, u32[]{:S(2)}, u32[]{:S(2)}) collective-permute-start(f32[544,128]{1,0:T(8,128)} %get-tuple-element.25), channel_id=1, source_target_pairs={{0,1},{1,0},{2,3},{3,2},{4,5},{5,4},{6,7},{7,6},{8,9},{9,8},{10,11... | collective-permute-start | bytes 835592 | tf_op jit(solution)/shard_map/ppermute | solution.py:666
  14.2 1.2 %copy-start = (f32[256,1024]{1,0:T(8,128)S(1)}, f32[256,1024]{1,0:T(8,128)}, u32[]{:S(2)}) copy-start(f32[256,1024]{1,0:T(8,128)} %loads_ref.1) | copy-start | bytes 3145732
  15.4 0.9 %copy-start.1 = (f32[3,64,64]{2,1,0:T(8,128)S(1)}, f32[3,64,64]{2,1,0:T(8,128)}, u32[]{:S(2)}) copy-start(f32[3,64,64]{2,1,0:T(8,128)} %blocks_ref.7) | copy-start | bytes 147460
  16.3 0.9 %copy-start.3 = (f32[128,256]{1,0:T(8,128)S(1)}, f32[128,256]{1,0:T(8,128)}, u32[]{:S(2)}) copy-start(f32[128,256]{1,0:T(8,128)} %get-tuple-element.26.meta_ref) | copy-start | bytes 393220
  17.2 9.9 %copy-start.2 = (f32[3,64,64]{2,1,0:T(8,128)S(1)}, f32[3,64,64]{2,1,0:T(8,128)}, u32[]{:S(2)}) copy-start(f32[3,64,64]{2,1,0:T(8,128)} %blocks_ref.7) | copy-start | bytes 147460
  26.3 10.2 %collective-permute-start.5 = (f32[96,1152]{1,0:T(8,128)S(1)}, f32[96,1152]{1,0:T(8,128)S(1)}, u32[]{:S(2)}, u32[]{:S(2)}) collective-permute-start(f32[96,1152]{1,0:T(8,128)S(1)} %get-tuple-element.30), channel_id=1, source_target_pairs={{0,1},{1,0},{2,3},{3,2},{4,5},{5,4},{6,7},{7,6},{8,9},{9,8},{10,11... | collective-permute-start | bytes 1327112 | tf_op jit(solution)/shard_map/ppermute | solution.py:698
  26.4 10.1 %collective-permute-start.6 = (f32[96,1152]{1,0:T(8,128)S(1)}, f32[96,1152]{1,0:T(8,128)S(1)}, u32[]{:S(2)}, u32[]{:S(2)}) collective-permute-start(f32[96,1152]{1,0:T(8,128)S(1)} %get-tuple-element.31), channel_id=1, source_target_pairs={{1,2},{3,4},{5,6},{7,8},{9,10},{11,12},{13,14},{2,1},{4,3},{6,5},{... | collective-permute-start | bytes 1327112 | tf_op jit(solution)/shard_map/ppermute | solution.py:697
  51.3 4.8 %collective-permute-start.9 = (f32[16,128]{1,0:T(8,128)S(1)}, f32[16,128]{1,0:T(8,128)S(1)}, u32[]{:S(2)}, u32[]{:S(2)}) collective-permute-start(f32[16,128]{1,0:T(8,128)S(1)} %get-tuple-element.39), channel_id=1, source_target_pairs={{0,3},{1,2},{2,1},{3,0},{4,7},{5,6},{6,5},{7,4},{8,11},{9,10},{10,... | collective-permute-start | bytes 24584 | tf_op jit(solution)/shard_map/ppermute | solution.py:739
  52.4 5.3 %collective-permute-start.8 = (f32[16,128]{1,0:T(8,128)S(1)}, f32[16,128]{1,0:T(8,128)S(1)}, u32[]{:S(2)}, u32[]{:S(2)}) collective-permute-start(f32[16,128]{1,0:T(8,128)S(1)} %get-tuple-element.39), channel_id=1, source_target_pairs={{0,2},{1,3},{2,0},{3,1},{4,6},{5,7},{6,4},{7,5},{8,10},{9,11},{10,... | collective-permute-start | bytes 24584 | tf_op jit(solution)/shard_map/ppermute | solution.py:739
  56.0 1.6 %collective-permute-start.7 = (f32[16,128]{1,0:T(8,128)S(1)}, f32[16,128]{1,0:T(8,128)S(1)}, u32[]{:S(2)}, u32[]{:S(2)}) collective-permute-start(f32[16,128]{1,0:T(8,128)S(1)} %get-tuple-element.39), channel_id=1, source_target_pairs={{0,1},{1,0},{2,3},{3,2},{4,5},{5,4},{6,7},{7,6},{8,9},{9,8},{10,11... | collective-permute-start | bytes 24584 | tf_op jit(solution)/shard_map/ppermute | solution.py:739
  57.7 5.5 %collective-permute-start.12 = (f32[16,128]{1,0:T(8,128)S(1)}, f32[16,128]{1,0:T(8,128)S(1)}, u32[]{:S(2)}, u32[]{:S(2)}) collective-permute-start(f32[16,128]{1,0:T(8,128)S(1)} %add_add_fusion.refs_0_), channel_id=1, source_target_pairs={{0,12},{1,13},{2,14},{3,15},{4,8},{5,9},{6,10},{7,11},{8,4},{9,5},... | collective-permute-start | bytes 24584 | tf_op jit(solution)/shard_map/ppermute | solution.py:739
  60.6 4.5 %collective-permute-start.11 = (f32[16,128]{1,0:T(8,128)S(1)}, f32[16,128]{1,0:T(8,128)S(1)}, u32[]{:S(2)}, u32[]{:S(2)}) collective-permute-start(f32[16,128]{1,0:T(8,128)S(1)} %add_add_fusion.refs_0_), channel_id=1, source_target_pairs={{0,8},{1,9},{2,10},{3,11},{4,12},{5,13},{6,14},{7,15},{8,0},{9,1},... | collective-permute-start | bytes 24584 | tf_op jit(solution)/shard_map/ppermute | solution.py:739
  60.9 4.2 %collective-permute-start.10 = (f32[16,128]{1,0:T(8,128)S(1)}, f32[16,128]{1,0:T(8,128)S(1)}, u32[]{:S(2)}, u32[]{:S(2)}) collective-permute-start(f32[16,128]{1,0:T(8,128)S(1)} %add_add_fusion.refs_0_), channel_id=1, source_target_pairs={{0,4},{1,5},{2,6},{3,7},{4,0},{5,1},{6,2},{7,3},{8,12},{9,13},{10,... | collective-permute-start | bytes 24584 | tf_op jit(solution)/shard_map/ppermute | solution.py:739

commit v7 on v5

--- a/solution.py
+++ b/solution.py
@@ -308,7 +308,11 @@
 
 
 def gathered(weights, near, fine):
-    return halves(dot(weights, jnp.concatenate([near, fine, near], axis=0)))
+    parts = [near, fine, near]
+    spare = weights.shape[1] - 3 * near.shape[0]
+    if spare:
+        parts.append(jnp.zeros((spare, near.shape[1]), BF16))
+    return halves(dot(weights, jnp.concatenate(parts, axis=0)))
 
 
 def mixed(buckets, mixer_ref, count):
@@ -324,16 +328,12 @@
     shift = basis_shift(blocks_ref[...], slots)
     inside = rows - 2 * HALO
 
-    def build(chunk, carry):
-        first = pl.multiple_of(chunk * HALO, HALO)
-        start = pl.multiple_of(chunk * HALO + HALO, HALO)
+    for first in range(0, inside, HALO):
+        start = first + HALO
         for kind, value in enumerate(
-            stencil_rows(meta_ref[pl.ds(start, HALO), :], slots, first + HALO)
+            stencil_rows(meta_ref[start:start + HALO, :], slots, first + HALO)
         ):
-            stencil[kind, pl.ds(first, HALO), :] = value
-        return carry
-
-    lax.fori_loop(0, inside // HALO, build, 0)
+            stencil[kind, first:first + HALO, :] = value
 
     def build_outer(side, chunk):
         first = chunk * HALO
@@ -391,7 +391,6 @@
     edge = ITERS * HALO
     outer = edge - HALO
     count = edge
-    rest = TILE - edge
     shift = basis_shift(blocks_ref[...], slots)
     even = lax.rem(pos_ref[0, 0], jnp.int32(2)) == 0
 
@@ -414,19 +413,20 @@
             ):
                 stencil[side, kind, first:first + HALO, :] = value
 
+    reach = count + 2 * HALO
+
     def window(step, side, part, tile):
         near = v_refs[step, side, part, tile]
-        if step == 0:
-            if side == 0:
-                return jnp.concatenate([near, field_ref[part, tile, :rest, :]], axis=0)
-            return jnp.concatenate([field_ref[part, tile, rows - rest:, :], near], axis=0)
-        blank = jnp.zeros((HALO * step, TILE), BF16)
         begin = HALO * step
         if side == 0:
-            far = inner_ref[step - 1, part, tile, begin:rest, :]
-            return jnp.concatenate([blank, near, far], axis=0)
-        far = inner_ref[step - 1, part, tile, rows - rest:rows - begin, :]
-        return jnp.concatenate([far, near, blank], axis=0)
+            block = slice(begin, begin + reach - count)
+        else:
+            block = slice(rows - begin - (reach - count), rows - begin)
+        if step == 0:
+            far = field_ref[part, tile, block, :]
+        else:
+            far = inner_ref[step - 1, part, tile, block, :]
+        return jnp.concatenate([near, far] if side == 0 else [far, near], axis=0)
 
     def weight_rows(step, side, kind):
         keep = outer - HALO * step
@@ -438,7 +438,12 @@
             pieces = [weights_ref[1, kind, keep:, :]]
             if keep:
                 pieces.append(stencil[1, kind, :keep, :])
-        return jnp.concatenate(pieces, axis=0)
+        rows_all = jnp.concatenate(pieces, axis=0)
+        first = HALO * step if side == 0 else TILE - reach - HALO * step
+        high = rows_all[:, first:first + reach]
+        low = rows_all[:, 2 * TILE + first:2 * TILE + first + reach]
+        blank = jnp.zeros((count, 2 * TILE - 3 * reach), BF16)
+        return jnp.concatenate([high, high, low, blank], axis=1)
 
     def convert(step):
         begin = HALO * step
@@ -463,9 +468,6 @@
         if step == 0:
             return jnp.concatenate([geo_ref[part, tile] for tile in range(tiles)], axis=0)
         return jnp.concatenate([basis_ref[step - 1, part, tile] for tile in range(tiles)], axis=0)
-
-    def mixed_gram(high, low):
-        return folded_rows(high[:, :TILE] + high[:, TILE:] + low, cases)
 
     def even_gram(high):
         cross = high[:, TILE:]
@@ -483,8 +485,7 @@
             for tile in range(tiles):
                 row = (side * tiles + tile) * count
                 near, fine = (window(step, side, part, tile) for part in range(2))
-                first = HALO * (step + 1) if side == 0 else TILE - HALO * (step + 1) - count
-                centres.append((near[first:first + count], fine[first:first + count]))
+                centres.append((near[HALO:HALO + count], fine[HALO:HALO + count]))
                 for part, half in enumerate(gathered(weights, near, fine)):
                     for kind in range(TYPES):
                         buckets[part, kind, row:row + count, :] = (
@@ -501,19 +502,27 @@
                     v_refs[step + 1, side, part, tile] = half
 
         convert(step + 1)
-        if step == 1:
-            others = [tall(k, part) for k in range(3) for part in range(2)]
-            high = dot_tn(tall(1, 0), jnp.concatenate(others, axis=1))
-            low = dot_tn(tall(1, 1), jnp.concatenate([others[0], others[4]], axis=1))
-            sums.append(mixed_gram(high[:, :2 * TILE], low[:, :TILE]))
-            sums.append(even_gram(high[:, 2 * TILE:4 * TILE]))
-            sums.append(mixed_gram(high[:, 4 * TILE:], low[:, TILE:]))
-        elif step == 2:
-            others = [tall(k, part) for k in range(2, 4) for part in range(2)]
-            high = dot_tn(tall(2, 0), jnp.concatenate(others, axis=1))
-            low = dot_tn(tall(2, 1), others[2])
-            sums.append(even_gram(high[:, :2 * TILE]))
-            sums.append(mixed_gram(high[:, 2 * TILE:], low))
+        if step == 0:
+            flat = [tall(1, part).T for part in range(2)]
+            left = jnp.concatenate(flat, axis=0)
+            high = dot(left, tall(0, 0))
+            fine = dot(
+                flat[0], jnp.concatenate([tall(0, 1), tall(1, 0), tall(1, 1)], axis=1)
+            )
+            sums.append(folded_rows(high[:TILE] + high[TILE:] + fine[:, :TILE], cases))
+            sums.append(even_gram(fine[:, TILE:]))
+        elif step == 1:
+            next_flat = [tall(2, part).T for part in range(2)]
+            high = dot(jnp.concatenate([flat[0], next_flat[0], flat[1]], axis=0), tall(2, 0))
+            fine = dot(jnp.concatenate([flat[0], next_flat[0]], axis=0), tall(2, 1))
+            sums.append(folded_rows(high[:TILE] + high[2 * TILE:] + fine[:TILE], cases))
+            sums.append(
+                even_gram(jnp.concatenate([high[TILE:2 * TILE], fine[TILE:]], axis=1))
+            )
+        else:
+            high = dot(jnp.concatenate(next_flat, axis=0), tall(3, 0))
+            fine = dot(next_flat[0], tall(3, 1))
+            sums.append(folded_rows(high[:TILE] + high[TILE:] + fine, cases))
 
     remainder = jnp.concatenate(sums, axis=0)
     pieces = []
@@ -745,7 +754,7 @@
 
     bits = devices.bit_length() - 1
     gathered_moments = [moments]
-    for low, high in ((0, bits // 2), (bits // 2, bits)):
+    for low, high in ((0, 1), (1, bits // 2), (bits // 2, bits)):
         partial = sum(gathered_moments[1:], gathered_moments[0])
         gathered_moments = [partial]
         for mask in range(1, 1 << (high - low)):

time: 71.8 us -> 74.3 us (1.035)
  waiting for transfers between devices: 11.8 us -> 13.3 us
  Pallas kernels: 38.8 us -> 40.1 us
    ppermute x6 -> x5, waiting for transfers between devices: 4.57 us -> 6.07 us  [on_device(): gathered_moments.append(lax.ppermute(partial, 'sub', swap))]
    pallas_call x1, Pallas kernels: 13.7 us -> 14.6 us  [on_device(): pl.pallas_call(functools.partial(sides_kernel, slots), out_shape=(basis_s...]
    ppermute x6 -> x5, starting transfers between devices: 9.24 us -> 8.8 us  [on_device(): gathered_moments.append(lax.ppermute(partial, 'sub', swap))]
  transfers between devices with their start and end apart: 11 -> 10, of which waited for: 4 -> 5; matrix products, arithmetic and copies ran while one was open for 0% -> 0% of each run, Pallas kernels for 19% -> 19%
where the time goes in v7:
time: 74.3 us; the launch traced here: 74 us
  Pallas kernels  40.1 us (54%)
  starting transfers between devices  16.7 us (22%)
  waiting for transfers between devices  13.3 us (18%)
  local copies, waits for them, and re-layouts  3.02 us (4%)
  between operations  0.93 us (1%)
    pallas_call x1, Pallas kernels, on_device(): pl.pallas_call(functools.partial(sides_kernel, slots), out_shape=(basis_s...  14.6 us
    pallas_call x1, Pallas kernels, on_device(): pl.pallas_call(functools.partial(interior_kernel, slots), out_shape=(basi...  9.78 us
    ppermute x5, starting transfers between devices, on_device(): gathered_moments.append(lax.ppermute(partial, 'sub', swap))  8.8 us
    pallas_call x1, Pallas kernels, on_device(): pl.pallas_call(functools.partial(finish_kernel, slots), out_shape=(shape(...  7.66 us
    ppermute x1, waiting for transfers between devices, on_device(): from_second = lax.ppermute(to_second, 'sub', rounds[1])  7.2 us
    ppermute x5, waiting for transfers between devices, on_device(): gathered_moments.append(lax.ppermute(partial, 'sub', swap))  6.07 us
    ppermute x1, starting transfers between devices, on_device(): from_core = lax.ppermute(to_core, 'sub', same_chip)  4.89 us
    unnamed x8, local copies, waits for them, and re-layouts  3.02 us
  transfers between devices with their start and end apart: 10, of which 5 were waited for; matrix products, arithmetic and copies ran while one was open for 0% of the time, Pallas kernels for 19%

profile of v7, /device:TPU:0, one launch (start us, length us, event | category | flops | bytes accessed | tf_op | source)
XLA Modules:
  0.0 74.0 jit_solution(10117903032752074835)
XLA Ops:
  0.6 2.4 %pack_first.1 = (f32[544,128]{1,0:T(8,128)}, f32[128,256]{1,0:T(8,128)}, s32[8,256]{1,0:T(8,128)}) custom-call(s32[1,1]{1,0:T(1,128)} %bitcast.pos_ref, f32[256,1024]{1,0:T(8,128)} %loads_hbm.3, s32[1,256]{1,0:T(1,128)} %bitcast.8, f32[12,256]{1,0:T(8,128)} %bitcast.5, s32[12,256]{1,0:T(8,128)} %bitcast.6, s32[12,256]{1,0:T(8,128)} %bitcast.7), custom_call_target="tpu_custom_call" | custom-call | tf_op jit(solution)/shard_map/pack_first/pallas_call | solution.py:656
  3.1 0.7 collective-permute-start.1
  3.8 2.6 %pack_second.1 = (f32[544,128]{1,0:T(8,128)}, f32[544,128]{1,0:T(8,128)}) custom-call(s32[1,1]{1,0:T(1,128)} %bitcast.pos_ref, s32[8,256]{1,0:T(8,128)} %get-tuple-element.23.target_hbm, f32[128,256]{1,0:T(8,128)} %get-tuple-element.20.meta_ref.meta_hbm, f32[256,1024]{1,0:T(8,128)} %loads_hbm.3), custom_call_target="tpu_custom_call" | custom-call | tf_op jit(solution)/shard_map/pack_second/pallas_call | solution.py:674
  6.4 4.9 %collective-permute-start = (f32[544,128]{1,0:T(8,128)}, f32[544,128]{1,0:T(8,128)S(1)}, u32[]{:S(2)}, u32[]{:S(2)}) collective-permute-start(f32[544,128]{1,0:T(8,128)} %get-tuple-element.24), channel_id=1, source_target_pairs={{0,1},{1,0},{2,3},{3,2},{4,5},{5,4},{6,7},{7,6},{8,9},{9,8},{10,11... | collective-permute-start | bytes 835592 | tf_op jit(solution)/shard_map/ppermute | solution.py:689
  11.3 1.4 %collective-permute-start.2 = (f32[544,128]{1,0:T(8,128)}, f32[544,128]{1,0:T(8,128)S(1)}, u32[]{:S(2)}, u32[]{:S(2)}) collective-permute-start(f32[544,128]{1,0:T(8,128)} %get-tuple-element.26), channel_id=1, source_target_pairs={{0,8},{1,2},{2,1},{3,11},{4,12},{5,6},{6,5},{7,15},{8,0},{9,10},{1... | collective-permute-start | bytes 835592 | tf_op jit(solution)/shard_map/ppermute | solution.py:688
  12.7 0.0 copy-start
  12.7 1.2 %copy-done = f32[256,1024]{1,0:T(8,128)S(1)} copy-done((f32[256,1024]{1,0:T(8,128)S(1)}, f32[256,1024]{1,0:T(8,128)}, u32[]{:S(2)}) %copy-start) | copy-done | bytes 1048600
  13.9 0.0 copy-start.1
  13.9 0.9 %copy-done.1 = f32[3,64,64]{2,1,0:T(8,128)S(1)} copy-done((f32[3,64,64]{2,1,0:T(8,128)S(1)}, f32[3,64,64]{2,1,0:T(8,128)}, u32[]{:S(2)}) %copy-start.1) | copy-done | bytes 49176
  14.8 0.0 copy-start.3
  14.8 0.9 %copy-done.3 = f32[128,256]{1,0:T(8,128)S(1)} copy-done((f32[128,256]{1,0:T(8,128)S(1)}, f32[128,256]{1,0:T(8,128)}, u32[]{:S(2)}) %copy-start.3) | copy-done | bytes 131096
  15.7 0.0 copy-start.2
  15.7 1.9 %prepare.1 = (f32[256,1024]{1,0:T(8,128)S(1)}, f32[256,128]{1,0:T(8,128)S(1)}, bf16[2304,256]{1,0:T(8,128)(2,1)S(1)}, f32[16,256]{1,0:T(8,128)S(1)}) custom-call(f32[256,1024]{1,0:T(8,128)S(1)} %copy-done, f32[128,256]{1,0:T(8,128)S(1)} %copy-done.3, f32[3,64,64]{2,1,0:T(8,128)S(1)} %copy-done.1), custom_call_target="tpu_custom_call" | custom-call | flops 4000000000 | bytes 4000000 | tf_op jit(solution)/shard_map/prepare/pallas_call | solution.py:692
  17.6 0.0 collective-permute-done.1.first_ref
  17.6 0.0 collective-permute-done.core_ref
  17.6 7.2 %collective-permute-done.2.second_ref = f32[544,128]{1,0:T(8,128)S(1)} collective-permute-done((f32[544,128]{1,0:T(8,128)}, f32[544,128]{1,0:T(8,128)S(1)}, u32[]{:S(2)}, u32[]{:S(2)}) %collective-permute-start.2) | collective-permute-done | bytes 278560 | tf_op jit(solution)/shard_map/ppermute | solution.py:688
  24.8 1.1 %arrange.1 = (bf16[2,4,256,256]{3,2,1,0:T(8,128)(2,1)S(1)}, bf16[2,4,256,256]{3,2,1,0:T(8,128)(2,1)S(1)}, f32[256,128]{1,0:T(8,128)S(1)}, f32[96,1152]{1,0:T(8,128)S(1)}, f32[96,1152]{1,0:T(8,128)S(1)}) custom-call(s32[1,1]{1,0:T(1,128)} %bitcast.pos_ref, f32[256,1024]{1,0:T(8,128)S(1)} %get-tuple-element.21.kept_ref, ...), custom_call_target="tpu_custom_call" | custom-call | tf_op jit(solution)/shard_map/arrange/pallas_call | solution.py:711
  25.9 0.1 collective-permute-start.3
  26.0 0.9 %collective-permute-start.4 = (f32[96,1152]{1,0:T(8,128)S(1)}, f32[96,1152]{1,0:T(8,128)S(1)}, u32[]{:S(2)}, u32[]{:S(2)}) collective-permute-start(f32[96,1152]{1,0:T(8,128)S(1)} %get-tuple-element.29), channel_id=1, source_target_pairs={{1,2},{3,4},{5,6},{7,8},{9,10},{11,12},{13,14},{2,1},{4,3},{6,5},{... | collective-permute-start | bytes 1327112 | tf_op jit(solution)/shard_map/ppermute | solution.py:720
  26.8 0.0 copy-done.2
  26.9 9.8 %interior.1 = (bf16[3,2,4,256,256]{4,3,2,1,0:T(8,128)(2,1)S(1)}, bf16[2,3,96,768]{3,2,1,0:T(8,128)(2,1)S(1)}) custom-call(bf16[2,4,256,256]{3,2,1,0:T(8,128)(2,1)S(1)} %get-tuple-element.30.field_ref, f32[256,128]{1,0:T(8,128)S(1)} %get-tuple-element.31.meta_ref, bf16[2304,256]{1,0:T(8,128)(2,1)S(1)} %get-tuple-element.32.mixer_ref, f32[3,64,64]{2,1,0:T(8,128)S(1)} %copy-done.2), custom_call_target="tpu_custom_call" | custom-call | flops 10000000000 | bytes 8000000 | tf_op jit(solution)/shard_map/interior/pallas_call | solution.py:724
  36.6 0.0 collective-permute-done.3.core_ref
  36.7 0.0 collective-permute-done.4.chip_ref
  36.7 14.6 %sides.1 = (bf16[3,2,4,256,256]{4,3,2,1,0:T(8,128)(2,1)S(1)}, f32[16,128]{1,0:T(8,128)S(1)}) custom-call(s32[1,1]{1,0:T(1,128)} %bitcast.pos_ref, f32[96,1152]{1,0:T(8,128)S(1)} %collective-permute-done.3.core_ref, f32[96,1152]{1,0:T(8,128)S(1)} %collective-permute-done.4.chip_ref, bf16[2,4,256,256]{3,2,1,0:T(8,128)(2,1)S(1)} %get-tuple-element.30.field_ref, ...), custom_call_target="tpu_custom_call" | custom-call | tf_op jit(solution)/shard_map/sides/pallas_call | solution.py:740
  51.3 1.8 %collective-permute-start.5 = (f32[16,128]{1,0:T(8,128)S(1)}, f32[16,128]{1,0:T(8,128)S(1)}, u32[]{:S(2)}, u32[]{:S(2)}) collective-permute-start(f32[16,128]{1,0:T(8,128)S(1)} %get-tuple-element.37), channel_id=1, source_target_pairs={{0,1},{1,0},{2,3},{3,2},{4,5},{5,4},{6,7},{7,6},{8,9},{9,8},{10,11... | collective-permute-start | bytes 24584 | tf_op jit(solution)/shard_map/ppermute | solution.py:762
  53.1 0.8 %collective-permute-done.5 = f32[16,128]{1,0:T(8,128)S(1)} collective-permute-done((f32[16,128]{1,0:T(8,128)S(1)}, f32[16,128]{1,0:T(8,128)S(1)}, u32[]{:S(2)}, u32[]{:S(2)}) %collective-permute-start.5) | collective-permute-done | bytes 8224 | tf_op jit(solution)/shard_map/ppermute | solution.py:762
  53.9 2.6 %collective-permute-start.6 = (f32[16,128]{1,0:T(8,128)S(1)}, f32[16,128]{1,0:T(8,128)S(1)}, u32[]{:S(2)}, u32[]{:S(2)}) collective-permute-start(f32[16,128]{1,0:T(8,128)S(1)} %add.6), channel_id=1, source_target_pairs={{0,2},{1,3},{2,0},{3,1},{4,6},{5,7},{6,4},{7,5},{8,10},{9,11},{10,... | collective-permute-start | bytes 24584 | tf_op jit(solution)/shard_map/ppermute | solution.py:762
  56.5 1.6 %collective-permute-done.6 = f32[16,128]{1,0:T(8,128)S(1)} collective-permute-done((f32[16,128]{1,0:T(8,128)S(1)}, f32[16,128]{1,0:T(8,128)S(1)}, u32[]{:S(2)}, u32[]{:S(2)}) %collective-permute-start.6) | collective-permute-done | bytes 8224 | tf_op jit(solution)/shard_map/ppermute | solution.py:762
  58.2 3.4 %collective-permute-start.9 = (f32[16,128]{1,0:T(8,128)S(1)}, f32[16,128]{1,0:T(8,128)S(1)}, u32[]{:S(2)}, u32[]{:S(2)}) collective-permute-start(f32[16,128]{1,0:T(8,128)S(1)} %add.7.refs_0_), channel_id=1, source_target_pairs={{0,12},{1,13},{2,14},{3,15},{4,8},{5,9},{6,10},{7,11},{8,4},{9,5},... | collective-permute-start | bytes 24584 | tf_op jit(solution)/shard_map/ppermute | solution.py:762
  61.6 0.0 collective-permute-start.8
  61.6 0.9 %collective-permute-start.7 = (f32[16,128]{1,0:T(8,128)S(1)}, f32[16,128]{1,0:T(8,128)S(1)}, u32[]{:S(2)}, u32[]{:S(2)}) collective-permute-start(f32[16,128]{1,0:T(8,128)S(1)} %add.7.refs_0_), channel_id=1, source_target_pairs={{0,4},{1,5},{2,6},{3,7},{4,0},{5,1},{6,2},{7,3},{8,12},{9,13},{10,... | collective-permute-start | bytes 24584 | tf_op jit(solution)/shard_map/ppermute | solution.py:762
  62.6 1.1 %collective-permute-done.9.refs_3_ = f32[16,128]{1,0:T(8,128)S(1)} collective-permute-done((f32[16,128]{1,0:T(8,128)S(1)}, f32[16,128]{1,0:T(8,128)S(1)}, u32[]{:S(2)}, u32[]{:S(2)}) %collective-permute-start.9) | collective-permute-done | bytes 8224 | tf_op jit(solution)/shard_map/ppermute | solution.py:762
  63.6 2.5 %collective-permute-done.8.refs_2_ = f32[16,128]{1,0:T(8,128)S(1)} collective-permute-done((f32[16,128]{1,0:T(8,128)S(1)}, f32[16,128]{1,0:T(8,128)S(1)}, u32[]{:S(2)}, u32[]{:S(2)}) %collective-permute-start.8) | collective-permute-done | bytes 8224 | tf_op jit(solution)/shard_map/ppermute | solution.py:762
  66.2 0.0 collective-permute-done.7.refs_1_
  66.2 7.7 %finish.1 = (f32[256,1024]{1,0:T(8,128)}, f32[256,1024]{1,0:T(8,128)}) custom-call(f32[3,64,64]{2,1,0:T(8,128)S(1)} %copy-done.2, bf16[2,4,256,256]{3,2,1,0:T(8,128)(2,1)S(1)} %get-tuple-element.27.geo_ref, bf16[3,2,4,256,256]{4,3,2,1,0:T(8,128)(2,1)S(1)} %get-tuple-element.36.basis_ref, f32[16,128]{1,0:T(8,128)S(1)} %add.7.refs_0_, ...), custom_call_target="tpu_custom_call" | custom-call | tf_op jit(solution)/shard_map/finish/pallas_call | solution.py:764
  (2 shorter events, 0.0 us)
Async XLA Ops:
  3.1 14.5 %collective-permute-start.1 = (f32[544,128]{1,0:T(8,128)}, f32[544,128]{1,0:T(8,128)S(1)}, u32[]{:S(2)}, u32[]{:S(2)}) collective-permute-start(f32[544,128]{1,0:T(8,128)} %get-tuple-element.25), channel_id=1, source_target_pairs={{1,9},{2,10},{3,4},{4,3},{5,13},{6,14},{7,8},{8,7},{9,1},{10,2},{1... | collective-permute-start | bytes 835592 | tf_op jit(solution)/shard_map/ppermute | solution.py:672
  6.4 11.2 %collective-permute-start = (f32[544,128]{1,0:T(8,128)}, f32[544,128]{1,0:T(8,128)S(1)}, u32[]{:S(2)}, u32[]{:S(2)}) collective-permute-start(f32[544,128]{1,0:T(8,128)} %get-tuple-element.24), channel_id=1, source_target_pairs={{0,1},{1,0},{2,3},{3,2},{4,5},{5,4},{6,7},{7,6},{8,9},{9,8},{10,11... | collective-permute-start | bytes 835592 | tf_op jit(solution)/shard_map/ppermute | solution.py:689
  11.3 13.5 %collective-permute-start.2 = (f32[544,128]{1,0:T(8,128)}, f32[544,128]{1,0:T(8,128)S(1)}, u32[]{:S(2)}, u32[]{:S(2)}) collective-permute-start(f32[544,128]{1,0:T(8,128)} %get-tuple-element.26), channel_id=1, source_target_pairs={{0,8},{1,2},{2,1},{3,11},{4,12},{5,6},{6,5},{7,15},{8,0},{9,10},{1... | collective-permute-start | bytes 835592 | tf_op jit(solution)/shard_map/ppermute | solution.py:688
  12.7 1.2 %copy-start = (f32[256,1024]{1,0:T(8,128)S(1)}, f32[256,1024]{1,0:T(8,128)}, u32[]{:S(2)}) copy-start(f32[256,1024]{1,0:T(8,128)} %loads_hbm.3) | copy-start | bytes 3145732
  13.9 0.9 %copy-start.1 = (f32[3,64,64]{2,1,0:T(8,128)S(1)}, f32[3,64,64]{2,1,0:T(8,128)}, u32[]{:S(2)}) copy-start(f32[3,64,64]{2,1,0:T(8,128)} %blocks_ref.7) | copy-start | bytes 147460
  14.8 0.9 %copy-start.3 = (f32[128,256]{1,0:T(8,128)S(1)}, f32[128,256]{1,0:T(8,128)}, u32[]{:S(2)}) copy-start(f32[128,256]{1,0:T(8,128)} %get-tuple-element.20.meta_ref.meta_hbm) | copy-start | bytes 393220
  15.7 11.2 %copy-start.2 = (f32[3,64,64]{2,1,0:T(8,128)S(1)}, f32[3,64,64]{2,1,0:T(8,128)}, u32[]{:S(2)}) copy-start(f32[3,64,64]{2,1,0:T(8,128)} %blocks_ref.7) | copy-start | bytes 147460
  25.9 10.8 %collective-permute-start.3 = (f32[96,1152]{1,0:T(8,128)S(1)}, f32[96,1152]{1,0:T(8,128)S(1)}, u32[]{:S(2)}, u32[]{:S(2)}) collective-permute-start(f32[96,1152]{1,0:T(8,128)S(1)} %get-tuple-element.28), channel_id=1, source_target_pairs={{0,1},{1,0},{2,3},{3,2},{4,5},{5,4},{6,7},{7,6},{8,9},{9,8},{10,11... | collective-permute-start | bytes 1327112 | tf_op jit(solution)/shard_map/ppermute | solution.py:721
  26.0 10.7 %collective-permute-start.4 = (f32[96,1152]{1,0:T(8,128)S(1)}, f32[96,1152]{1,0:T(8,128)S(1)}, u32[]{:S(2)}, u32[]{:S(2)}) collective-permute-start(f32[96,1152]{1,0:T(8,128)S(1)} %get-tuple-element.29), channel_id=1, source_target_pairs={{1,2},{3,4},{5,6},{7,8},{9,10},{11,12},{13,14},{2,1},{4,3},{6,5},{... | collective-permute-start | bytes 1327112 | tf_op jit(solution)/shard_map/ppermute | solution.py:720
  51.3 2.6 %collective-permute-start.5 = (f32[16,128]{1,0:T(8,128)S(1)}, f32[16,128]{1,0:T(8,128)S(1)}, u32[]{:S(2)}, u32[]{:S(2)}) collective-permute-start(f32[16,128]{1,0:T(8,128)S(1)} %get-tuple-element.37), channel_id=1, source_target_pairs={{0,1},{1,0},{2,3},{3,2},{4,5},{5,4},{6,7},{7,6},{8,9},{9,8},{10,11... | collective-permute-start | bytes 24584 | tf_op jit(solution)/shard_map/ppermute | solution.py:762
  53.9 4.3 %collective-permute-start.6 = (f32[16,128]{1,0:T(8,128)S(1)}, f32[16,128]{1,0:T(8,128)S(1)}, u32[]{:S(2)}, u32[]{:S(2)}) collective-permute-start(f32[16,128]{1,0:T(8,128)S(1)} %add.6), channel_id=1, source_target_pairs={{0,2},{1,3},{2,0},{3,1},{4,6},{5,7},{6,4},{7,5},{8,10},{9,11},{10,... | collective-permute-start | bytes 24584 | tf_op jit(solution)/shard_map/ppermute | solution.py:762
  58.2 5.4 %collective-permute-start.9 = (f32[16,128]{1,0:T(8,128)S(1)}, f32[16,128]{1,0:T(8,128)S(1)}, u32[]{:S(2)}, u32[]{:S(2)}) collective-permute-start(f32[16,128]{1,0:T(8,128)S(1)} %add.7.refs_0_), channel_id=1, source_target_pairs={{0,12},{1,13},{2,14},{3,15},{4,8},{5,9},{6,10},{7,11},{8,4},{9,5},... | collective-permute-start | bytes 24584 | tf_op jit(solution)/shard_map/ppermute | solution.py:762
  61.6 4.5 %collective-permute-start.8 = (f32[16,128]{1,0:T(8,128)S(1)}, f32[16,128]{1,0:T(8,128)S(1)}, u32[]{:S(2)}, u32[]{:S(2)}) collective-permute-start(f32[16,128]{1,0:T(8,128)S(1)} %add.7.refs_0_), channel_id=1, source_target_pairs={{0,8},{1,9},{2,10},{3,11},{4,12},{5,13},{6,14},{7,15},{8,0},{9,1},... | collective-permute-start | bytes 24584 | tf_op jit(solution)/shard_map/ppermute | solution.py:762
  61.6 4.5 %collective-permute-start.7 = (f32[16,128]{1,0:T(8,128)S(1)}, f32[16,128]{1,0:T(8,128)S(1)}, u32[]{:S(2)}, u32[]{:S(2)}) collective-permute-start(f32[16,128]{1,0:T(8,128)S(1)} %add.7.refs_0_), channel_id=1, source_target_pairs={{0,4},{1,5},{2,6},{3,7},{4,0},{5,1},{6,2},{7,3},{8,12},{9,13},{10,... | collective-permute-start | bytes 24584 | tf_op jit(solution)/shard_map/ppermute | solution.py:762

commit v8 on v5

--- a/solution.py
+++ b/solution.py
@@ -246,13 +246,13 @@
                 mixer_ref[start:start + TILE, :] = wide
 
 
-def arrange_kernel(slots, pos_ref, kept_ref, kept_meta_ref, core_ref, first_ref, second_ref,
+def arrange_kernel(slots, pos_ref, first_ref, second_ref, core_ref, kept_ref, kept_meta_ref,
                    geo_ref, field_ref, meta_ref, to_core_ref, to_chip_ref):
     rows, width = kept_ref.shape
     tiles = width // TILE
     edge = to_core_ref.shape[0]
     even = lax.rem(pos_ref[0, 0], jnp.int32(2)) == 0
-    blocks = [read_block(ref, width) for ref in (core_ref, first_ref, second_ref)]
+    blocks = [read_block(ref, width) for ref in (first_ref, second_ref, core_ref)]
     arrived = jnp.concatenate([block[0] for block in blocks], axis=0)
     arrived_meta = jnp.concatenate([block[1] for block in blocks], axis=0)
     count = arrived.shape[0]
@@ -527,7 +527,8 @@
     for number in range(2 * ITERS):
         part = folded[number * cases:(number + 1) * cases]
         moments = jnp.where(group == number, part, moments)
-    moments_ref[...] = moments
+    for device in range(moments_ref.shape[0]):
+        moments_ref[device] = moments
 
 
 def refined_reciprocal(value):
@@ -537,17 +538,16 @@
     return guess
 
 
-def finish_kernel(slots, blocks_ref, geo_ref, basis_ref, *refs):
-    moment_refs = refs[:-4]
-    solution_hbm, residual_hbm, out_refs, sems = refs[-4:]
+def finish_kernel(slots, moments_ref, blocks_ref, geo_ref, basis_ref,
+                  solution_hbm, residual_hbm, out_refs, sems):
     rows, width = out_refs.shape[1:]
     dof = blocks_ref.shape[1]
     cases = width // dof
     tiles = width // TILE
     shift = basis_shift(blocks_ref[...], slots)
-    moments = moment_refs[0][...]
-    for ref in moment_refs[1:]:
-        moments = moments + ref[...]
+    moments = moments_ref[0]
+    for device in range(1, moments_ref.shape[0]):
+        moments = moments + moments_ref[device]
     group = iota((cases, META), 1) // cases
     system = []
     for row in range(ITERS):
@@ -706,7 +706,7 @@
         out_specs=(VMEM,) * 5,
         compiler_params=PARAMS,
         name="arrange",
-    )(position, kept, kept_meta, from_core, from_first, from_second)
+    )(position, from_first, from_second, from_core, kept, kept_meta)
 
     halo_chip = lax.ppermute(to_chip, "sub", next_chip)
     halo_core = lax.ppermute(to_core, "sub", same_chip)
@@ -730,7 +730,7 @@
 
     basis, moments = pl.pallas_call(
         functools.partial(sides_kernel, slots),
-        out_shape=(basis_shape, shape((cases, META), F32)),
+        out_shape=(basis_shape, shape((devices, cases, META), F32)),
         in_specs=[SMEM] + [VMEM] * 9,
         out_specs=(VMEM,) * 2,
         scratch_shapes=[
@@ -743,24 +743,17 @@
         name="sides",
     )(position, halo_core, halo_chip, field, inner, weights, mixer, ref_blocks, geo, first)
 
-    bits = devices.bit_length() - 1
-    gathered_moments = [moments]
-    for low, high in ((0, bits // 2), (bits // 2, bits)):
-        partial = sum(gathered_moments[1:], gathered_moments[0])
-        gathered_moments = [partial]
-        for mask in range(1, 1 << (high - low)):
-            swap = [(i, i ^ (mask << low)) for i in range(devices)]
-            gathered_moments.append(lax.ppermute(partial, "sub", swap))
+    moments = lax.all_to_all(moments, "sub", split_axis=0, concat_axis=0, tiled=True)
 
     return pl.pallas_call(
         functools.partial(finish_kernel, slots),
         out_shape=(shape((rows, width), F32), shape((rows, width), F32)),
-        in_specs=[VMEM] * (3 + len(gathered_moments)),
+        in_specs=[VMEM] * 4,
         out_specs=(HBM,) * 2,
         scratch_shapes=[pltpu.VMEM((2, rows, width), F32), pltpu.SemaphoreType.DMA((2,))],
         compiler_params=PARAMS,
         name="finish",
-    )(ref_blocks, geo, basis, *gathered_moments)
+    )(moments, ref_blocks, geo, basis)
 
 
 def solution(mesh):

time: 71.8 us -> 72.7 us (1.013)
  blocking collectives: 0 us -> 14.8 us
  starting transfers between devices: 16.9 us -> 8.41 us
  waiting for transfers between devices: 11.8 us -> 6.51 us
    all_to_all x0 -> x1, blocking collectives: none -> 14.8 us  [on_device(): lax.all_to_all(moments, 'sub', split_axis=0, concat_axis=0, tiled=True)]
    ppermute x6 -> x0, starting transfers between devices: 9.24 us -> none  [on_device(): gathered_moments.append(lax.ppermute(partial, 'sub', swap))]
    ppermute x1, starting transfers between devices: 1.37 us -> 6.18 us  [on_device(): from_second = lax.ppermute(to_second, 'sub', rounds[1])]
    ppermute x6 -> x0, waiting for transfers between devices: 4.57 us -> none  [on_device(): gathered_moments.append(lax.ppermute(partial, 'sub', swap))]
    ppermute x1, starting transfers between devices: 4.89 us -> 0.79 us  [on_device(): from_core = lax.ppermute(to_core, 'sub', same_chip)]
  transfers between devices with their start and end apart: 11 -> 5, of which waited for: 4 -> 1; matrix products, arithmetic and copies ran while one was open for 0% -> 0% of each run, Pallas kernels for 19% -> 19%
where the time goes in v8:
time: 72.7 us; the launch traced here: 72.4 us
  Pallas kernels  38.7 us (53%)
  blocking collectives  14.8 us (20%)
  starting transfers between devices  8.41 us (12%)
  waiting for transfers between devices  6.51 us (9%)
  local copies, waits for them, and re-layouts  3.02 us (4%)
  between operations  0.92 us (1%)
    all_to_all x1, blocking collectives, on_device(): lax.all_to_all(moments, 'sub', split_axis=0, concat_axis=0, tiled=True)  14.8 us
    pallas_call x1, Pallas kernels, on_device(): pl.pallas_call(functools.partial(sides_kernel, slots), out_shape=(basis_s...  13.7 us
    pallas_call x1, Pallas kernels, on_device(): pl.pallas_call(functools.partial(interior_kernel, slots), out_shape=(basi...  9.39 us
    pallas_call x1, Pallas kernels, on_device(): pl.pallas_call(functools.partial(finish_kernel, slots), out_shape=(shape(...  7.64 us
    ppermute x1, waiting for transfers between devices, on_device(): from_second = lax.ppermute(to_second, 'sub', rounds[1])  6.5 us
    ppermute x1, starting transfers between devices, on_device(): from_second = lax.ppermute(to_second, 'sub', rounds[1])  6.18 us
    unnamed x8, local copies, waits for them, and re-layouts  3.02 us
    pallas_call x1, Pallas kernels, on_device(): pl.pallas_call(functools.partial(pack_second_kernel, devices), out_shape=...  2.63 us
  transfers between devices with their start and end apart: 5, of which 1 were waited for; matrix products, arithmetic and copies ran while one was open for 0% of the time, Pallas kernels for 19%

profile of v8, /device:TPU:0, one launch (start us, length us, event | category | flops | bytes accessed | tf_op | source)
XLA Modules:
  0.0 72.4 jit_solution(2515221620334906257)
XLA Ops:
  0.6 2.4 %pack_first.1 = (f32[544,128]{1,0:T(8,128)}, f32[128,256]{1,0:T(8,128)}, s32[8,256]{1,0:T(8,128)}) custom-call(s32[1,1]{1,0:T(1,128)} %bitcast.pos_ref, f32[256,1024]{1,0:T(8,128)} %loads_ref.1, s32[1,256]{1,0:T(1,128)} %bitcast.8, f32[12,256]{1,0:T(8,128)} %bitcast.5, s32[12,256]{1,0:T(8,128)} %bitcast.6, s32[12,256]{1,0:T(8,128)} %bitcast.7), custom_call_target="tpu_custom_call" | custom-call | tf_op jit(solution)/shard_map/pack_first/pallas_call | solution.py:647
  3.1 0.7 collective-permute-start
  3.8 2.6 %pack_second.1 = (f32[544,128]{1,0:T(8,128)}, f32[544,128]{1,0:T(8,128)}) custom-call(s32[1,1]{1,0:T(1,128)} %bitcast.pos_ref, s32[8,256]{1,0:T(8,128)} %get-tuple-element.21.target_hbm, f32[128,256]{1,0:T(8,128)} %get-tuple-element.22.meta_hbm.meta_ref, f32[256,1024]{1,0:T(8,128)} %loads_ref.1), custom_call_target="tpu_custom_call" | custom-call | tf_op jit(solution)/shard_map/pack_second/pallas_call | solution.py:665
  6.4 6.2 %collective-permute-start.1 = (f32[544,128]{1,0:T(8,128)}, f32[544,128]{1,0:T(8,128)S(1)}, u32[]{:S(2)}, u32[]{:S(2)}) collective-permute-start(f32[544,128]{1,0:T(8,128)} %get-tuple-element.23), channel_id=1, source_target_pairs={{0,8},{1,2},{2,1},{3,11},{4,12},{5,6},{6,5},{7,15},{8,0},{9,10},{1... | collective-permute-start | bytes 835592 | tf_op jit(solution)/shard_map/ppermute | solution.py:679
  12.6 0.8 %collective-permute-start.2 = (f32[544,128]{1,0:T(8,128)}, f32[544,128]{1,0:T(8,128)S(1)}, u32[]{:S(2)}, u32[]{:S(2)}) collective-permute-start(f32[544,128]{1,0:T(8,128)} %get-tuple-element.24), channel_id=1, source_target_pairs={{0,1},{1,0},{2,3},{3,2},{4,5},{5,4},{6,7},{7,6},{8,9},{9,8},{10,11... | collective-permute-start | bytes 835592 | tf_op jit(solution)/shard_map/ppermute | solution.py:680
  13.4 0.0 copy-start
  13.4 1.2 %copy-done = f32[256,1024]{1,0:T(8,128)S(1)} copy-done((f32[256,1024]{1,0:T(8,128)S(1)}, f32[256,1024]{1,0:T(8,128)}, u32[]{:S(2)}) %copy-start) | copy-done | bytes 1048600
  14.6 0.0 copy-start.1
  14.6 0.9 %copy-done.1 = f32[3,64,64]{2,1,0:T(8,128)S(1)} copy-done((f32[3,64,64]{2,1,0:T(8,128)S(1)}, f32[3,64,64]{2,1,0:T(8,128)}, u32[]{:S(2)}) %copy-start.1) | copy-done | bytes 49176
  15.5 0.0 copy-start.3
  15.5 0.9 %copy-done.3 = f32[128,256]{1,0:T(8,128)S(1)} copy-done((f32[128,256]{1,0:T(8,128)S(1)}, f32[128,256]{1,0:T(8,128)}, u32[]{:S(2)}) %copy-start.3) | copy-done | bytes 131096
  16.4 0.0 copy-start.2
  16.4 1.9 %prepare.1 = (f32[256,1024]{1,0:T(8,128)S(1)}, f32[256,128]{1,0:T(8,128)S(1)}, bf16[2304,256]{1,0:T(8,128)(2,1)S(1)}, f32[16,256]{1,0:T(8,128)S(1)}) custom-call(f32[256,1024]{1,0:T(8,128)S(1)} %copy-done, f32[128,256]{1,0:T(8,128)S(1)} %copy-done.3, f32[3,64,64]{2,1,0:T(8,128)S(1)} %copy-done.1), custom_call_target="tpu_custom_call" | custom-call | flops 4000000000 | bytes 4000000 | tf_op jit(solution)/shard_map/prepare/pallas_call | solution.py:683
  18.3 0.0 collective-permute-done.first_ref
  18.3 6.5 %collective-permute-done.1.second_ref = f32[544,128]{1,0:T(8,128)S(1)} collective-permute-done((f32[544,128]{1,0:T(8,128)}, f32[544,128]{1,0:T(8,128)S(1)}, u32[]{:S(2)}, u32[]{:S(2)}) %collective-permute-start.1) | collective-permute-done | bytes 278560 | tf_op jit(solution)/shard_map/ppermute | solution.py:679
  24.8 0.0 collective-permute-done.2.core_ref
  24.8 1.1 %arrange.1 = (bf16[2,4,256,256]{3,2,1,0:T(8,128)(2,1)S(1)}, bf16[2,4,256,256]{3,2,1,0:T(8,128)(2,1)S(1)}, f32[256,128]{1,0:T(8,128)S(1)}, f32[96,1152]{1,0:T(8,128)S(1)}, f32[96,1152]{1,0:T(8,128)S(1)}) custom-call(s32[1,1]{1,0:T(1,128)} %bitcast.pos_ref, f32[544,128]{1,0:T(8,128)S(1)} %collective-permute-done.first_ref, ...), custom_call_target="tpu_custom_call" | custom-call | tf_op jit(solution)/shard_map/arrange/pallas_call | solution.py:702
  25.9 0.1 collective-permute-start.3
  26.0 0.7 collective-permute-start.4
  26.7 0.0 copy-done.2
  26.7 9.4 %interior.1 = (bf16[3,2,4,256,256]{4,3,2,1,0:T(8,128)(2,1)S(1)}, bf16[2,3,96,768]{3,2,1,0:T(8,128)(2,1)S(1)}) custom-call(bf16[2,4,256,256]{3,2,1,0:T(8,128)(2,1)S(1)} %get-tuple-element.29.field_ref, f32[256,128]{1,0:T(8,128)S(1)} %get-tuple-element.30.meta_ref, bf16[2304,256]{1,0:T(8,128)(2,1)S(1)} %get-tuple-element.31.mixer_ref, f32[3,64,64]{2,1,0:T(8,128)S(1)} %copy-done.2), custom_call_target="tpu_custom_call" | custom-call | flops 10000000000 | bytes 8000000 | tf_op jit(solution)/shard_map/interior/pallas_call | solution.py:715
  36.1 0.0 collective-permute-done.3.core_ref
  36.1 0.0 collective-permute-done.4.chip_ref
  36.1 13.7 %sides.1 = (bf16[3,2,4,256,256]{4,3,2,1,0:T(8,128)(2,1)S(1)}, f32[16,16,128]{2,1,0:T(8,128)S(1)}) custom-call(s32[1,1]{1,0:T(1,128)} %bitcast.pos_ref, f32[96,1152]{1,0:T(8,128)S(1)} %collective-permute-done.3.core_ref, f32[96,1152]{1,0:T(8,128)S(1)} %collective-permute-done.4.chip_ref, bf16[2,4,256,256]{3,2,1,0:T(8,128)(2,1)S(1)} %get-tuple-element.29.field_ref, ...), custom_call_target="tpu_custom_call" | custom-call | tf_op jit(solution)/shard_map/sides/pallas_call | solution.py:731
  49.8 14.8 %all_to_all.5.moments_ref = f32[16,16,128]{2,1,0:T(8,128)S(1)} all-to-all(f32[16,16,128]{2,1,0:T(8,128)S(1)} %get-tuple-element.36), channel_id=1, replica_groups=mesh['groups'=2,'sub'=16] {'sub'}, dimensions={0} | all-to-all | bytes 262144 | tf_op jit(solution)/shard_map/all_to_all | solution.py:746
  64.6 7.6 %finish.1 = (f32[256,1024]{1,0:T(8,128)}, f32[256,1024]{1,0:T(8,128)}) custom-call(f32[16,16,128]{2,1,0:T(8,128)S(1)} %all_to_all.5.moments_ref, f32[3,64,64]{2,1,0:T(8,128)S(1)} %copy-done.2, bf16[2,4,256,256]{3,2,1,0:T(8,128)(2,1)S(1)} %get-tuple-element.34.geo_ref, bf16[3,2,4,256,256]{4,3,2,1,0:T(8,128)(2,1)S(1)} %get-tuple-element.37.basis_ref), custom_call_target="tpu_custom_call" | custom-call | tf_op jit(solution)/shard_map/finish/pallas_call | solution.py:748
Async XLA Ops:
  3.1 15.2 %collective-permute-start = (f32[544,128]{1,0:T(8,128)}, f32[544,128]{1,0:T(8,128)S(1)}, u32[]{:S(2)}, u32[]{:S(2)}) collective-permute-start(f32[544,128]{1,0:T(8,128)} %get-tuple-element.20), channel_id=1, source_target_pairs={{1,9},{2,10},{3,4},{4,3},{5,13},{6,14},{7,8},{8,7},{9,1},{10,2},{1... | collective-permute-start | bytes 835592 | tf_op jit(solution)/shard_map/ppermute | solution.py:663
  6.4 18.4 %collective-permute-start.1 = (f32[544,128]{1,0:T(8,128)}, f32[544,128]{1,0:T(8,128)S(1)}, u32[]{:S(2)}, u32[]{:S(2)}) collective-permute-start(f32[544,128]{1,0:T(8,128)} %get-tuple-element.23), channel_id=1, source_target_pairs={{0,8},{1,2},{2,1},{3,11},{4,12},{5,6},{6,5},{7,15},{8,0},{9,10},{1... | collective-permute-start | bytes 835592 | tf_op jit(solution)/shard_map/ppermute | solution.py:679
  12.6 12.3 %collective-permute-start.2 = (f32[544,128]{1,0:T(8,128)}, f32[544,128]{1,0:T(8,128)S(1)}, u32[]{:S(2)}, u32[]{:S(2)}) collective-permute-start(f32[544,128]{1,0:T(8,128)} %get-tuple-element.24), channel_id=1, source_target_pairs={{0,1},{1,0},{2,3},{3,2},{4,5},{5,4},{6,7},{7,6},{8,9},{9,8},{10,11... | collective-permute-start | bytes 835592 | tf_op jit(solution)/shard_map/ppermute | solution.py:680
  13.4 1.2 %copy-start = (f32[256,1024]{1,0:T(8,128)S(1)}, f32[256,1024]{1,0:T(8,128)}, u32[]{:S(2)}) copy-start(f32[256,1024]{1,0:T(8,128)} %loads_ref.1) | copy-start | bytes 3145732
  14.6 0.9 %copy-start.1 = (f32[3,64,64]{2,1,0:T(8,128)S(1)}, f32[3,64,64]{2,1,0:T(8,128)}, u32[]{:S(2)}) copy-start(f32[3,64,64]{2,1,0:T(8,128)} %blocks_ref.7) | copy-start | bytes 147460
  15.5 0.9 %copy-start.3 = (f32[128,256]{1,0:T(8,128)S(1)}, f32[128,256]{1,0:T(8,128)}, u32[]{:S(2)}) copy-start(f32[128,256]{1,0:T(8,128)} %get-tuple-element.22.meta_hbm.meta_ref) | copy-start | bytes 393220
  16.4 10.3 %copy-start.2 = (f32[3,64,64]{2,1,0:T(8,128)S(1)}, f32[3,64,64]{2,1,0:T(8,128)}, u32[]{:S(2)}) copy-start(f32[3,64,64]{2,1,0:T(8,128)} %blocks_ref.7) | copy-start | bytes 147460
  25.9 10.2 %collective-permute-start.3 = (f32[96,1152]{1,0:T(8,128)S(1)}, f32[96,1152]{1,0:T(8,128)S(1)}, u32[]{:S(2)}, u32[]{:S(2)}) collective-permute-start(f32[96,1152]{1,0:T(8,128)S(1)} %get-tuple-element.27), channel_id=1, source_target_pairs={{0,1},{1,0},{2,3},{3,2},{4,5},{5,4},{6,7},{7,6},{8,9},{9,8},{10,11... | collective-permute-start | bytes 1327112 | tf_op jit(solution)/shard_map/ppermute | solution.py:712
  26.0 10.1 %collective-permute-start.4 = (f32[96,1152]{1,0:T(8,128)S(1)}, f32[96,1152]{1,0:T(8,128)S(1)}, u32[]{:S(2)}, u32[]{:S(2)}) collective-permute-start(f32[96,1152]{1,0:T(8,128)S(1)} %get-tuple-element.28), channel_id=1, source_target_pairs={{1,2},{3,4},{5,6},{7,8},{9,10},{11,12},{13,14},{2,1},{4,3},{6,5},{... | collective-permute-start | bytes 1327112 | tf_op jit(solution)/shard_map/ppermute | solution.py:711

commit v9 on v8

--- a/solution.py
+++ b/solution.py
@@ -134,9 +134,9 @@
     return body, jnp.where(iota(notes.shape, 1) < META // 2, notes, 0.0)
 
 
-def pack_first_kernel(devices, pos_ref, loads_hbm, rows_hbm, dens_hbm, cols_hbm, types_hbm,
-                      first_ref, meta_ref, target_ref,
-                      loads_ref, rows_ref, dens_ref, cols_ref, types_ref, sems):
+def pack_kernel(devices, pos_ref, loads_hbm, rows_hbm, dens_hbm, cols_hbm, types_hbm,
+                first_ref, second_ref, core_ref, meta_ref,
+                loads_ref, rows_ref, dens_ref, cols_ref, types_ref, sems):
     pairs = (
         (rows_hbm, rows_ref), (dens_hbm, dens_ref), (cols_hbm, cols_ref),
         (types_hbm, types_ref), (loads_hbm, loads_ref),
@@ -157,7 +157,6 @@
     owner = lax.div(ids, jnp.int32(rows))
     local = (ids - owner * rows + 1).astype(F32)
     target = targets(pos, ids, rows, devices)
-    target_ref[...] = jnp.broadcast_to(target, target_ref.shape)
 
     density = dens_ref[...]
     kinds = types_ref[...]
@@ -169,27 +168,9 @@
     meta_ref[4 * slots + 1:4 * slots + 2, :] = jnp.where(owner == pos, local, 0.0)
 
     copies[4].wait()
-    side = jnp.where(far_first(pos, devices), 2, 1)
-    pick = one_hot(iota((cap, rows), 0) + side * cap == target)
-    fill_block(pick, loads_ref[...], meta_ref[...], first_ref)
-
-
-def pack_second_kernel(devices, pos_ref, target_hbm, meta_hbm, loads_hbm, core_ref, second_ref,
-                       target_ref, meta_ref, loads_ref, sems):
-    pairs = ((target_hbm, target_ref), (meta_hbm, meta_ref), (loads_hbm, loads_ref))
-    copies = [
-        pltpu.make_async_copy(source, target, sems.at[number])
-        for number, (source, target) in enumerate(pairs)
-    ]
-    for copy in copies:
-        copy.start()
-    for copy in copies:
-        copy.wait()
-    rows = loads_ref.shape[0]
-    cap = rows // 4
-    late = jnp.where(far_first(pos_ref[0, 0], devices), 1, 2)
-    for side, out_ref in ((late, second_ref), (0, core_ref)):
-        pick = one_hot(iota((cap, rows), 0) + side * cap == target_ref[0:1, :])
+    early = jnp.where(far_first(pos, devices), 2, 1)
+    for side, out_ref in ((early, first_ref), (3 - early, second_ref), (0, core_ref)):
+        pick = one_hot(iota((cap, rows), 0) + side * cap == target)
         fill_block(pick, loads_ref[...], meta_ref[...], out_ref)
 
 
@@ -644,11 +625,11 @@
             rounds[1 - early].append((i, neighbour[i]))
 
     block = shape((cap * width // META + cap // 2, META), F32)
-    to_first, meta, target = pl.pallas_call(
-        functools.partial(pack_first_kernel, devices),
-        out_shape=(block, shape((META, rows), F32), shape((8, rows), jnp.int32)),
+    *outgoing, meta = pl.pallas_call(
+        functools.partial(pack_kernel, devices),
+        out_shape=(block, block, block, shape((META, rows), F32)),
         in_specs=[SMEM] + [HBM] * 5,
-        out_specs=(VMEM,) * 3,
+        out_specs=(VMEM,) * 4,
         scratch_shapes=[
             pltpu.VMEM((rows, width), F32),
             pltpu.VMEM((1, rows), jnp.int32),
@@ -658,26 +639,10 @@
             pltpu.SemaphoreType.DMA((5,)),
         ],
         compiler_params=PACK_PARAMS,
-        name="pack_first",
+        name="pack",
     )(position, loads, row_ids.reshape(1, rows), densities.T, block_cols.T, block_types.T)
-    from_first = lax.ppermute(to_first, "sub", rounds[0])
-
-    to_core, to_second = pl.pallas_call(
-        functools.partial(pack_second_kernel, devices),
-        out_shape=(block, block),
-        in_specs=[SMEM] + [HBM] * 3,
-        out_specs=(VMEM,) * 2,
-        scratch_shapes=[
-            pltpu.VMEM((8, rows), jnp.int32),
-            pltpu.VMEM((META, rows), F32),
-            pltpu.VMEM((rows, width), F32),
-            pltpu.SemaphoreType.DMA((3,)),
-        ],
-        compiler_params=PACK_PARAMS,
-        name="pack_second",
-    )(position, target, meta, loads)
-    from_second = lax.ppermute(to_second, "sub", rounds[1])
-    from_core = lax.ppermute(to_core, "sub", same_chip)
+    routes = (rounds[0], rounds[1], same_chip)
+    incoming = [lax.ppermute(part, "sub", route) for part, route in zip(outgoing, routes)]
 
     mixer_shape = shape((3 * TYPES * TILE, TILE), BF16)
     kept, kept_meta, mixer, first = pl.pallas_call(
@@ -706,7 +671,7 @@
         out_specs=(VMEM,) * 5,
         compiler_params=PARAMS,
         name="arrange",
-    )(position, from_first, from_second, from_core, kept, kept_meta)
+    )(position, *incoming, kept, kept_meta)
 
     halo_chip = lax.ppermute(to_chip, "sub", next_chip)
     halo_core = lax.ppermute(to_core, "sub", same_chip)

time: 72.7 us -> 73.2 us (level)
  waiting for transfers between devices: 6.51 us -> 9.15 us
  Pallas kernels: 38.7 us -> 36.6 us
    ppermute x3, waiting for transfers between devices: 6.5 us -> 9.15 us  [on_device(): lax.ppermute(part, 'sub', route)]
    pallas_call x2 -> x1, Pallas kernels: 5.06 us -> 2.89 us  [on_device(): pl.pallas_call(functools.partial(pack_kernel, devices), out_shape=(block,...]
  transfers between devices with their start and end apart: 5 -> 5, of which waited for: 1 -> 1; matrix products, arithmetic and copies ran while one was open for 0% -> 0% of each run, Pallas kernels for 19% -> 16%
where the time goes in v9:
time: 73.2 us; the launch traced here: 72.9 us
  Pallas kernels  36.6 us (50%)
  blocking collectives  14.9 us (20%)
  waiting for transfers between devices  9.15 us (12%)
  starting transfers between devices  8.4 us (11%)
  local copies, waits for them, and re-layouts  3.02 us (4%)
  between operations  0.91 us (1%)
    all_to_all x1, blocking collectives, on_device(): lax.all_to_all(moments, 'sub', split_axis=0, concat_axis=0, tiled=True)  14.9 us
    pallas_call x1, Pallas kernels, on_device(): pl.pallas_call(functools.partial(sides_kernel, slots), out_shape=(basis_s...  13.7 us
    pallas_call x1, Pallas kernels, on_device(): pl.pallas_call(functools.partial(interior_kernel, slots), out_shape=(basi...  9.39 us
    ppermute x3, waiting for transfers between devices, on_device(): lax.ppermute(part, 'sub', route)  9.15 us
    ppermute x3, starting transfers between devices, on_device(): lax.ppermute(part, 'sub', route)  7.64 us
    pallas_call x1, Pallas kernels, on_device(): pl.pallas_call(functools.partial(finish_kernel, slots), out_shape=(shape(...  7.64 us
    unnamed x8, local copies, waits for them, and re-layouts  3.02 us
    pallas_call x1, Pallas kernels, on_device(): pl.pallas_call(functools.partial(pack_kernel, devices), out_shape=(block,...  2.89 us
  transfers between devices with their start and end apart: 5, of which 1 were waited for; matrix products, arithmetic and copies ran while one was open for 0% of the time, Pallas kernels for 16%

profile of v9, /device:TPU:0, one launch (start us, length us, event | category | flops | bytes accessed | tf_op | source)
XLA Modules:
  0.0 72.9 jit_solution(10358081795885251978)
XLA Ops:
  0.6 2.9 %pack.1 = (f32[544,128]{1,0:T(8,128)}, f32[544,128]{1,0:T(8,128)}, f32[544,128]{1,0:T(8,128)}, f32[128,256]{1,0:T(8,128)}) custom-call(s32[1,1]{1,0:T(1,128)} %bitcast.pos_ref, f32[256,1024]{1,0:T(8,128)} %loads_ref.1, s32[1,256]{1,0:T(1,128)} %bitcast.8, f32[12,256]{1,0:T(8,128)} %bitcast.5, s32[12,256]{1,0:T(8,128)} %bitcast.6, s32[12,256]{1,0:T(8,128)} %bitcast.7), custom_call_target="tpu_custom_call" | custom-call | tf_op jit(solution)/shard_map/pack/pallas_call | solution.py:628
  3.5 0.7 collective-permute-start
  4.2 6.2 %collective-permute-start.1 = (f32[544,128]{1,0:T(8,128)}, f32[544,128]{1,0:T(8,128)S(1)}, u32[]{:S(2)}, u32[]{:S(2)}) collective-permute-start(f32[544,128]{1,0:T(8,128)} %get-tuple-element.20), channel_id=1, source_target_pairs={{0,8},{1,2},{2,1},{3,11},{4,12},{5,6},{6,5},{7,15},{8,0},{9,10},{1... | collective-permute-start | bytes 835592 | tf_op jit(solution)/shard_map/ppermute | solution.py:645
  10.4 0.8 %collective-permute-start.2 = (f32[544,128]{1,0:T(8,128)}, f32[544,128]{1,0:T(8,128)S(1)}, u32[]{:S(2)}, u32[]{:S(2)}) collective-permute-start(f32[544,128]{1,0:T(8,128)} %get-tuple-element.21), channel_id=1, source_target_pairs={{0,1},{1,0},{2,3},{3,2},{4,5},{5,4},{6,7},{7,6},{8,9},{9,8},{10,11... | collective-permute-start | bytes 835592 | tf_op jit(solution)/shard_map/ppermute | solution.py:645
  11.2 0.0 copy-start
  11.2 1.2 %copy-done = f32[256,1024]{1,0:T(8,128)S(1)} copy-done((f32[256,1024]{1,0:T(8,128)S(1)}, f32[256,1024]{1,0:T(8,128)}, u32[]{:S(2)}) %copy-start) | copy-done | bytes 1048600
  12.4 0.0 copy-start.1
  12.4 0.9 %copy-done.1 = f32[3,64,64]{2,1,0:T(8,128)S(1)} copy-done((f32[3,64,64]{2,1,0:T(8,128)S(1)}, f32[3,64,64]{2,1,0:T(8,128)}, u32[]{:S(2)}) %copy-start.1) | copy-done | bytes 49176
  13.3 0.0 copy-start.3
  13.3 0.9 %copy-done.3 = f32[128,256]{1,0:T(8,128)S(1)} copy-done((f32[128,256]{1,0:T(8,128)S(1)}, f32[128,256]{1,0:T(8,128)}, u32[]{:S(2)}) %copy-start.3) | copy-done | bytes 131096
  14.2 0.0 copy-start.2
  14.2 1.9 %prepare.1 = (f32[256,1024]{1,0:T(8,128)S(1)}, f32[256,128]{1,0:T(8,128)S(1)}, bf16[2304,256]{1,0:T(8,128)(2,1)S(1)}, f32[16,256]{1,0:T(8,128)S(1)}) custom-call(f32[256,1024]{1,0:T(8,128)S(1)} %copy-done, f32[128,256]{1,0:T(8,128)S(1)} %copy-done.3, f32[3,64,64]{2,1,0:T(8,128)S(1)} %copy-done.1), custom_call_target="tpu_custom_call" | custom-call | flops 4000000000 | bytes 4000000 | tf_op jit(solution)/shard_map/prepare/pallas_call | solution.py:648
  16.1 0.0 collective-permute-done.first_ref
  16.1 9.1 %collective-permute-done.1.second_ref = f32[544,128]{1,0:T(8,128)S(1)} collective-permute-done((f32[544,128]{1,0:T(8,128)}, f32[544,128]{1,0:T(8,128)S(1)}, u32[]{:S(2)}, u32[]{:S(2)}) %collective-permute-start.1) | collective-permute-done | bytes 278560 | tf_op jit(solution)/shard_map/ppermute | solution.py:645
  25.3 0.0 collective-permute-done.2.core_ref
  25.3 1.1 %arrange.1 = (bf16[2,4,256,256]{3,2,1,0:T(8,128)(2,1)S(1)}, bf16[2,4,256,256]{3,2,1,0:T(8,128)(2,1)S(1)}, f32[256,128]{1,0:T(8,128)S(1)}, f32[96,1152]{1,0:T(8,128)S(1)}, f32[96,1152]{1,0:T(8,128)S(1)}) custom-call(s32[1,1]{1,0:T(1,128)} %bitcast.pos_ref, f32[544,128]{1,0:T(8,128)S(1)} %collective-permute-done.first_ref, ...), custom_call_target="tpu_custom_call" | custom-call | tf_op jit(solution)/shard_map/arrange/pallas_call | solution.py:667
  26.4 0.1 collective-permute-start.3
  26.4 0.7 collective-permute-start.4
  27.1 0.0 copy-done.2
  27.1 9.4 %interior.1 = (bf16[3,2,4,256,256]{4,3,2,1,0:T(8,128)(2,1)S(1)}, bf16[2,3,96,768]{3,2,1,0:T(8,128)(2,1)S(1)}) custom-call(bf16[2,4,256,256]{3,2,1,0:T(8,128)(2,1)S(1)} %get-tuple-element.27.field_ref, f32[256,128]{1,0:T(8,128)S(1)} %get-tuple-element.28.meta_ref, bf16[2304,256]{1,0:T(8,128)(2,1)S(1)} %get-tuple-element.29.mixer_ref, f32[3,64,64]{2,1,0:T(8,128)S(1)} %copy-done.2), custom_call_target="tpu_custom_call" | custom-call | flops 10000000000 | bytes 8000000 | tf_op jit(solution)/shard_map/interior/pallas_call | solution.py:680
  36.5 0.0 collective-permute-done.3.core_ref
  36.5 0.0 collective-permute-done.4.chip_ref
  36.6 13.7 %sides.1 = (bf16[3,2,4,256,256]{4,3,2,1,0:T(8,128)(2,1)S(1)}, f32[16,16,128]{2,1,0:T(8,128)S(1)}) custom-call(s32[1,1]{1,0:T(1,128)} %bitcast.pos_ref, f32[96,1152]{1,0:T(8,128)S(1)} %collective-permute-done.3.core_ref, f32[96,1152]{1,0:T(8,128)S(1)} %collective-permute-done.4.chip_ref, bf16[2,4,256,256]{3,2,1,0:T(8,128)(2,1)S(1)} %get-tuple-element.27.field_ref, ...), custom_call_target="tpu_custom_call" | custom-call | tf_op jit(solution)/shard_map/sides/pallas_call | solution.py:696
  50.3 14.9 %all_to_all.5.moments_ref = f32[16,16,128]{2,1,0:T(8,128)S(1)} all-to-all(f32[16,16,128]{2,1,0:T(8,128)S(1)} %get-tuple-element.34), channel_id=1, replica_groups=mesh['groups'=2,'sub'=16] {'sub'}, dimensions={0} | all-to-all | bytes 262144 | tf_op jit(solution)/shard_map/all_to_all | solution.py:711
  65.1 7.6 %finish.1 = (f32[256,1024]{1,0:T(8,128)}, f32[256,1024]{1,0:T(8,128)}) custom-call(f32[16,16,128]{2,1,0:T(8,128)S(1)} %all_to_all.5.moments_ref, f32[3,64,64]{2,1,0:T(8,128)S(1)} %copy-done.2, bf16[2,4,256,256]{3,2,1,0:T(8,128)(2,1)S(1)} %get-tuple-element.32.geo_ref, bf16[3,2,4,256,256]{4,3,2,1,0:T(8,128)(2,1)S(1)} %get-tuple-element.35.basis_ref), custom_call_target="tpu_custom_call" | custom-call | tf_op jit(solution)/shard_map/finish/pallas_call | solution.py:713
Async XLA Ops:
  3.5 12.6 %collective-permute-start = (f32[544,128]{1,0:T(8,128)}, f32[544,128]{1,0:T(8,128)S(1)}, u32[]{:S(2)}, u32[]{:S(2)}) collective-permute-start(f32[544,128]{1,0:T(8,128)} %get-tuple-element.19), channel_id=1, source_target_pairs={{1,9},{2,10},{3,4},{4,3},{5,13},{6,14},{7,8},{8,7},{9,1},{10,2},{1... | collective-permute-start | bytes 835592 | tf_op jit(solution)/shard_map/ppermute | solution.py:645
  4.2 21.1 %collective-permute-start.1 = (f32[544,128]{1,0:T(8,128)}, f32[544,128]{1,0:T(8,128)S(1)}, u32[]{:S(2)}, u32[]{:S(2)}) collective-permute-start(f32[544,128]{1,0:T(8,128)} %get-tuple-element.20), channel_id=1, source_target_pairs={{0,8},{1,2},{2,1},{3,11},{4,12},{5,6},{6,5},{7,15},{8,0},{9,10},{1... | collective-permute-start | bytes 835592 | tf_op jit(solution)/shard_map/ppermute | solution.py:645
  10.4 14.9 %collective-permute-start.2 = (f32[544,128]{1,0:T(8,128)}, f32[544,128]{1,0:T(8,128)S(1)}, u32[]{:S(2)}, u32[]{:S(2)}) collective-permute-start(f32[544,128]{1,0:T(8,128)} %get-tuple-element.21), channel_id=1, source_target_pairs={{0,1},{1,0},{2,3},{3,2},{4,5},{5,4},{6,7},{7,6},{8,9},{9,8},{10,11... | collective-permute-start | bytes 835592 | tf_op jit(solution)/shard_map/ppermute | solution.py:645
  11.2 1.2 %copy-start = (f32[256,1024]{1,0:T(8,128)S(1)}, f32[256,1024]{1,0:T(8,128)}, u32[]{:S(2)}) copy-start(f32[256,1024]{1,0:T(8,128)} %loads_ref.1) | copy-start | bytes 3145732
  12.4 0.9 %copy-start.1 = (f32[3,64,64]{2,1,0:T(8,128)S(1)}, f32[3,64,64]{2,1,0:T(8,128)}, u32[]{:S(2)}) copy-start(f32[3,64,64]{2,1,0:T(8,128)} %blocks_ref.7) | copy-start | bytes 147460
  13.3 0.9 %copy-start.3 = (f32[128,256]{1,0:T(8,128)S(1)}, f32[128,256]{1,0:T(8,128)}, u32[]{:S(2)}) copy-start(f32[128,256]{1,0:T(8,128)} %get-tuple-element.22.meta_ref) | copy-start | bytes 393220
  14.2 12.9 %copy-start.2 = (f32[3,64,64]{2,1,0:T(8,128)S(1)}, f32[3,64,64]{2,1,0:T(8,128)}, u32[]{:S(2)}) copy-start(f32[3,64,64]{2,1,0:T(8,128)} %blocks_ref.7) | copy-start | bytes 147460
  26.4 10.2 %collective-permute-start.3 = (f32[96,1152]{1,0:T(8,128)S(1)}, f32[96,1152]{1,0:T(8,128)S(1)}, u32[]{:S(2)}, u32[]{:S(2)}) collective-permute-start(f32[96,1152]{1,0:T(8,128)S(1)} %get-tuple-element.25), channel_id=1, source_target_pairs={{0,1},{1,0},{2,3},{3,2},{4,5},{5,4},{6,7},{7,6},{8,9},{9,8},{10,11... | collective-permute-start | bytes 1327112 | tf_op jit(solution)/shard_map/ppermute | solution.py:677
  26.4 10.1 %collective-permute-start.4 = (f32[96,1152]{1,0:T(8,128)S(1)}, f32[96,1152]{1,0:T(8,128)S(1)}, u32[]{:S(2)}, u32[]{:S(2)}) collective-permute-start(f32[96,1152]{1,0:T(8,128)S(1)} %get-tuple-element.26), channel_id=1, source_target_pairs={{1,2},{3,4},{5,6},{7,8},{9,10},{11,12},{13,14},{2,1},{4,3},{6,5},{... | collective-permute-start | bytes 1327112 | tf_op jit(solution)/shard_map/ppermute | solution.py:676

commit v10 on v8

--- a/solution.py
+++ b/solution.py
@@ -85,12 +85,6 @@
         pos - 1 + 2 * odd,
         lax.rem(pos + devices // 2, jnp.int32(devices)),
     )
-
-
-def far_first(pos, devices):
-    half = devices // 2
-    group = (pos % half + 1) // 2 % max(half // 2, 1)
-    return group % 2 == 1
 
 
 def targets(pos, ids, rows, devices):
@@ -169,12 +163,11 @@
     meta_ref[4 * slots + 1:4 * slots + 2, :] = jnp.where(owner == pos, local, 0.0)
 
     copies[4].wait()
-    side = jnp.where(far_first(pos, devices), 2, 1)
-    pick = one_hot(iota((cap, rows), 0) + side * cap == target)
+    pick = one_hot(iota((cap, rows), 0) + 2 * cap == target)
     fill_block(pick, loads_ref[...], meta_ref[...], first_ref)
 
 
-def pack_second_kernel(devices, pos_ref, target_hbm, meta_hbm, loads_hbm, core_ref, second_ref,
+def pack_second_kernel(target_hbm, meta_hbm, loads_hbm, core_ref, second_ref,
                        target_ref, meta_ref, loads_ref, sems):
     pairs = ((target_hbm, target_ref), (meta_hbm, meta_ref), (loads_hbm, loads_ref))
     copies = [
@@ -187,8 +180,7 @@
         copy.wait()
     rows = loads_ref.shape[0]
     cap = rows // 4
-    late = jnp.where(far_first(pos_ref[0, 0], devices), 1, 2)
-    for side, out_ref in ((late, second_ref), (0, core_ref)):
+    for side, out_ref in enumerate((core_ref, second_ref)):
         pick = one_hot(iota((cap, rows), 0) + side * cap == target_ref[0:1, :])
         fill_block(pick, loads_ref[...], meta_ref[...], out_ref)
 
@@ -246,7 +238,7 @@
                 mixer_ref[start:start + TILE, :] = wide
 
 
-def arrange_kernel(slots, pos_ref, first_ref, second_ref, core_ref, kept_ref, kept_meta_ref,
+def arrange_kernel(slots, pos_ref, first_ref, core_ref, second_ref, kept_ref, kept_meta_ref,
                    geo_ref, field_ref, meta_ref, to_core_ref, to_chip_ref):
     rows, width = kept_ref.shape
     tiles = width // TILE
@@ -635,13 +627,7 @@
     same_chip = [(i, i ^ 1) for i in range(devices)]
     next_chip = [(i, i + 1) for i in range(1, devices - 1, 2)]
     next_chip += [(i + 1, i) for i in range(1, devices - 1, 2)]
-    neighbour = dict(next_chip)
-    rounds = [[], []]
-    for i in range(devices):
-        early = 0 if far_first(i, devices) else 1
-        rounds[early].append((i, (i + devices // 2) % devices))
-        if i in neighbour:
-            rounds[1 - early].append((i, neighbour[i]))
+    across = [(i, (i + devices // 2) % devices) for i in range(devices)]
 
     block = shape((cap * width // META + cap // 2, META), F32)
     to_first, meta, target = pl.pallas_call(
@@ -660,12 +646,12 @@
         compiler_params=PACK_PARAMS,
         name="pack_first",
     )(position, loads, row_ids.reshape(1, rows), densities.T, block_cols.T, block_types.T)
-    from_first = lax.ppermute(to_first, "sub", rounds[0])
+    from_first = lax.ppermute(to_first, "sub", across)
 
     to_core, to_second = pl.pallas_call(
-        functools.partial(pack_second_kernel, devices),
+        pack_second_kernel,
         out_shape=(block, block),
-        in_specs=[SMEM] + [HBM] * 3,
+        in_specs=[HBM] * 3,
         out_specs=(VMEM,) * 2,
         scratch_shapes=[
             pltpu.VMEM((8, rows), jnp.int32),
@@ -675,8 +661,8 @@
         ],
         compiler_params=PACK_PARAMS,
         name="pack_second",
-    )(position, target, meta, loads)
-    from_second = lax.ppermute(to_second, "sub", rounds[1])
+    )(target, meta, loads)
+    from_second = lax.ppermute(to_second, "sub", next_chip)
     from_core = lax.ppermute(to_core, "sub", same_chip)
 
     mixer_shape = shape((3 * TYPES * TILE, TILE), BF16)
@@ -706,7 +692,7 @@
         out_specs=(VMEM,) * 5,
         compiler_params=PARAMS,
         name="arrange",
-    )(position, from_first, from_second, from_core, kept, kept_meta)
+    )(position, from_first, from_core, from_second, kept, kept_meta)
 
     halo_chip = lax.ppermute(to_chip, "sub", next_chip)
     halo_core = lax.ppermute(to_core, "sub", same_chip)

time: 72.7 us -> 73.2 us (level)
  blocking collectives: 14.8 us -> 20 us
  starting transfers between devices: 8.41 us -> 5.61 us
  waiting for transfers between devices: 6.51 us -> 4.59 us
    all_to_all x1, blocking collectives: 14.8 us -> 20 us  [on_device(): lax.all_to_all(moments, 'sub', split_axis=0, concat_axis=0, tiled=True)]
    ppermute x2, starting transfers between devices: 6.85 us -> 4.78 us  [the longest x1 4.1 us: on_device(): from_first = lax.ppermute(to_first, 'sub', across)]
    ppermute x2, waiting for transfers between devices: 6.5 us -> 4.59 us  [the longest x1 4.58 us: on_device(): from_first = lax.ppermute(to_first, 'sub', across)]
where the time goes in v10:
time: 73.2 us; the launch traced here: 72.9 us
  Pallas kernels  38.7 us (53%)
  blocking collectives  20 us (27%)
  starting transfers between devices  5.61 us (8%)
  waiting for transfers between devices  4.59 us (6%)
  local copies, waits for them, and re-layouts  3.02 us (4%)
  between operations  0.93 us (1%)
    all_to_all x1, blocking collectives, on_device(): lax.all_to_all(moments, 'sub', split_axis=0, concat_axis=0, tiled=True)  20 us
    pallas_call x1, Pallas kernels, on_device(): pl.pallas_call(functools.partial(sides_kernel, slots), out_shape=(basis_s...  13.7 us
    pallas_call x1, Pallas kernels, on_device(): pl.pallas_call(functools.partial(interior_kernel, slots), out_shape=(basi...  9.39 us
    pallas_call x1, Pallas kernels, on_device(): pl.pallas_call(functools.partial(finish_kernel, slots), out_shape=(shape(...  7.64 us
    ppermute x1, waiting for transfers between devices, on_device(): from_first = lax.ppermute(to_first, 'sub', across)  4.58 us
    ppermute x1, starting transfers between devices, on_device(): from_first = lax.ppermute(to_first, 'sub', across)  4.1 us
    unnamed x8, local copies, waits for them, and re-layouts  3.02 us
    pallas_call x1, Pallas kernels, on_device(): pl.pallas_call(pack_second_kernel, out_shape=(block, block), in_specs=[HB...  2.62 us
  transfers between devices with their start and end apart: 5, of which 1 were waited for; matrix products, arithmetic and copies ran while one was open for 0% of the time, Pallas kernels for 19%

profile of v10, /device:TPU:0, one launch (start us, length us, event | category | flops | bytes accessed | tf_op | source)
XLA Modules:
  0.0 72.9 jit_solution(3180316083396263165)
XLA Ops:
  0.6 2.4 %pack_first.1 = (f32[544,128]{1,0:T(8,128)}, f32[128,256]{1,0:T(8,128)}, s32[8,256]{1,0:T(8,128)}) custom-call(s32[1,1]{1,0:T(1,128)} %bitcast.pos_ref, f32[256,1024]{1,0:T(8,128)} %loads_ref.1, s32[1,256]{1,0:T(1,128)} %bitcast.8, f32[12,256]{1,0:T(8,128)} %bitcast.5, s32[12,256]{1,0:T(8,128)} %bitcast.6, s32[12,256]{1,0:T(8,128)} %bitcast.7), custom_call_target="tpu_custom_call" | custom-call | tf_op jit(solution)/shard_map/pack_first/pallas_call | solution.py:633
  3.1 4.1 %collective-permute-start = (f32[544,128]{1,0:T(8,128)}, f32[544,128]{1,0:T(8,128)S(1)}, u32[]{:S(2)}, u32[]{:S(2)}) collective-permute-start(f32[544,128]{1,0:T(8,128)} %get-tuple-element.20), channel_id=1, source_target_pairs={{0,8},{1,9},{2,10},{3,11},{4,12},{5,13},{6,14},{7,15},{8,0},{9,1},... | collective-permute-start | bytes 835592 | tf_op jit(solution)/shard_map/ppermute | solution.py:649
  7.2 2.6 %pack_second.1 = (f32[544,128]{1,0:T(8,128)}, f32[544,128]{1,0:T(8,128)}) custom-call(s32[8,256]{1,0:T(8,128)} %get-tuple-element.21.target_hbm, f32[128,256]{1,0:T(8,128)} %get-tuple-element.22.meta_hbm.meta_ref, f32[256,1024]{1,0:T(8,128)} %loads_ref.1), custom_call_target="tpu_custom_call" | custom-call | tf_op jit(solution)/shard_map/pack_second/pallas_call | solution.py:651
  9.8 0.1 collective-permute-start.1
  9.9 0.7 collective-permute-start.2
  10.6 0.0 copy-start
  10.6 1.2 %copy-done = f32[256,1024]{1,0:T(8,128)S(1)} copy-done((f32[256,1024]{1,0:T(8,128)S(1)}, f32[256,1024]{1,0:T(8,128)}, u32[]{:S(2)}) %copy-start) | copy-done | bytes 1048600
  11.8 0.0 copy-start.1
  11.8 0.9 %copy-done.1 = f32[3,64,64]{2,1,0:T(8,128)S(1)} copy-done((f32[3,64,64]{2,1,0:T(8,128)S(1)}, f32[3,64,64]{2,1,0:T(8,128)}, u32[]{:S(2)}) %copy-start.1) | copy-done | bytes 49176
  12.7 0.0 copy-start.3
  12.7 0.9 %copy-done.3 = f32[128,256]{1,0:T(8,128)S(1)} copy-done((f32[128,256]{1,0:T(8,128)S(1)}, f32[128,256]{1,0:T(8,128)}, u32[]{:S(2)}) %copy-start.3) | copy-done | bytes 131096
  13.6 0.0 copy-start.2
  13.6 1.9 %prepare.1 = (f32[256,1024]{1,0:T(8,128)S(1)}, f32[256,128]{1,0:T(8,128)S(1)}, bf16[2304,256]{1,0:T(8,128)(2,1)S(1)}, f32[16,256]{1,0:T(8,128)S(1)}) custom-call(f32[256,1024]{1,0:T(8,128)S(1)} %copy-done, f32[128,256]{1,0:T(8,128)S(1)} %copy-done.3, f32[3,64,64]{2,1,0:T(8,128)S(1)} %copy-done.1), custom_call_target="tpu_custom_call" | custom-call | flops 4000000000 | bytes 4000000 | tf_op jit(solution)/shard_map/prepare/pallas_call | solution.py:669
  15.5 4.6 %collective-permute-done.first_ref = f32[544,128]{1,0:T(8,128)S(1)} collective-permute-done((f32[544,128]{1,0:T(8,128)}, f32[544,128]{1,0:T(8,128)S(1)}, u32[]{:S(2)}, u32[]{:S(2)}) %collective-permute-start) | collective-permute-done | bytes 278560 | tf_op jit(solution)/shard_map/ppermute | solution.py:649
  20.1 0.0 collective-permute-done.1.core_ref
  20.1 0.0 collective-permute-done.2.second_ref
  20.1 1.1 %arrange.1 = (bf16[2,4,256,256]{3,2,1,0:T(8,128)(2,1)S(1)}, bf16[2,4,256,256]{3,2,1,0:T(8,128)(2,1)S(1)}, f32[256,128]{1,0:T(8,128)S(1)}, f32[96,1152]{1,0:T(8,128)S(1)}, f32[96,1152]{1,0:T(8,128)S(1)}) custom-call(s32[1,1]{1,0:T(1,128)} %bitcast.pos_ref, f32[544,128]{1,0:T(8,128)S(1)} %collective-permute-done.first_ref, ...), custom_call_target="tpu_custom_call" | custom-call | tf_op jit(solution)/shard_map/arrange/pallas_call | solution.py:688
  21.2 0.1 collective-permute-start.3
  21.3 0.7 collective-permute-start.4
  22.0 0.0 copy-done.2
  22.0 9.4 %interior.1 = (bf16[3,2,4,256,256]{4,3,2,1,0:T(8,128)(2,1)S(1)}, bf16[2,3,96,768]{3,2,1,0:T(8,128)(2,1)S(1)}) custom-call(bf16[2,4,256,256]{3,2,1,0:T(8,128)(2,1)S(1)} %get-tuple-element.29.field_ref, f32[256,128]{1,0:T(8,128)S(1)} %get-tuple-element.30.meta_ref, bf16[2304,256]{1,0:T(8,128)(2,1)S(1)} %get-tuple-element.31.mixer_ref, f32[3,64,64]{2,1,0:T(8,128)S(1)} %copy-done.2), custom_call_target="tpu_custom_call" | custom-call | flops 10000000000 | bytes 8000000 | tf_op jit(solution)/shard_map/interior/pallas_call | solution.py:701
  31.4 0.0 collective-permute-done.3.core_ref
  31.4 0.0 collective-permute-done.4.chip_ref
  31.4 13.7 %sides.1 = (bf16[3,2,4,256,256]{4,3,2,1,0:T(8,128)(2,1)S(1)}, f32[16,16,128]{2,1,0:T(8,128)S(1)}) custom-call(s32[1,1]{1,0:T(1,128)} %bitcast.pos_ref, f32[96,1152]{1,0:T(8,128)S(1)} %collective-permute-done.3.core_ref, f32[96,1152]{1,0:T(8,128)S(1)} %collective-permute-done.4.chip_ref, bf16[2,4,256,256]{3,2,1,0:T(8,128)(2,1)S(1)} %get-tuple-element.29.field_ref, ...), custom_call_target="tpu_custom_call" | custom-call | tf_op jit(solution)/shard_map/sides/pallas_call | solution.py:717
  45.1 20.0 %all_to_all.5.moments_ref = f32[16,16,128]{2,1,0:T(8,128)S(1)} all-to-all(f32[16,16,128]{2,1,0:T(8,128)S(1)} %get-tuple-element.36), channel_id=1, replica_groups=mesh['groups'=2,'sub'=16] {'sub'}, dimensions={0} | all-to-all | bytes 262144 | tf_op jit(solution)/shard_map/all_to_all | solution.py:732
  65.0 7.6 %finish.1 = (f32[256,1024]{1,0:T(8,128)}, f32[256,1024]{1,0:T(8,128)}) custom-call(f32[16,16,128]{2,1,0:T(8,128)S(1)} %all_to_all.5.moments_ref, f32[3,64,64]{2,1,0:T(8,128)S(1)} %copy-done.2, bf16[2,4,256,256]{3,2,1,0:T(8,128)(2,1)S(1)} %get-tuple-element.34.geo_ref, bf16[3,2,4,256,256]{4,3,2,1,0:T(8,128)(2,1)S(1)} %get-tuple-element.37.basis_ref), custom_call_target="tpu_custom_call" | custom-call | tf_op jit(solution)/shard_map/finish/pallas_call | solution.py:734
Async XLA Ops:
  3.1 17.0 %collective-permute-start = (f32[544,128]{1,0:T(8,128)}, f32[544,128]{1,0:T(8,128)S(1)}, u32[]{:S(2)}, u32[]{:S(2)}) collective-permute-start(f32[544,128]{1,0:T(8,128)} %get-tuple-element.20), channel_id=1, source_target_pairs={{0,8},{1,9},{2,10},{3,11},{4,12},{5,13},{6,14},{7,15},{8,0},{9,1},... | collective-permute-start | bytes 835592 | tf_op jit(solution)/shard_map/ppermute | solution.py:649
  9.8 10.3 %collective-permute-start.1 = (f32[544,128]{1,0:T(8,128)}, f32[544,128]{1,0:T(8,128)S(1)}, u32[]{:S(2)}, u32[]{:S(2)}) collective-permute-start(f32[544,128]{1,0:T(8,128)} %get-tuple-element.23), channel_id=1, source_target_pairs={{0,1},{1,0},{2,3},{3,2},{4,5},{5,4},{6,7},{7,6},{8,9},{9,8},{10,11... | collective-permute-start | bytes 835592 | tf_op jit(solution)/shard_map/ppermute | solution.py:666
  9.9 10.2 %collective-permute-start.2 = (f32[544,128]{1,0:T(8,128)}, f32[544,128]{1,0:T(8,128)S(1)}, u32[]{:S(2)}, u32[]{:S(2)}) collective-permute-start(f32[544,128]{1,0:T(8,128)} %get-tuple-element.24), channel_id=1, source_target_pairs={{1,2},{3,4},{5,6},{7,8},{9,10},{11,12},{13,14},{2,1},{4,3},{6,5},{... | collective-permute-start | bytes 835592 | tf_op jit(solution)/shard_map/ppermute | solution.py:665
  10.6 1.2 %copy-start = (f32[256,1024]{1,0:T(8,128)S(1)}, f32[256,1024]{1,0:T(8,128)}, u32[]{:S(2)}) copy-start(f32[256,1024]{1,0:T(8,128)} %loads_ref.1) | copy-start | bytes 3145732
  11.8 0.9 %copy-start.1 = (f32[3,64,64]{2,1,0:T(8,128)S(1)}, f32[3,64,64]{2,1,0:T(8,128)}, u32[]{:S(2)}) copy-start(f32[3,64,64]{2,1,0:T(8,128)} %blocks_ref.7) | copy-start | bytes 147460
  12.7 0.9 %copy-start.3 = (f32[128,256]{1,0:T(8,128)S(1)}, f32[128,256]{1,0:T(8,128)}, u32[]{:S(2)}) copy-start(f32[128,256]{1,0:T(8,128)} %get-tuple-element.22.meta_hbm.meta_ref) | copy-start | bytes 393220
  13.6 8.4 %copy-start.2 = (f32[3,64,64]{2,1,0:T(8,128)S(1)}, f32[3,64,64]{2,1,0:T(8,128)}, u32[]{:S(2)}) copy-start(f32[3,64,64]{2,1,0:T(8,128)} %blocks_ref.7) | copy-start | bytes 147460
  21.2 10.2 %collective-permute-start.3 = (f32[96,1152]{1,0:T(8,128)S(1)}, f32[96,1152]{1,0:T(8,128)S(1)}, u32[]{:S(2)}, u32[]{:S(2)}) collective-permute-start(f32[96,1152]{1,0:T(8,128)S(1)} %get-tuple-element.27), channel_id=1, source_target_pairs={{0,1},{1,0},{2,3},{3,2},{4,5},{5,4},{6,7},{7,6},{8,9},{9,8},{10,11... | collective-permute-start | bytes 1327112 | tf_op jit(solution)/shard_map/ppermute | solution.py:698
  21.3 10.1 %collective-permute-start.4 = (f32[96,1152]{1,0:T(8,128)S(1)}, f32[96,1152]{1,0:T(8,128)S(1)}, u32[]{:S(2)}, u32[]{:S(2)}) collective-permute-start(f32[96,1152]{1,0:T(8,128)S(1)} %get-tuple-element.28), channel_id=1, source_target_pairs={{1,2},{3,4},{5,6},{7,8},{9,10},{11,12},{13,14},{2,1},{4,3},{6,5},{... | collective-permute-start | bytes 1327112 | tf_op jit(solution)/shard_map/ppermute | solution.py:697

commit v11 on v5

--- a/solution.py
+++ b/solution.py
@@ -745,7 +745,7 @@
 
     bits = devices.bit_length() - 1
     gathered_moments = [moments]
-    for low, high in ((0, bits // 2), (bits // 2, bits)):
+    for low, high in ((bits // 2, bits), (0, bits // 2)):
         partial = sum(gathered_moments[1:], gathered_moments[0])
         gathered_moments = [partial]
         for mask in range(1, 1 << (high - low)):

time: 71.8 us -> 71.6 us (level)
  starting transfers between devices: 16.9 us -> 16.1 us
    ppermute x6, starting transfers between devices: 9.24 us -> 8.44 us  [on_device(): gathered_moments.append(lax.ppermute(partial, 'sub', swap))]
  transfers between devices with their start and end apart: 11 -> 11, of which waited for: 4 -> 5; matrix products, arithmetic and copies ran while one was open for 0% -> 0% of each run, Pallas kernels for 19% -> 20%
where the time goes in v11:
time: 71.6 us; the launch traced here: 70.8 us
  Pallas kernels  38.8 us (54%)
  starting transfers between devices  16.1 us (22%)
  waiting for transfers between devices  11.9 us (17%)
  local copies, waits for them, and re-layouts  3.02 us (4%)
  between operations  0.94 us (1%)
    pallas_call x1, Pallas kernels, on_device(): pl.pallas_call(functools.partial(sides_kernel, slots), out_shape=(basis_s...  13.7 us
    pallas_call x1, Pallas kernels, on_device(): pl.pallas_call(functools.partial(interior_kernel, slots), out_shape=(basi...  9.39 us
    ppermute x6, starting transfers between devices, on_device(): gathered_moments.append(lax.ppermute(partial, 'sub', swap))  8.44 us
    pallas_call x1, Pallas kernels, on_device(): pl.pallas_call(functools.partial(finish_kernel, slots), out_shape=(shape(...  7.66 us
    ppermute x1, waiting for transfers between devices, on_device(): from_second = lax.ppermute(to_second, 'sub', rounds[1])  7.2 us
    ppermute x1, starting transfers between devices, on_device(): from_core = lax.ppermute(to_core, 'sub', same_chip)  4.89 us
    ppermute x6, waiting for transfers between devices, on_device(): gathered_moments.append(lax.ppermute(partial, 'sub', swap))  4.72 us
    unnamed x8, local copies, waits for them, and re-layouts  3.02 us
  transfers between devices with their start and end apart: 11, of which 5 were waited for; matrix products, arithmetic and copies ran while one was open for 0% of the time, Pallas kernels for 20%

profile of v11, /device:TPU:0, one launch (start us, length us, event | category | flops | bytes accessed | tf_op | source)
XLA Modules:
  0.0 70.8 jit_solution(13901447395782157040)
XLA Ops:
  0.6 2.4 %pack_first.1 = (f32[544,128]{1,0:T(8,128)}, f32[128,256]{1,0:T(8,128)}, s32[8,256]{1,0:T(8,128)}) custom-call(s32[1,1]{1,0:T(1,128)} %bitcast.pos_ref, f32[256,1024]{1,0:T(8,128)} %loads_hbm.3, s32[1,256]{1,0:T(1,128)} %bitcast.8, f32[12,256]{1,0:T(8,128)} %bitcast.5, s32[12,256]{1,0:T(8,128)} %bitcast.6, s32[12,256]{1,0:T(8,128)} %bitcast.7), custom_call_target="tpu_custom_call" | custom-call | tf_op jit(solution)/shard_map/pack_first/pallas_call | solution.py:647
  3.1 0.7 collective-permute-start.1
  3.8 2.6 %pack_second.1 = (f32[544,128]{1,0:T(8,128)}, f32[544,128]{1,0:T(8,128)}) custom-call(s32[1,1]{1,0:T(1,128)} %bitcast.pos_ref, s32[8,256]{1,0:T(8,128)} %get-tuple-element.23.target_hbm, f32[128,256]{1,0:T(8,128)} %get-tuple-element.20.meta_ref.meta_hbm, f32[256,1024]{1,0:T(8,128)} %loads_hbm.3), custom_call_target="tpu_custom_call" | custom-call | tf_op jit(solution)/shard_map/pack_second/pallas_call | solution.py:665
  6.4 4.9 %collective-permute-start = (f32[544,128]{1,0:T(8,128)}, f32[544,128]{1,0:T(8,128)S(1)}, u32[]{:S(2)}, u32[]{:S(2)}) collective-permute-start(f32[544,128]{1,0:T(8,128)} %get-tuple-element.24), channel_id=1, source_target_pairs={{0,1},{1,0},{2,3},{3,2},{4,5},{5,4},{6,7},{7,6},{8,9},{9,8},{10,11... | collective-permute-start | bytes 835592 | tf_op jit(solution)/shard_map/ppermute | solution.py:680
  11.3 1.4 %collective-permute-start.2 = (f32[544,128]{1,0:T(8,128)}, f32[544,128]{1,0:T(8,128)S(1)}, u32[]{:S(2)}, u32[]{:S(2)}) collective-permute-start(f32[544,128]{1,0:T(8,128)} %get-tuple-element.26), channel_id=1, source_target_pairs={{0,8},{1,2},{2,1},{3,11},{4,12},{5,6},{6,5},{7,15},{8,0},{9,10},{1... | collective-permute-start | bytes 835592 | tf_op jit(solution)/shard_map/ppermute | solution.py:679
  12.7 0.0 copy-start
  12.7 1.2 %copy-done = f32[256,1024]{1,0:T(8,128)S(1)} copy-done((f32[256,1024]{1,0:T(8,128)S(1)}, f32[256,1024]{1,0:T(8,128)}, u32[]{:S(2)}) %copy-start) | copy-done | bytes 1048600
  13.9 0.0 copy-start.1
  13.9 0.9 %copy-done.1 = f32[3,64,64]{2,1,0:T(8,128)S(1)} copy-done((f32[3,64,64]{2,1,0:T(8,128)S(1)}, f32[3,64,64]{2,1,0:T(8,128)}, u32[]{:S(2)}) %copy-start.1) | copy-done | bytes 49176
  14.8 0.0 copy-start.3
  14.8 0.9 %copy-done.3 = f32[128,256]{1,0:T(8,128)S(1)} copy-done((f32[128,256]{1,0:T(8,128)S(1)}, f32[128,256]{1,0:T(8,128)}, u32[]{:S(2)}) %copy-start.3) | copy-done | bytes 131096
  15.7 0.0 copy-start.2
  15.7 1.9 %prepare.1 = (f32[256,1024]{1,0:T(8,128)S(1)}, f32[256,128]{1,0:T(8,128)S(1)}, bf16[2304,256]{1,0:T(8,128)(2,1)S(1)}, f32[16,256]{1,0:T(8,128)S(1)}) custom-call(f32[256,1024]{1,0:T(8,128)S(1)} %copy-done, f32[128,256]{1,0:T(8,128)S(1)} %copy-done.3, f32[3,64,64]{2,1,0:T(8,128)S(1)} %copy-done.1), custom_call_target="tpu_custom_call" | custom-call | flops 4000000000 | bytes 4000000 | tf_op jit(solution)/shard_map/prepare/pallas_call | solution.py:683
  17.6 0.0 collective-permute-done.1.first_ref
  17.6 0.0 collective-permute-done.core_ref
  17.6 7.2 %collective-permute-done.2.second_ref = f32[544,128]{1,0:T(8,128)S(1)} collective-permute-done((f32[544,128]{1,0:T(8,128)}, f32[544,128]{1,0:T(8,128)S(1)}, u32[]{:S(2)}, u32[]{:S(2)}) %collective-permute-start.2) | collective-permute-done | bytes 278560 | tf_op jit(solution)/shard_map/ppermute | solution.py:679
  24.8 1.1 %arrange.1 = (bf16[2,4,256,256]{3,2,1,0:T(8,128)(2,1)S(1)}, bf16[2,4,256,256]{3,2,1,0:T(8,128)(2,1)S(1)}, f32[256,128]{1,0:T(8,128)S(1)}, f32[96,1152]{1,0:T(8,128)S(1)}, f32[96,1152]{1,0:T(8,128)S(1)}) custom-call(s32[1,1]{1,0:T(1,128)} %bitcast.pos_ref, f32[256,1024]{1,0:T(8,128)S(1)} %get-tuple-element.21.kept_ref, ...), custom_call_target="tpu_custom_call" | custom-call | tf_op jit(solution)/shard_map/arrange/pallas_call | solution.py:702
  25.9 0.1 collective-permute-start.3
  26.0 0.7 collective-permute-start.4
  26.7 0.0 copy-done.2
  26.7 9.4 %interior.1 = (bf16[3,2,4,256,256]{4,3,2,1,0:T(8,128)(2,1)S(1)}, bf16[2,3,96,768]{3,2,1,0:T(8,128)(2,1)S(1)}) custom-call(bf16[2,4,256,256]{3,2,1,0:T(8,128)(2,1)S(1)} %get-tuple-element.30.field_ref, f32[256,128]{1,0:T(8,128)S(1)} %get-tuple-element.31.meta_ref, bf16[2304,256]{1,0:T(8,128)(2,1)S(1)} %get-tuple-element.32.mixer_ref, f32[3,64,64]{2,1,0:T(8,128)S(1)} %copy-done.2), custom_call_target="tpu_custom_call" | custom-call | flops 10000000000 | bytes 8000000 | tf_op jit(solution)/shard_map/interior/pallas_call | solution.py:715
  36.1 0.0 collective-permute-done.3.core_ref
  36.1 0.0 collective-permute-done.4.chip_ref
  36.1 13.7 %sides.1 = (bf16[3,2,4,256,256]{4,3,2,1,0:T(8,128)(2,1)S(1)}, f32[16,128]{1,0:T(8,128)S(1)}) custom-call(s32[1,1]{1,0:T(1,128)} %bitcast.pos_ref, f32[96,1152]{1,0:T(8,128)S(1)} %collective-permute-done.3.core_ref, f32[96,1152]{1,0:T(8,128)S(1)} %collective-permute-done.4.chip_ref, bf16[2,4,256,256]{3,2,1,0:T(8,128)(2,1)S(1)} %get-tuple-element.30.field_ref, ...), custom_call_target="tpu_custom_call" | custom-call | tf_op jit(solution)/shard_map/sides/pallas_call | solution.py:731
  49.8 1.8 %collective-permute-start.7 = (f32[16,128]{1,0:T(8,128)S(1)}, f32[16,128]{1,0:T(8,128)S(1)}, u32[]{:S(2)}, u32[]{:S(2)}) collective-permute-start(f32[16,128]{1,0:T(8,128)S(1)} %get-tuple-element.37), channel_id=1, source_target_pairs={{0,12},{1,13},{2,14},{3,15},{4,8},{5,9},{6,10},{7,11},{8,4},{9,5},... | collective-permute-start | bytes 24584 | tf_op jit(solution)/shard_map/ppermute | solution.py:753
  51.7 2.1 %collective-permute-start.6 = (f32[16,128]{1,0:T(8,128)S(1)}, f32[16,128]{1,0:T(8,128)S(1)}, u32[]{:S(2)}, u32[]{:S(2)}) collective-permute-start(f32[16,128]{1,0:T(8,128)S(1)} %get-tuple-element.37), channel_id=1, source_target_pairs={{0,8},{1,9},{2,10},{3,11},{4,12},{5,13},{6,14},{7,15},{8,0},{9,1},... | collective-permute-start | bytes 24584 | tf_op jit(solution)/shard_map/ppermute | solution.py:753
  53.8 0.5 collective-permute-start.5
  54.3 1.1 %collective-permute-done.7 = f32[16,128]{1,0:T(8,128)S(1)} collective-permute-done((f32[16,128]{1,0:T(8,128)S(1)}, f32[16,128]{1,0:T(8,128)S(1)}, u32[]{:S(2)}, u32[]{:S(2)}) %collective-permute-start.7) | collective-permute-done | bytes 8224 | tf_op jit(solution)/shard_map/ppermute | solution.py:753
  55.4 0.8 %collective-permute-done.6 = f32[16,128]{1,0:T(8,128)S(1)} collective-permute-done((f32[16,128]{1,0:T(8,128)S(1)}, f32[16,128]{1,0:T(8,128)S(1)}, u32[]{:S(2)}, u32[]{:S(2)}) %collective-permute-start.6) | collective-permute-done | bytes 8224 | tf_op jit(solution)/shard_map/ppermute | solution.py:753
  56.2 1.2 %collective-permute-done.5 = f32[16,128]{1,0:T(8,128)S(1)} collective-permute-done((f32[16,128]{1,0:T(8,128)S(1)}, f32[16,128]{1,0:T(8,128)S(1)}, u32[]{:S(2)}, u32[]{:S(2)}) %collective-permute-start.5) | collective-permute-done | bytes 8224 | tf_op jit(solution)/shard_map/ppermute | solution.py:753
  57.4 0.0 collective-permute-start.10
  57.4 3.9 %collective-permute-start.9 = (f32[16,128]{1,0:T(8,128)S(1)}, f32[16,128]{1,0:T(8,128)S(1)}, u32[]{:S(2)}, u32[]{:S(2)}) collective-permute-start(f32[16,128]{1,0:T(8,128)S(1)} %add_add_fusion.refs_0_), channel_id=1, source_target_pairs={{0,2},{1,3},{2,0},{3,1},{4,6},{5,7},{6,4},{7,5},{8,10},{9,11},{10,... | collective-permute-start | bytes 24584 | tf_op jit(solution)/shard_map/ppermute | solution.py:753
  61.4 0.0 collective-permute-start.8
  61.4 0.0 collective-permute-done.10.refs_3_
  61.4 1.6 %collective-permute-done.9.refs_2_ = f32[16,128]{1,0:T(8,128)S(1)} collective-permute-done((f32[16,128]{1,0:T(8,128)S(1)}, f32[16,128]{1,0:T(8,128)S(1)}, u32[]{:S(2)}, u32[]{:S(2)}) %collective-permute-start.9) | collective-permute-done | bytes 8224 | tf_op jit(solution)/shard_map/ppermute | solution.py:753
  63.0 0.0 collective-permute-done.8.refs_1_
  63.0 7.7 %finish.1 = (f32[256,1024]{1,0:T(8,128)}, f32[256,1024]{1,0:T(8,128)}) custom-call(f32[3,64,64]{2,1,0:T(8,128)S(1)} %copy-done.2, bf16[2,4,256,256]{3,2,1,0:T(8,128)(2,1)S(1)} %get-tuple-element.27.geo_ref, bf16[3,2,4,256,256]{4,3,2,1,0:T(8,128)(2,1)S(1)} %get-tuple-element.36.basis_ref, f32[16,128]{1,0:T(8,128)S(1)} %add_add_fusion.refs_0_, ...), custom_call_target="tpu_custom_call" | custom-call | tf_op jit(solution)/shard_map/finish/pallas_call | solution.py:755
  (1 shorter events, 0.0 us)
Async XLA Ops:
  3.1 14.5 %collective-permute-start.1 = (f32[544,128]{1,0:T(8,128)}, f32[544,128]{1,0:T(8,128)S(1)}, u32[]{:S(2)}, u32[]{:S(2)}) collective-permute-start(f32[544,128]{1,0:T(8,128)} %get-tuple-element.25), channel_id=1, source_target_pairs={{1,9},{2,10},{3,4},{4,3},{5,13},{6,14},{7,8},{8,7},{9,1},{10,2},{1... | collective-permute-start | bytes 835592 | tf_op jit(solution)/shard_map/ppermute | solution.py:663
  6.4 11.2 %collective-permute-start = (f32[544,128]{1,0:T(8,128)}, f32[544,128]{1,0:T(8,128)S(1)}, u32[]{:S(2)}, u32[]{:S(2)}) collective-permute-start(f32[544,128]{1,0:T(8,128)} %get-tuple-element.24), channel_id=1, source_target_pairs={{0,1},{1,0},{2,3},{3,2},{4,5},{5,4},{6,7},{7,6},{8,9},{9,8},{10,11... | collective-permute-start | bytes 835592 | tf_op jit(solution)/shard_map/ppermute | solution.py:680
  11.3 13.5 %collective-permute-start.2 = (f32[544,128]{1,0:T(8,128)}, f32[544,128]{1,0:T(8,128)S(1)}, u32[]{:S(2)}, u32[]{:S(2)}) collective-permute-start(f32[544,128]{1,0:T(8,128)} %get-tuple-element.26), channel_id=1, source_target_pairs={{0,8},{1,2},{2,1},{3,11},{4,12},{5,6},{6,5},{7,15},{8,0},{9,10},{1... | collective-permute-start | bytes 835592 | tf_op jit(solution)/shard_map/ppermute | solution.py:679
  12.7 1.2 %copy-start = (f32[256,1024]{1,0:T(8,128)S(1)}, f32[256,1024]{1,0:T(8,128)}, u32[]{:S(2)}) copy-start(f32[256,1024]{1,0:T(8,128)} %loads_hbm.3) | copy-start | bytes 3145732
  13.9 0.9 %copy-start.1 = (f32[3,64,64]{2,1,0:T(8,128)S(1)}, f32[3,64,64]{2,1,0:T(8,128)}, u32[]{:S(2)}) copy-start(f32[3,64,64]{2,1,0:T(8,128)} %blocks_ref.7) | copy-start | bytes 147460
  14.8 0.9 %copy-start.3 = (f32[128,256]{1,0:T(8,128)S(1)}, f32[128,256]{1,0:T(8,128)}, u32[]{:S(2)}) copy-start(f32[128,256]{1,0:T(8,128)} %get-tuple-element.20.meta_ref.meta_hbm) | copy-start | bytes 393220
  15.7 11.0 %copy-start.2 = (f32[3,64,64]{2,1,0:T(8,128)S(1)}, f32[3,64,64]{2,1,0:T(8,128)}, u32[]{:S(2)}) copy-start(f32[3,64,64]{2,1,0:T(8,128)} %blocks_ref.7) | copy-start | bytes 147460
  25.9 10.2 %collective-permute-start.3 = (f32[96,1152]{1,0:T(8,128)S(1)}, f32[96,1152]{1,0:T(8,128)S(1)}, u32[]{:S(2)}, u32[]{:S(2)}) collective-permute-start(f32[96,1152]{1,0:T(8,128)S(1)} %get-tuple-element.28), channel_id=1, source_target_pairs={{0,1},{1,0},{2,3},{3,2},{4,5},{5,4},{6,7},{7,6},{8,9},{9,8},{10,11... | collective-permute-start | bytes 1327112 | tf_op jit(solution)/shard_map/ppermute | solution.py:712
  26.0 10.1 %collective-permute-start.4 = (f32[96,1152]{1,0:T(8,128)S(1)}, f32[96,1152]{1,0:T(8,128)S(1)}, u32[]{:S(2)}, u32[]{:S(2)}) collective-permute-start(f32[96,1152]{1,0:T(8,128)S(1)} %get-tuple-element.29), channel_id=1, source_target_pairs={{1,2},{3,4},{5,6},{7,8},{9,10},{11,12},{13,14},{2,1},{4,3},{6,5},{... | collective-permute-start | bytes 1327112 | tf_op jit(solution)/shard_map/ppermute | solution.py:711
  49.8 5.6 %collective-permute-start.7 = (f32[16,128]{1,0:T(8,128)S(1)}, f32[16,128]{1,0:T(8,128)S(1)}, u32[]{:S(2)}, u32[]{:S(2)}) collective-permute-start(f32[16,128]{1,0:T(8,128)S(1)} %get-tuple-element.37), channel_id=1, source_target_pairs={{0,12},{1,13},{2,14},{3,15},{4,8},{5,9},{6,10},{7,11},{8,4},{9,5},... | collective-permute-start | bytes 24584 | tf_op jit(solution)/shard_map/ppermute | solution.py:753
  51.7 4.5 %collective-permute-start.6 = (f32[16,128]{1,0:T(8,128)S(1)}, f32[16,128]{1,0:T(8,128)S(1)}, u32[]{:S(2)}, u32[]{:S(2)}) collective-permute-start(f32[16,128]{1,0:T(8,128)S(1)} %get-tuple-element.37), channel_id=1, source_target_pairs={{0,8},{1,9},{2,10},{3,11},{4,12},{5,13},{6,14},{7,15},{8,0},{9,1},... | collective-permute-start | bytes 24584 | tf_op jit(solution)/shard_map/ppermute | solution.py:753
  53.8 3.7 %collective-permute-start.5 = (f32[16,128]{1,0:T(8,128)S(1)}, f32[16,128]{1,0:T(8,128)S(1)}, u32[]{:S(2)}, u32[]{:S(2)}) collective-permute-start(f32[16,128]{1,0:T(8,128)S(1)} %get-tuple-element.37), channel_id=1, source_target_pairs={{0,4},{1,5},{2,6},{3,7},{4,0},{5,1},{6,2},{7,3},{8,12},{9,13},{10,... | collective-permute-start | bytes 24584 | tf_op jit(solution)/shard_map/ppermute | solution.py:753
  57.4 4.0 %collective-permute-start.10 = (f32[16,128]{1,0:T(8,128)S(1)}, f32[16,128]{1,0:T(8,128)S(1)}, u32[]{:S(2)}, u32[]{:S(2)}) collective-permute-start(f32[16,128]{1,0:T(8,128)S(1)} %add_add_fusion.refs_0_), channel_id=1, source_target_pairs={{0,3},{1,2},{2,1},{3,0},{4,7},{5,6},{6,5},{7,4},{8,11},{9,10},{10,... | collective-permute-start | bytes 24584 | tf_op jit(solution)/shard_map/ppermute | solution.py:753
  57.4 5.6 %collective-permute-start.9 = (f32[16,128]{1,0:T(8,128)S(1)}, f32[16,128]{1,0:T(8,128)S(1)}, u32[]{:S(2)}, u32[]{:S(2)}) collective-permute-start(f32[16,128]{1,0:T(8,128)S(1)} %add_add_fusion.refs_0_), channel_id=1, source_target_pairs={{0,2},{1,3},{2,0},{3,1},{4,6},{5,7},{6,4},{7,5},{8,10},{9,11},{10,... | collective-permute-start | bytes 24584 | tf_op jit(solution)/shard_map/ppermute | solution.py:753
  61.4 1.6 %collective-permute-start.8 = (f32[16,128]{1,0:T(8,128)S(1)}, f32[16,128]{1,0:T(8,128)S(1)}, u32[]{:S(2)}, u32[]{:S(2)}) collective-permute-start(f32[16,128]{1,0:T(8,128)S(1)} %add_add_fusion.refs_0_), channel_id=1, source_target_pairs={{0,1},{1,0},{2,3},{3,2},{4,5},{5,4},{6,7},{7,6},{8,9},{9,8},{10,11... | collective-permute-start | bytes 24584 | tf_op jit(solution)/shard_map/ppermute | solution.py:753
